TPU v7x, 512 devices: a whole 4x8x8 slice. The times are simulated.
512 devices in a mesh: frow: 16 (over y_hi, x, core), fcol: 32 (over y_lo, z).
Axes of the slice: x: 4, y: 8 (y_hi: 2, y_lo: 4; y = y_hi * 4 + y_lo), z: 8, core: 2. Of those that a mesh axis runs over, the one named last changes fastest.
Arguments:
- state: bfloat16 [12, 256, 256, 256], P(None, 'frow', 'fcol'), may hold values from -6 to 6
- gate_kernel: bfloat16 [3, 3, 256, 128], replicated, may hold values from -0.125 to 0.125
- dilated_kernel: bfloat16 [3, 3, 256, 128], replicated, may hold values from -0.125 to 0.125
- hidden_grad: bfloat16 [12, 256, 256, 128], P(None, 'frow', 'fcol'), may hold values from -6 to 6
- seam_face: int32 [12, 4], replicated, may hold values from 0 to 11
- seam_code: int32 [12, 4], replicated, may hold values from 0 to 3
- corner_mask: int32 [12, 4], replicated, may hold values 0 or 1
Outputs:
- hidden: bfloat16 [12, 256, 256, 128], P(None, 'frow', 'fcol')
- gate_kernel_grad: float32 [294912], P(('frow', 'fcol'))
- dilated_kernel_grad: float32 [294912], P(('frow', 'fcol'))
Inputs may be any that keep to these rules, and one draw needn't show every extreme that they name: `seam_face`: faces are numbered 0 to 11. `seam_code`: bit 1 picks the neighbour's side within the pair (north or south, west or east), bit 0 reverses the edge.
All inputs are finite; a program needn't handle non-finite values.
Results may differ from a plain program's by a relative error of at most 0.0029.
Values may be sent and summed in bfloat16 or wider, within the bound.
No kernel may reach another device: no remote copies, remote signals or barrier semaphores. Data moves between devices by JAX's collectives and lax.ppermute only.
A program may use at most 64 MiB of HBM per device.

v0:
```python
import jax
import jax.numpy as jnp
from jax import lax
from jax.sharding import PartitionSpec as P


def with_halo(shard, sides, width):
    for axis, dim in sides:
        count, length = (lax.axis_size(axis), shard.shape[dim])
        up = [(i, (i + 1) % count) for i in range(count)]
        down = [(j, i) for i, j in up]
        last = lax.slice_in_dim(shard, length - width, length, axis=dim)
        leading = lax.slice_in_dim(shard, 0, width, axis=dim)
        before = lax.ppermute(last, axis, up)
        after = lax.ppermute(leading, axis, down)
        shard = jnp.concatenate([before, shard, after], axis=dim)
    return shard


def swapped(shard, axis, distance):
    return lax.ppermute(shard, axis, [(i, i ^ 1 << distance) for i in range(lax.axis_size(axis))])


def corner_factor(upper, lower, left, right, corner_mask):
    weights = corner_mask.astype(jnp.float32) - 1.0
    factor = 1.0 + weights[:, 0, None, None] * upper[None, :, None] * left[None, None, :]
    factor = factor + weights[:, 1, None, None] * upper[None, :, None] * right[None, None, :]
    factor = factor + weights[:, 2, None, None] * lower[None, :, None] * left[None, None, :]
    factor = factor + weights[:, 3, None, None] * lower[None, :, None] * right[None, None, :]
    return factor


def kernel_grad(padded, delta, spacing):
    height = delta.shape[1]
    width = delta.shape[2]
    flat_delta = delta.reshape(-1, delta.shape[-1])
    taps = []
    for tap_row in range(3):
        for tap_col in range(3):
            window = padded[
                :,
                tap_row * spacing : tap_row * spacing + height,
                tap_col * spacing : tap_col * spacing + width,
            ]
            window = window.reshape(-1, padded.shape[-1])
            taps.append(
                lax.dot_general(
                    window, flat_delta, (((0,), (0,)), ((), ())), preferred_element_type=jnp.float32
                )
            )
    return jnp.stack(taps)


def on_device(state, gate_kernel, dilated_kernel, hidden_grad, seam_face, seam_code, corner_mask):
    count = state.shape[0]
    row_index = lax.axis_index("frow")
    col_index = lax.axis_index("fcol")
    row_last = lax.axis_size("frow") - 1
    col_last = lax.axis_size("fcol") - 1
    north_side = state[:, :2]
    south_side = jnp.flip(state, 1)[:, :2]
    wrapped = with_halo(jnp.stack([north_side, south_side]), (("frow", 0),), 1)
    from_above = wrapped[0]
    from_below = wrapped[3]
    north_edge = jnp.where(row_index == row_last, from_below, north_side)
    south_edge = jnp.where(row_index == 0, from_above, south_side)
    mirrored = jnp.stack([north_edge, south_edge])
    for bit_number in range(lax.axis_size("fcol").bit_length() - 1):
        mirrored = swapped(mirrored, "fcol", bit_number)
    mirrored = jnp.flip(mirrored, 3)
    candidates = jnp.stack([north_edge, mirrored[0], south_edge, mirrored[1]])
    candidates = candidates.reshape((4 * count,) + north_side.shape[1:])
    upper_rows = jnp.where(
        row_index == 0,
        jnp.take(candidates, seam_code[:, 0] * count + seam_face[:, 0], axis=0),
        from_above,
    )
    lower_rows = jnp.where(
        row_index == row_last,
        jnp.take(candidates, seam_code[:, 1] * count + seam_face[:, 1], axis=0),
        from_below,
    )
    rows_padded = jnp.concatenate([jnp.flip(upper_rows, 1), state, lower_rows], axis=1)
    west_side = rows_padded[:, :, :2]
    east_side = jnp.flip(rows_padded, 2)[:, :, :2]
    sideways = with_halo(jnp.stack([west_side, east_side]), (("fcol", 0),), 1)
    from_left = sideways[0]
    from_right = sideways[3]
    west_edge = jnp.where(col_index == col_last, from_right, west_side)
    east_edge = jnp.where(col_index == 0, from_left, east_side)
    reflected = jnp.stack([west_edge, east_edge])
    for bit_number in range(lax.axis_size("frow").bit_length() - 1):
        reflected = swapped(reflected, "frow", bit_number)
    reflected = jnp.flip(reflected, 2)
    options_cols = jnp.stack([west_edge, reflected[0], east_edge, reflected[1]])
    options_cols = options_cols.reshape((4 * count,) + west_side.shape[1:])
    left_cols = jnp.where(
        col_index == 0,
        jnp.take(options_cols, seam_code[:, 2] * count + seam_face[:, 2], axis=0),
        from_left,
    )
    right_cols = jnp.where(
        col_index == col_last,
        jnp.take(options_cols, seam_code[:, 3] * count + seam_face[:, 3], axis=0),
        from_right,
    )
    padded = jnp.concatenate([jnp.flip(left_cols, 2), rows_padded, right_cols], axis=2)
    row_places = jnp.arange(padded.shape[1])
    col_places = jnp.arange(padded.shape[2])
    upper_band = ((row_places < 2) & (row_index == 0)).astype(jnp.float32)
    lower_band = ((row_places >= padded.shape[1] - 2) & (row_index == row_last)).astype(jnp.float32)
    left_band = ((col_places < 2) & (col_index == 0)).astype(jnp.float32)
    right_band = ((col_places >= padded.shape[2] - 2) & (col_index == col_last)).astype(jnp.float32)
    factor = corner_factor(upper_band, lower_band, left_band, right_band, corner_mask)
    padded = padded * factor.astype(padded.dtype)[..., None]
    numbers = ("NHWC", "HWIO", "NHWC")
    inner = padded[:, 1:-1, 1:-1]
    gate_pre = lax.conv_general_dilated(
        inner,
        gate_kernel,
        (1, 1),
        "VALID",
        dimension_numbers=numbers,
        preferred_element_type=jnp.float32,
    )
    value_pre = lax.conv_general_dilated(
        padded,
        dilated_kernel,
        (1, 1),
        "VALID",
        rhs_dilation=(2, 2),
        dimension_numbers=numbers,
        preferred_element_type=jnp.float32,
    )
    activated, pullback = jax.vjp(jax.nn.gelu, gate_pre)
    hidden = (activated * value_pre).astype(jnp.bfloat16)
    upstream = hidden_grad.astype(jnp.float32)
    gate_delta = pullback(upstream * value_pre)[0].astype(jnp.bfloat16)
    value_delta = (upstream * activated).astype(jnp.bfloat16)
    total_cells = (
        count * state.shape[1] * state.shape[2] * lax.axis_size("frow") * lax.axis_size("fcol")
    )
    scale = total_cells ** (-0.5)
    gate_term = (kernel_grad(inner, gate_delta, 1) * scale).reshape(-1)
    dilated_term = (kernel_grad(padded, value_delta, 2) * scale).reshape(-1)
    gate_part, dilated_part = (
        lax.psum_scatter(gate_term, ("frow", "fcol"), scatter_dimension=0, tiled=True),
        lax.psum_scatter(dilated_term, ("frow", "fcol"), scatter_dimension=0, tiled=True),
    )
    return (hidden, gate_part, dilated_part)


def solution(mesh):
    return jax.shard_map(
        on_device,
        mesh=mesh,
        in_specs=(
            P(None, "frow", "fcol", None),
            P(),
            P(),
            P(None, "frow", "fcol", None),
            P(),
            P(),
            P(),
        ),
        out_specs=(P(None, "frow", "fcol", None), P(("frow", "fcol")), P(("frow", "fcol"))),
        check_vma=False,
    )
```

profile of v0, /device:TPU:1, one launch (start us, length us, event | category | flops | bytes accessed | tf_op | source)
XLA Modules:
  0.0 483.8 jit_solution(6596148341882211913)
XLA Ops:
  7.2 1.4 copy.63
  8.7 8.8 %collective-permute-start = (bf16[1,12,2,8,256]{4,2,3,1,0:T(2,128)(2,1)S(1)}, bf16[1,12,2,8,256]{4,2,3,1,0:T(2,128)(2,1)S(1)}, u32[]{:S(2)}, u32[]{:S(2)}) collective-permute-start(bf16[1,12,2,8,256]{4,2,3,1,0:T(2,128)(2,1)S(1)} %slice_bitcast_fusion), channel_id=1, source_target_pairs={{32,0},{64,32},{96,64},{128,96},{160,128},{192,160},{224,192},{256... | collective-permute-start | bytes 294920 | tf_op jit(solution)/shard_map/ppermute | solution.py:15
  19.1 1.9 collective-permute-start.1
  21.1 5.1 %collective-permute-done.1 = bf16[1,12,2,8,256]{4,2,3,1,0:T(2,128)(2,1)S(1)} collective-permute-done((bf16[1,12,2,8,256]{4,2,3,1,0:T(2,128)(2,1)S(1)}, bf16[1,12,2,8,256]{4,2,3,1,0:T(2,128)(2,1)S(1)}, u32[]{:S(2)}, u32[]{:S(2)}) %collective-permute-start.1) | collective-permute-done | bytes 98336 | tf_op jit(solution)/shard_map/ppermute | solution.py:14
  26.6 4.0 collective-permute-start.2
  30.6 3.3 collective-permute-done.2
  33.9 5.8 %collective-permute-start.3 = (bf16[2,12,2,8,256]{4,2,3,1,0:T(2,128)(2,1)S(1)}, bf16[2,12,2,8,256]{4,2,3,1,0:T(2,128)(2,1)S(1)}, u32[]{:S(2)}, u32[]{:S(2)}) collective-permute-start(bf16[2,12,2,8,256]{4,2,3,1,0:T(2,128)(2,1)S(1)} %collective-permute-done.2), channel_id=1, source_target_pairs={{0,2},{1,3},{2,0},{3,1},{4,6},{5,7},{6,4},{7,5},{8,10},{9,11},{10,... | collective-permute-start | bytes 589832 | tf_op jit(solution)/shard_map/ppermute | solution.py:21
  39.7 5.2 %collective-permute-done.3 = bf16[2,12,2,8,256]{4,2,3,1,0:T(2,128)(2,1)S(1)} collective-permute-done((bf16[2,12,2,8,256]{4,2,3,1,0:T(2,128)(2,1)S(1)}, bf16[2,12,2,8,256]{4,2,3,1,0:T(2,128)(2,1)S(1)}, u32[]{:S(2)}, u32[]{:S(2)}) %collective-permute-start.3) | collective-permute-done | bytes 196640 | tf_op jit(solution)/shard_map/ppermute | solution.py:21
  44.9 8.5 %collective-permute-start.4 = (bf16[2,12,2,8,256]{4,2,3,1,0:T(2,128)(2,1)S(1)}, bf16[2,12,2,8,256]{4,2,3,1,0:T(2,128)(2,1)S(1)}, u32[]{:S(2)}, u32[]{:S(2)}) collective-permute-start(bf16[2,12,2,8,256]{4,2,3,1,0:T(2,128)(2,1)S(1)} %collective-permute-done.3), channel_id=1, source_target_pairs={{0,4},{1,5},{2,6},{3,7},{4,0},{5,1},{6,2},{7,3},{8,12},{9,13},{10,... | collective-permute-start | bytes 589832 | tf_op jit(solution)/shard_map/ppermute | solution.py:21
  53.4 4.7 collective-permute-done.4
  58.1 1.9 collective-permute-start.5
  60.0 4.4 collective-permute-done.5
  64.5 1.9 collective-permute-start.6
  66.4 7.2 %collective-permute-done.6 = bf16[2,12,2,8,256]{4,2,3,1,0:T(2,128)(2,1)S(1)} collective-permute-done((bf16[2,12,2,8,256]{4,2,3,1,0:T(2,128)(2,1)S(1)}, bf16[2,12,2,8,256]{4,2,3,1,0:T(2,128)(2,1)S(1)}, u32[]{:S(2)}, u32[]{:S(2)}) %collective-permute-start.6) | collective-permute-done | bytes 196640 | tf_op jit(solution)/shard_map/ppermute | solution.py:21
  77.8 1.9 collective-permute-start.8
  79.7 7.3 %collective-permute-start.7 = (bf16[1,12,20,2,256]{4,2,3,1,0:T(8,128)(2,1)S(1)}, bf16[1,12,20,2,256]{4,2,3,1,0:T(8,128)(2,1)S(1)}, u32[]{:S(2)}, u32[]{:S(2)}) collective-permute-start(bf16[1,12,20,2,256]{4,2,3,1,0:T(8,128)(2,1)S(1)} %bitcast.204), channel_id=1, source_target_pairs={{1,0},{2,1},{3,2},{4,3},{5,4},{6,5},{7,6},{8,7},{9,8},{10,9},{11,1... | collective-permute-start | bytes 737288 | tf_op jit(solution)/shard_map/ppermute | solution.py:15
  87.0 2.2 collective-permute-done.8
  89.3 1.4 collective-permute-done.7
  91.4 21.6 %collective-permute-start.9 = (bf16[2,12,20,2,256]{4,3,2,1,0:T(2,128)(2,1)S(1)}, bf16[2,12,20,2,256]{4,3,2,1,0:T(2,128)(2,1)S(1)}, u32[]{:S(2)}, u32[]{:S(2)}) collective-permute-start(bf16[2,12,20,2,256]{4,3,2,1,0:T(2,128)(2,1)S(1)} %copy.66), channel_id=1, source_target_pairs={{0,32},{32,0},{64,96},{96,64},{128,160},{160,128},{192,224},{224,1... | collective-permute-start | bytes 1474568 | tf_op jit(solution)/shard_map/ppermute | solution.py:21
  113.0 1.5 collective-permute-done.9
  114.5 1.9 collective-permute-start.10
  116.4 12.3 %collective-permute-done.10 = bf16[2,12,20,2,256]{4,3,2,1,0:T(2,128)(2,1)S(1)} collective-permute-done((bf16[2,12,20,2,256]{4,3,2,1,0:T(2,128)(2,1)S(1)}, bf16[2,12,20,2,256]{4,3,2,1,0:T(2,128)(2,1)S(1)}, u32[]{:S(2)}, u32[]{:S(2)}) %collective-permute-start.10) | collective-permute-done | bytes 491552 | tf_op jit(solution)/shard_map/ppermute | solution.py:21
  128.8 2.3 collective-permute-start.11
  131.1 12.5 %collective-permute-done.11 = bf16[2,12,20,2,256]{4,3,2,1,0:T(2,128)(2,1)S(1)} collective-permute-done((bf16[2,12,20,2,256]{4,3,2,1,0:T(2,128)(2,1)S(1)}, bf16[2,12,20,2,256]{4,3,2,1,0:T(2,128)(2,1)S(1)}, u32[]{:S(2)}, u32[]{:S(2)}) %collective-permute-start.11) | collective-permute-done | bytes 491552 | tf_op jit(solution)/shard_map/ppermute | solution.py:21
  143.7 4.8 collective-permute-start.12
  149.2 22.8 %collective-permute-done.12 = bf16[2,12,20,2,256]{4,3,2,1,0:T(2,128)(2,1)S(1)} collective-permute-done((bf16[2,12,20,2,256]{4,3,2,1,0:T(2,128)(2,1)S(1)}, bf16[2,12,20,2,256]{4,3,2,1,0:T(2,128)(2,1)S(1)}, u32[]{:S(2)}, u32[]{:S(2)}) %collective-permute-start.12) | collective-permute-done | bytes 491552 | tf_op jit(solution)/shard_map/ppermute | solution.py:21
  180.1 3.4 fusion
  183.5 2.8 fusion.2
  186.3 1.6 fusion.29
  198.5 275.7 %all-reduce.5.cloned.1.call-done = (f32[294912]{0:T(1024)}, f32[294912]{0:T(1024)}) async-done(((f32[294912]{0:T(1024)}, f32[294912]{0:T(1024)}), (f32[294912]{0:T(1024)}, f32[294912]{0:T(1024)})) %all-reduce.5.cloned.1.call-update) | async-done | bytes 2359312
  474.2 1.4 dynamic-slice
  475.6 1.4 dynamic-slice.1
  (94 shorter events, 26.3 us)
Async XLA Ops:
  7.2 172.9 %copy-start = (bf16[3,3,256,128]{3,2,1,0:T(8,128)(2,1)S(1)}, bf16[3,3,256,128]{3,2,1,0:T(8,128)(2,1)}, u32[]{:S(2)}) copy-start(bf16[3,3,256,128]{3,2,1,0:T(8,128)(2,1)} %param.13) | copy-start | bytes 1769476
  7.2 467.0 %all-reduce.5.cloned.1.call-start = ((), (), s32[]{:S(2)}) async-start(), calls=%async_computation | async-start | bytes 4718592
  8.6 51.4 %copy-start.10 = (s32[12,4]{0,1:T(4,128)S(1)}, s32[12,4]{0,1:T(4,128)}, u32[]{:S(2)}) copy-start(s32[12,4]{0,1:T(4,128)} %param.15) | copy-start | bytes 580
  8.6 51.4 %copy-start.11 = (s32[12,4]{0,1:T(4,128)S(1)}, s32[12,4]{0,1:T(4,128)}, u32[]{:S(2)}) copy-start(s32[12,4]{0,1:T(4,128)} %param.16) | copy-start | bytes 580
  8.7 9.7 %collective-permute-start = (bf16[1,12,2,8,256]{4,2,3,1,0:T(2,128)(2,1)S(1)}, bf16[1,12,2,8,256]{4,2,3,1,0:T(2,128)(2,1)S(1)}, u32[]{:S(2)}, u32[]{:S(2)}) collective-permute-start(bf16[1,12,2,8,256]{4,2,3,1,0:T(2,128)(2,1)S(1)} %slice_bitcast_fusion), channel_id=1, source_target_pairs={{32,0},{64,32},{96,64},{128,96},{160,128},{192,160},{224,192},{256... | collective-permute-start | bytes 294920 | tf_op jit(solution)/shard_map/ppermute | solution.py:15
  19.1 7.0 %collective-permute-start.1 = (bf16[1,12,2,8,256]{4,2,3,1,0:T(2,128)(2,1)S(1)}, bf16[1,12,2,8,256]{4,2,3,1,0:T(2,128)(2,1)S(1)}, u32[]{:S(2)}, u32[]{:S(2)}) collective-permute-start(bf16[1,12,2,8,256]{4,2,3,1,0:T(2,128)(2,1)S(1)} %bitcast.207), channel_id=1, source_target_pairs={{0,32},{32,64},{64,96},{96,128},{128,160},{160,192},{192,224},{224... | collective-permute-start | bytes 294920 | tf_op jit(solution)/shard_map/ppermute | solution.py:14
  26.6 7.3 %collective-permute-start.2 = (bf16[2,12,2,8,256]{4,2,3,1,0:T(2,128)(2,1)S(1)}, bf16[2,12,2,8,256]{4,2,3,1,0:T(2,128)(2,1)S(1)}, u32[]{:S(2)}, u32[]{:S(2)}) collective-permute-start(bf16[2,12,2,8,256]{4,2,3,1,0:T(2,128)(2,1)S(1)} %pad_maximum_fusion.6), channel_id=1, source_target_pairs={{0,1},{1,0},{2,3},{3,2},{4,5},{5,4},{6,7},{7,6},{8,9},{9,8},{10,11... | collective-permute-start | bytes 589832 | tf_op jit(solution)/shard_map/ppermute | solution.py:21
  33.9 11.0 %collective-permute-start.3 = (bf16[2,12,2,8,256]{4,2,3,1,0:T(2,128)(2,1)S(1)}, bf16[2,12,2,8,256]{4,2,3,1,0:T(2,128)(2,1)S(1)}, u32[]{:S(2)}, u32[]{:S(2)}) collective-permute-start(bf16[2,12,2,8,256]{4,2,3,1,0:T(2,128)(2,1)S(1)} %collective-permute-done.2), channel_id=1, source_target_pairs={{0,2},{1,3},{2,0},{3,1},{4,6},{5,7},{6,4},{7,5},{8,10},{9,11},{10,... | collective-permute-start | bytes 589832 | tf_op jit(solution)/shard_map/ppermute | solution.py:21
  44.9 13.2 %collective-permute-start.4 = (bf16[2,12,2,8,256]{4,2,3,1,0:T(2,128)(2,1)S(1)}, bf16[2,12,2,8,256]{4,2,3,1,0:T(2,128)(2,1)S(1)}, u32[]{:S(2)}, u32[]{:S(2)}) collective-permute-start(bf16[2,12,2,8,256]{4,2,3,1,0:T(2,128)(2,1)S(1)} %collective-permute-done.3), channel_id=1, source_target_pairs={{0,4},{1,5},{2,6},{3,7},{4,0},{5,1},{6,2},{7,3},{8,12},{9,13},{10,... | collective-permute-start | bytes 589832 | tf_op jit(solution)/shard_map/ppermute | solution.py:21
  58.1 6.4 %collective-permute-start.5 = (bf16[2,12,2,8,256]{4,2,3,1,0:T(2,128)(2,1)S(1)}, bf16[2,12,2,8,256]{4,2,3,1,0:T(2,128)(2,1)S(1)}, u32[]{:S(2)}, u32[]{:S(2)}) collective-permute-start(bf16[2,12,2,8,256]{4,2,3,1,0:T(2,128)(2,1)S(1)} %collective-permute-done.4), channel_id=1, source_target_pairs={{0,8},{1,9},{2,10},{3,11},{4,12},{5,13},{6,14},{7,15},{8,0},{9,1},... | collective-permute-start | bytes 589832 | tf_op jit(solution)/shard_map/ppermute | solution.py:21
  64.5 9.1 %collective-permute-start.6 = (bf16[2,12,2,8,256]{4,2,3,1,0:T(2,128)(2,1)S(1)}, bf16[2,12,2,8,256]{4,2,3,1,0:T(2,128)(2,1)S(1)}, u32[]{:S(2)}, u32[]{:S(2)}) collective-permute-start(bf16[2,12,2,8,256]{4,2,3,1,0:T(2,128)(2,1)S(1)} %collective-permute-done.5), channel_id=1, source_target_pairs={{0,16},{1,17},{2,18},{3,19},{4,20},{5,21},{6,22},{7,23},{8,24},{9,... | collective-permute-start | bytes 589832 | tf_op jit(solution)/shard_map/ppermute | solution.py:21
  77.1 0.6 copy-start.5
  77.8 11.4 %collective-permute-start.8 = (bf16[1,12,20,2,256]{4,2,3,1,0:T(8,128)(2,1)S(1)}, bf16[1,12,20,2,256]{4,2,3,1,0:T(8,128)(2,1)S(1)}, u32[]{:S(2)}, u32[]{:S(2)}) collective-permute-start(bf16[1,12,20,2,256]{4,2,3,1,0:T(8,128)(2,1)S(1)} %reverse_bitcast_fusion), channel_id=1, source_target_pairs={{0,1},{1,2},{2,3},{3,4},{4,5},{5,6},{6,7},{7,8},{8,9},{9,10},{10,1... | collective-permute-start | bytes 737288 | tf_op jit(solution)/shard_map/ppermute | solution.py:14
  79.7 10.9 %collective-permute-start.7 = (bf16[1,12,20,2,256]{4,2,3,1,0:T(8,128)(2,1)S(1)}, bf16[1,12,20,2,256]{4,2,3,1,0:T(8,128)(2,1)S(1)}, u32[]{:S(2)}, u32[]{:S(2)}) collective-permute-start(bf16[1,12,20,2,256]{4,2,3,1,0:T(8,128)(2,1)S(1)} %bitcast.204), channel_id=1, source_target_pairs={{1,0},{2,1},{3,2},{4,3},{5,4},{6,5},{7,6},{8,7},{9,8},{10,9},{11,1... | collective-permute-start | bytes 737288 | tf_op jit(solution)/shard_map/ppermute | solution.py:15
  89.2 1.6 copy-start.1
  90.7 0.7 copy-start.3
  90.7 25.7 %copy-start.9 = (s32[12,4]{0,1:T(4,128)S(1)}, s32[12,4]{0,1:T(4,128)}, u32[]{:S(2)}) copy-start(s32[12,4]{0,1:T(4,128)} %param.17) | copy-start | bytes 580
  91.4 23.1 %collective-permute-start.9 = (bf16[2,12,20,2,256]{4,3,2,1,0:T(2,128)(2,1)S(1)}, bf16[2,12,20,2,256]{4,3,2,1,0:T(2,128)(2,1)S(1)}, u32[]{:S(2)}, u32[]{:S(2)}) collective-permute-start(bf16[2,12,20,2,256]{4,3,2,1,0:T(2,128)(2,1)S(1)} %copy.66), channel_id=1, source_target_pairs={{0,32},{32,0},{64,96},{96,64},{128,160},{160,128},{192,224},{224,1... | collective-permute-start | bytes 1474568 | tf_op jit(solution)/shard_map/ppermute | solution.py:21
  114.5 14.3 %collective-permute-start.10 = (bf16[2,12,20,2,256]{4,3,2,1,0:T(2,128)(2,1)S(1)}, bf16[2,12,20,2,256]{4,3,2,1,0:T(2,128)(2,1)S(1)}, u32[]{:S(2)}, u32[]{:S(2)}) collective-permute-start(bf16[2,12,20,2,256]{4,3,2,1,0:T(2,128)(2,1)S(1)} %collective-permute-done.9), channel_id=1, source_target_pairs={{0,64},{32,96},{64,0},{96,32},{128,192},{160,224},{192,128},{224,1... | collective-permute-start | bytes 1474568 | tf_op jit(solution)/shard_map/ppermute | solution.py:21
  128.8 14.9 %collective-permute-start.11 = (bf16[2,12,20,2,256]{4,3,2,1,0:T(2,128)(2,1)S(1)}, bf16[2,12,20,2,256]{4,3,2,1,0:T(2,128)(2,1)S(1)}, u32[]{:S(2)}, u32[]{:S(2)}) collective-permute-start(bf16[2,12,20,2,256]{4,3,2,1,0:T(2,128)(2,1)S(1)} %collective-permute-done.10), channel_id=1, source_target_pairs={{0,128},{32,160},{64,192},{96,224},{128,0},{160,32},{192,64},{224,... | collective-permute-start | bytes 1474568 | tf_op jit(solution)/shard_map/ppermute | solution.py:21
  143.7 28.3 %collective-permute-start.12 = (bf16[2,12,20,2,256]{4,3,2,1,0:T(2,128)(2,1)S(1)}, bf16[2,12,20,2,256]{4,3,2,1,0:T(2,128)(2,1)S(1)}, u32[]{:S(2)}, u32[]{:S(2)}) collective-permute-start(bf16[2,12,20,2,256]{4,3,2,1,0:T(2,128)(2,1)S(1)} %collective-permute-done.11), channel_id=1, source_target_pairs={{0,256},{32,288},{64,320},{96,352},{128,384},{160,416},{192,448},{... | collective-permute-start | bytes 1474568 | tf_op jit(solution)/shard_map/ppermute | solution.py:21
  174.9 2.6 copy-start.2
  174.9 2.6 copy-start.4
  177.5 1.3 copy-start.6
  177.5 1.3 copy-start.8
  180.0 3.5 copy-start.12
  183.5 2.8 copy-start.7
Sparse Core Ops, SparseCore 0:
  198.6 275.5 all-reduce.4
where the time goes:
time: 484 us
  waiting for transfers between devices  359 us (74%)
  starting transfers between devices  72.6 us (15%)
  between operations  14.7 us (3%)
  matrix products  14.4 us (3%)
  local copies, waits for them, and re-layouts  12.2 us (3%)
  other arithmetic  10.6 us (2%)
    unnamed x2, waiting for transfers between devices  276 us
    ppermute x9, waiting for transfers between devices, swapped(): lax.ppermute(shard, axis, [(i, i ^ 1 << distance) for i in range(lax.axis...  73.9 us
    ppermute x9, starting transfers between devices, swapped(): lax.ppermute(shard, axis, [(i, i ^ 1 << distance) for i in range(lax.axis...  52.7 us
    ppermute x2, starting transfers between devices, with_halo(): after = lax.ppermute(leading, axis, down)  16.1 us
  transfers between devices with their start and end apart: 14, of which 14 were waited for; matrix products, arithmetic and copies ran while one was open for 0% of the time, Pallas kernels for 0%

commit v1 on v0

v1 whole, which is shorter than its diff:
```python
import jax
import jax.numpy as jnp
from jax import lax
from jax.sharding import Mesh
from jax.sharding import PartitionSpec as P

ROWS = ("yh", "x", "c")
COLS = ("yl", "z")


def on_device(state, gate_kernel, dilated_kernel, hidden_grad, seam_face, seam_code, corner_mask):
    count, height, width, _ = state.shape
    n_row = lax.axis_size(ROWS)
    n_col = lax.axis_size(COLS)
    row_index = lax.axis_index(ROWS)
    col_index = lax.axis_index(COLS)
    row_last = n_row - 1
    col_last = n_col - 1
    everywhere = ROWS + COLS

    def place(i, j):
        return i * n_col + j

    def edge_index(side):
        return seam_code[:, side] * count + seam_face[:, side]

    north = state[:, :2]
    south = state[:, height - 2 :]
    own_edge = jnp.where(row_index == 0, north, jnp.flip(south, 1))
    from_above = lax.ppermute(south, ROWS, [(i, (i + 1) % n_row) for i in range(n_row)])
    from_below = lax.ppermute(north, ROWS, [((i + 1) % n_row, i) for i in range(n_row)])
    same = [(place(i, j), place(i, col_last - j)) for i in (0, row_last) for j in range(n_col)]
    other = [
        (place(i, j), place(row_last - i, col_last - j)) for i in (0, row_last) for j in range(n_col)
    ]
    mirror_same = jnp.flip(lax.ppermute(own_edge, everywhere, same), 2)
    mirror_other = jnp.flip(lax.ppermute(own_edge, everywhere, other), 2)
    first = row_index == 0
    far_edge = jnp.where(first, jnp.flip(from_above, 1), from_below)
    candidates = jnp.stack(
        [
            jnp.where(first, own_edge, far_edge),
            jnp.where(first, mirror_same, mirror_other),
            jnp.where(first, far_edge, own_edge),
            jnp.where(first, mirror_other, mirror_same),
        ]
    ).reshape((4 * count,) + north.shape[1:])
    picked = jnp.take(candidates, jnp.where(first, edge_index(0), edge_index(1)), axis=0)
    upper = jnp.where(first, jnp.flip(picked, 1), from_above)
    lower = jnp.where(row_index == row_last, picked, from_below)
    rows_padded = jnp.concatenate([upper, state, lower], axis=1)

    west = rows_padded[:, :, :2]
    east = rows_padded[:, :, width - 2 :]
    first = col_index == 0
    own_edge = jnp.where(first, west, jnp.flip(east, 2))
    from_left = lax.ppermute(east, COLS, [(i, (i + 1) % n_col) for i in range(n_col)])
    from_right = lax.ppermute(west, COLS, [((i + 1) % n_col, i) for i in range(n_col)])
    same = [(place(i, j), place(row_last - i, j)) for i in range(n_row) for j in (0, col_last)]
    other = [
        (place(i, j), place(row_last - i, col_last - j)) for i in range(n_row) for j in (0, col_last)
    ]
    mirror_same = jnp.flip(lax.ppermute(own_edge, everywhere, same), 1)
    mirror_other = jnp.flip(lax.ppermute(own_edge, everywhere, other), 1)
    far_edge = jnp.where(first, jnp.flip(from_left, 2), from_right)
    candidates = jnp.stack(
        [
            jnp.where(first, own_edge, far_edge),
            jnp.where(first, mirror_same, mirror_other),
            jnp.where(first, far_edge, own_edge),
            jnp.where(first, mirror_other, mirror_same),
        ]
    ).reshape((4 * count,) + west.shape[1:])
    picked = jnp.take(candidates, jnp.where(first, edge_index(2), edge_index(3)), axis=0)
    left = jnp.where(first, jnp.flip(picked, 2), from_left)
    right = jnp.where(col_index == col_last, picked, from_right)

    spots = jnp.arange(height + 4)
    top = ((spots < 2) & (row_index == 0))[None, :]
    bottom = ((spots >= height + 2) & (row_index == row_last))[None, :]

    def masked(cols, here, north_mask, south_mask):
        gone = (top & (north_mask == 0)[:, None]) | (bottom & (south_mask == 0)[:, None])
        return jnp.where((gone & here)[:, :, None, None], 0, cols)

    left = masked(left, col_index == 0, corner_mask[:, 0], corner_mask[:, 2])
    right = masked(right, col_index == col_last, corner_mask[:, 1], corner_mask[:, 3])
    padded = jnp.concatenate([left, rows_padded, right], axis=2)

    numbers = ("NHWC", "HWIO", "NHWC")
    inner = padded[:, 1:-1, 1:-1]
    gate_pre = lax.conv_general_dilated(
        inner, gate_kernel, (1, 1), "VALID", dimension_numbers=numbers, preferred_element_type=jnp.float32
    )
    value_pre = lax.conv_general_dilated(
        padded,
        dilated_kernel,
        (1, 1),
        "VALID",
        rhs_dilation=(2, 2),
        dimension_numbers=numbers,
        preferred_element_type=jnp.float32,
    )
    activated, pullback = jax.vjp(jax.nn.gelu, gate_pre)
    hidden = (activated * value_pre).astype(jnp.bfloat16)
    upstream = hidden_grad.astype(jnp.float32)
    gate_delta = pullback(upstream * value_pre)[0].astype(jnp.bfloat16)
    value_delta = (upstream * activated).astype(jnp.bfloat16)

    terms = []
    for windows, delta, spacing in ((inner, gate_delta, 1), (padded, value_delta, 2)):
        flat_delta = delta.reshape(-1, delta.shape[-1])
        for a in range(3):
            for b in range(3):
                window = windows[:, a * spacing : a * spacing + height, b * spacing : b * spacing + width]
                window = window.reshape(-1, windows.shape[-1])
                terms.append(
                    lax.dot_general(
                        window, flat_delta, (((0,), (0,)), ((), ())), preferred_element_type=jnp.float32
                    )
                )
    scale = (count * height * width * n_row * n_col) ** (-0.5)
    gate_part, dilated_part = scattered_sum(jnp.stack(terms), scale)
    return (hidden, gate_part, dilated_part)


def scattered_sum(terms, scale):
    yh, x, c, yl, z = (lax.axis_size(a) for a in ROWS + COLS)
    lanes = terms.shape[-1]
    span = terms.size // 2 // lanes // (yh * x * c * yl)
    terms = terms.reshape(2, yh, x, c, yl, span, lanes)
    core = lax.axis_index("c")
    mine = lax.dynamic_index_in_dim(terms, core, 3, keepdims=False)
    theirs = lax.dynamic_index_in_dim(terms, 1 - core, 3, keepdims=False)
    both = mine + lax.ppermute(theirs, "c", [(0, 1), (1, 0)])
    sends = jnp.transpose(both.astype(jnp.bfloat16), (2, 3, 0, 1, 4, 5)).reshape(x * yl, -1, lanes)
    arrived = lax.all_to_all(sends, ("x", "yl"), 0, 0)
    part = jnp.sum(arrived.astype(jnp.float32), axis=0).reshape(2, yh, span, lanes)
    share = span * lanes // z
    tall = -(-(share + lanes // 2) // lanes)
    starts = [i * share // lanes for i in range(z)]
    sends = jnp.stack([part[:, :, s : s + tall] for s in starts])
    sends = jnp.transpose(sends, (2, 0, 1, 3, 4)).reshape(yh * z, 2 * tall, lanes)
    sends = jnp.pad(sends, ((0, 0), (0, -2 * tall % 8), (0, 0)))
    arrived = lax.all_to_all(sends, ("yh", "z"), 0, 0)
    total = jnp.sum(arrived[:, : 2 * tall], axis=0).reshape(2, tall * lanes) * scale
    skip = lax.axis_index("z") * share % lanes
    total = lax.dynamic_slice_in_dim(total, skip, share, axis=1)
    return total[0], total[1]


def solution(mesh):
    fine = Mesh(mesh.devices.reshape(2, 4, 2, 4, 8), ROWS + COLS)
    cells = P(None, ROWS, COLS, None)
    return jax.shard_map(
        on_device,
        mesh=fine,
        in_specs=(cells, P(), P(), cells, P(), P(), P()),
        out_specs=(cells, P(ROWS + COLS), P(ROWS + COLS)),
        check_vma=False,
    )
```

time: 484 us -> 174 us (0.36)
  waiting for transfers between devices: 359 us -> 31 us
  blocking collectives: 0 us -> 20 us
  matrix products: 14.4 us -> 29.9 us
  between operations: 14.7 us -> 1.17 us
    unnamed x2 -> x0, waiting for transfers between devices: 276 us -> none
    ppermute x13 -> x9, waiting for transfers between devices: 83.5 us -> 20.5 us  [the longest x1 6.83 us: on_device(): lax.ppermute(east, COLS, [(i, (i + 1) % n_col) for i in range(n_col)])]
    all_to_all x0 -> x1, blocking collectives: none -> 20 us  [scattered_sum(): arrived = lax.all_to_all(sends, ('x', 'yl'), 0, 0)]
    ppermute x13 -> x9, starting transfers between devices: 72.6 us -> 58.7 us  [the longest x1 24.6 us: scattered_sum(): both = mine + lax.ppermute(theirs, 'c', [(0, 1), (1, 0)])]
    dot_general x18, matrix products: 8.2 us -> 21.6 us  [on_device(): lax.dot_general(window, flat_delta, (((0,), (0,)), ((), ())), preferred_e...]
    all_to_all x0 -> x1, waiting for transfers between devices: none -> 10.5 us  [scattered_sum(): arrived = lax.all_to_all(sends, ('yh', 'z'), 0, 0)]
    all_to_all x0 -> x1, starting transfers between devices: none -> 9.05 us  [scattered_sum(): arrived = lax.all_to_all(sends, ('yh', 'z'), 0, 0)]
  transfers between devices with their start and end apart: 14 -> 10, of which waited for: 14 -> 6; matrix products, arithmetic and copies ran while one was open for 0% -> 4% of each run, Pallas kernels for 0% -> 0%
where the time goes in v1:
time: 174 us; the launch traced here: 172 us
  starting transfers between devices  67.8 us (39%)
  waiting for transfers between devices  31 us (18%)
  matrix products  29.9 us (17%)
  blocking collectives  20 us (11%)
  local copies, waits for them, and re-layouts  16.7 us (10%)
  other arithmetic  5.94 us (3%)
    ppermute x1, starting transfers between devices, scattered_sum(): both = mine + lax.ppermute(theirs, 'c', [(0, 1), (1, 0)])  24.6 us
    dot_general x18, matrix products, on_device(): lax.dot_general(window, flat_delta, (((0,), (0,)), ((), ())), preferred_e...  21.6 us
    all_to_all x1, blocking collectives, scattered_sum(): arrived = lax.all_to_all(sends, ('x', 'yl'), 0, 0)  20 us
    ppermute x1, starting transfers between devices, on_device(): lax.ppermute(west, COLS, [((i + 1) % n_col, i) for i in range(n_col)])  11 us
    all_to_all x1, waiting for transfers between devices, scattered_sum(): arrived = lax.all_to_all(sends, ('yh', 'z'), 0, 0)  10.5 us
    all_to_all x1, starting transfers between devices, scattered_sum(): arrived = lax.all_to_all(sends, ('yh', 'z'), 0, 0)  9.05 us
    ppermute x1, starting transfers between devices, on_device(): lax.ppermute(north, ROWS, [((i + 1) % n_row, i) for i in range(n_row)])  8.79 us
    ppermute x1, waiting for transfers between devices, on_device(): lax.ppermute(east, COLS, [(i, (i + 1) % n_col) for i in range(n_col)])  6.83 us
  transfers between devices with their start and end apart: 10, of which 6 were waited for; matrix products, arithmetic and copies ran while one was open for 4% of the time, Pallas kernels for 0%

profile of v1, /device:TPU:1, one launch (start us, length us, event | category | flops | bytes accessed | tf_op | source)
XLA Modules:
  0.0 172.5 jit_solution(17855292503159984670)
XLA Ops:
  0.7 1.7 copy.126
  2.4 8.8 %collective-permute-start.1 = (bf16[12,2,8,256]{3,0,2,1:T(8,128)(2,1)S(1)}, bf16[12,2,8,256]{3,0,2,1:T(8,128)(2,1)S(1)}, u32[]{:S(2)}, u32[]{:S(2)}) collective-permute-start(bf16[12,2,8,256]{3,0,2,1:T(8,128)(2,1)S(1)} %get-tuple-element.33), channel_id=1, source_target_pairs={{32,0},{64,32},{96,64},{128,96},{160,128},{192,160},{224,192},{256... | collective-permute-start | bytes 294920 | tf_op jit(solution)/shard_map/ppermute | solution.py:31
  11.2 1.9 %collective-permute-start = (bf16[12,2,8,256]{3,0,2,1:T(8,128)(2,1)S(1)}, bf16[12,2,8,256]{3,0,2,1:T(8,128)(2,1)S(1)}, u32[]{:S(2)}, u32[]{:S(2)}) collective-permute-start(bf16[12,2,8,256]{3,0,2,1:T(8,128)(2,1)S(1)} %get-tuple-element.32), channel_id=1, source_target_pairs={{0,32},{32,64},{64,96},{96,128},{128,160},{160,192},{192,224},{224... | collective-permute-start | bytes 294920 | tf_op jit(solution)/shard_map/ppermute | solution.py:30
  13.1 1.4 constant_dynamic-update-slice_fusion
  19.4 11.0 %collective-permute-start.5 = (bf16[12,20,2,256]{3,0,2,1:T(8,128)(2,1)}, bf16[12,20,2,256]{3,0,2,1:T(8,128)(2,1)S(1)}, u32[]{:S(2)}, u32[]{:S(2)}) collective-permute-start(bf16[12,20,2,256]{3,0,2,1:T(8,128)(2,1)} %get-tuple-element.31), channel_id=1, source_target_pairs={{1,0},{2,1},{3,2},{4,3},{5,4},{6,5},{7,6},{8,7},{9,8},{10,9},{11,1... | collective-permute-start | bytes 737288 | tf_op jit(solution)/shard_map/ppermute | solution.py:58
  30.4 1.9 %collective-permute-start.4 = (bf16[12,20,2,256]{3,0,2,1:T(8,128)(2,1)S(1)}, bf16[12,20,2,256]{3,0,2,1:T(8,128)(2,1)S(1)}, u32[]{:S(2)}, u32[]{:S(2)}) collective-permute-start(bf16[12,20,2,256]{3,0,2,1:T(8,128)(2,1)S(1)} %get-tuple-element.30), channel_id=1, source_target_pairs={{0,1},{1,2},{2,3},{3,4},{4,5},{5,6},{6,7},{7,8},{8,9},{9,10},{10,1... | collective-permute-start | bytes 737288 | tf_op jit(solution)/shard_map/ppermute | solution.py:57
  33.0 1.6 copy.134
  35.4 6.8 %collective-permute-done.4 = bf16[12,20,2,256]{3,0,2,1:T(8,128)(2,1)S(1)} collective-permute-done((bf16[12,20,2,256]{3,0,2,1:T(8,128)(2,1)S(1)}, bf16[12,20,2,256]{3,0,2,1:T(8,128)(2,1)S(1)}, u32[]{:S(2)}, u32[]{:S(2)}) %collective-permute-start.4) | collective-permute-done | bytes 245792 | tf_op jit(solution)/shard_map/ppermute | solution.py:57
  42.2 1.2 select_bitcast_fusion.3
  43.4 2.5 %collective-permute-start.7 = (bf16[12,20,2,256]{3,0,2,1:T(8,128)(2,1)S(1)}, bf16[12,20,2,256]{3,0,2,1:T(8,128)(2,1)S(1)}, u32[]{:S(2)}, u32[]{:S(2)}) collective-permute-start(bf16[12,20,2,256]{3,0,2,1:T(8,128)(2,1)S(1)} %get-tuple-element.20), channel_id=1, source_target_pairs={{0,511},{31,480},{32,479},{63,448},{64,447},{95,416},{96,415},{127... | collective-permute-start | bytes 737288 | tf_op jit(solution)/shard_map/ppermute | solution.py:64
  45.9 6.6 %collective-permute-start.6 = (bf16[12,20,2,256]{3,0,2,1:T(8,128)(2,1)S(1)}, bf16[12,20,2,256]{3,0,2,1:T(8,128)(2,1)S(1)}, u32[]{:S(2)}, u32[]{:S(2)}) collective-permute-start(bf16[12,20,2,256]{3,0,2,1:T(8,128)(2,1)S(1)} %get-tuple-element.20), channel_id=1, source_target_pairs={{0,480},{31,511},{32,448},{63,479},{64,416},{95,447},{96,384},{127... | collective-permute-start | bytes 737288 | tf_op jit(solution)/shard_map/ppermute | solution.py:63
  52.7 4.9 %collective-permute-done.7 = bf16[12,20,2,256]{3,0,2,1:T(8,128)(2,1)S(1)} collective-permute-done((bf16[12,20,2,256]{3,0,2,1:T(8,128)(2,1)S(1)}, bf16[12,20,2,256]{3,0,2,1:T(8,128)(2,1)S(1)}, u32[]{:S(2)}, u32[]{:S(2)}) %collective-permute-start.7) | collective-permute-done | bytes 245792 | tf_op jit(solution)/shard_map/ppermute | solution.py:64
  57.6 5.5 %collective-permute-done.6 = bf16[12,20,2,256]{3,0,2,1:T(8,128)(2,1)S(1)} collective-permute-done((bf16[12,20,2,256]{3,0,2,1:T(8,128)(2,1)S(1)}, bf16[12,20,2,256]{3,0,2,1:T(8,128)(2,1)S(1)}, u32[]{:S(2)}, u32[]{:S(2)}) %collective-permute-start.6) | collective-permute-done | bytes 245792 | tf_op jit(solution)/shard_map/ppermute | solution.py:63
  63.5 1.7 %copy.131 = bf16[4,12,20,2,256]{4,3,2,1,0:T(2,128)(2,1)} copy(bf16[4,12,20,2,256]{4,1,3,2,0:T(8,128)(2,1)S(1)} %pad_maximum_fusion.2) | data formatting | bytes 1966080 | tf_op jit(solution)/shard_map/stack | solution.py:66
  65.3 3.0 %gather_fusion.1 = bf16[12,20,2,256]{3,2,1,0:T(2,128)(2,1)} fusion(bf16[48,20,2,256]{3,2,1,0:T(2,128)(2,1)} %bitcast.239, s32[1024]{0:T(1024)S(1)} %pad_clamp_fusion), kind=kCustom, calls=%fused_computation.1 | custom fusion | bytes 491568 | tf_op jit(solution)/shard_map/jit(_take)/gather | solution.py:74
  69.5 3.8 %fusion.41 = f32[12,16,8,128]{3,0,2,1:T(8,128)S(1)} fusion(bf16[3,3,256,128]{3,2,1,0:T(8,128)(2,1)} %param.9, bf16[12,20,2,256]{3,0,2,1:T(8,128)(2,1)S(1)} %get-tuple-element.41, bf16[12,2,8,256]{3,0,2,1:T(8,128)(2,1)S(1)} %get-tuple-element.43, bf16[12,16,8,256]{3,0,2,1:T(8,128)(2,1)S(1)} %copy.126, bf16[12,2,8,256]{3,0,2,1:T(8,128)(2,1)S(1)} %copy-done.3, ...), kind=kOutput, calls=%fused_computation.138 | convolution fusion | flops 908918784 | bytes 2850816 | tf_op jit(solution)/shard_map/conv_general_dilated | solution.py:95
  73.3 4.6 %fusion.26 = (bf16[12,16,8,128]{3,0,2,1:T(8,128)(2,1)S(1)}, bf16[12,16,8,128]{3,0,2,1:T(8,128)(2,1)}, bf16[12,16,8,128]{3,0,2,1:T(8,128)(2,1)S(1)}) fusion(f32[12,16,8,128]{3,0,2,1:T(8,128)S(1)} %fusion.41, bf16[12,16,8,128]{3,2,1,0:T(8,128)(2,1)S(1)} %copy-done.11, bf16[3,3,256,128]{3,2,1,0:T(8,128)(2,1)S(1)} %copy-done, ...), kind=kOutput, calls=%fused_computation.59 | convolution fusion | flops 918650880 | bytes 4423680 | tf_op jit(solution)/shard_map/conv_general_dilated | solution.py:92
  79.0 1.3 fusion.4
  82.6 1.4 fusion.18
  86.4 1.3 fusion.3
  88.8 1.1 fusion.10
  89.9 1.3 fusion.2
  93.5 1.4 fusion.17
  96.1 1.1 fusion.6
  97.2 1.2 fusion.1
  98.4 1.1 fusion.5
  99.6 2.4 %reshape.187 = f32[2,2,4,2,4,36,128]{6,5,4,3,2,1,0:T(8,128)S(1)} reshape(f32[18,256,128]{2,1,0:T(8,128)} %fusion.5) | data formatting | bytes 4718592 | tf_op jit(solution)/shard_map/reshape | solution.py:131
  102.5 24.6 %collective-permute-start.8 = (f32[2,2,4,4,36,128]{5,3,4,2,1,0:T(4,128)S(1)}, f32[2,2,4,4,36,128]{5,3,4,2,1,0:T(4,128)S(1)}, u32[]{:S(2)}, u32[]{:S(2)}) collective-permute-start(f32[2,2,4,4,36,128]{5,3,4,2,1,0:T(4,128)S(1)} %bitcast.240), channel_id=1, source_target_pairs={{0,32},{32,0},{1,33},{33,1},{2,34},{34,2},{3,35},{35,3},{4,36},{36... | collective-permute-start | bytes 3538952 | tf_op jit(solution)/shard_map/ppermute | solution.py:135
  127.1 2.5 %collective-permute-done.8 = f32[2,2,4,4,36,128]{5,3,4,2,1,0:T(4,128)S(1)} collective-permute-done((f32[2,2,4,4,36,128]{5,3,4,2,1,0:T(4,128)S(1)}, f32[2,2,4,4,36,128]{5,3,4,2,1,0:T(4,128)S(1)}, u32[]{:S(2)}, u32[]{:S(2)}) %collective-permute-start.8) | collective-permute-done | bytes 1179680 | tf_op jit(solution)/shard_map/ppermute | solution.py:135
  130.3 20.0 %all_to_all.10 = bf16[16,144,128]{2,1,0:T(8,128)(2,1)S(1)} all-to-all(bf16[16,144,128]{2,1,0:T(8,128)(2,1)S(1)} %copy.149), channel_id=1, replica_groups=mesh['yh'=2,'x'=4,'c'=2,'yl'=4,'z'=8] {'x','yl'}, dimensions={0} | all-to-all | bytes 1179648 | tf_op jit(solution)/shard_map/all_to_all | solution.py:137
  151.3 9.1 %all-to-all-start.1 = ((f32[16,16,128]{2,1,0:T(8,128)}), f32[16,16,128]{2,1,0:T(8,128)S(1)}, u32[]{:S(2)}, u32[]{:S(2)}) async-start(f32[16,16,128]{2,1,0:T(8,128)} %pad.4.clone), calls=%async_computation.1 | async-start | bytes 262144 | tf_op jit(solution)/shard_map/all_to_all | solution.py:145
  161.2 10.5 %all-to-all-done.1 = f32[16,16,128]{2,1,0:T(8,128)S(1)} async-done(((f32[16,16,128]{2,1,0:T(8,128)}), f32[16,16,128]{2,1,0:T(8,128)S(1)}, u32[]{:S(2)}, u32[]{:S(2)}) %all-to-all-start.1) | async-done | bytes 131104 | tf_op jit(solution)/shard_map/all_to_all | solution.py:145
  (86 shorter events, 21.9 us)
Async XLA Ops:
  0.6 72.6 %copy-start = (bf16[3,3,256,128]{3,2,1,0:T(8,128)(2,1)S(1)}, bf16[3,3,256,128]{3,2,1,0:T(8,128)(2,1)}, u32[]{:S(2)}) copy-start(bf16[3,3,256,128]{3,2,1,0:T(8,128)(2,1)} %param.8) | copy-start | bytes 1769476
  0.6 12.5 %copy-start.1 = (bf16[12,16,8,256]{3,2,1,0:T(8,128)(2,1)S(1)}, bf16[12,16,8,256]{3,2,1,0:T(8,128)(2,1)}, u32[]{:S(2)}) copy-start(bf16[12,16,8,256]{3,2,1,0:T(8,128)(2,1)} %param.7) | copy-start | bytes 2359300
  0.7 13.9 %copy-start.10 = (s32[12,4]{0,1:T(4,128)S(1)}, s32[12,4]{0,1:T(4,128)}, u32[]{:S(2)}) copy-start(s32[12,4]{0,1:T(4,128)} %param.13) | copy-start | bytes 580
  0.7 13.9 %copy-start.8 = (s32[12,4]{0,1:T(4,128)S(1)}, s32[12,4]{0,1:T(4,128)}, u32[]{:S(2)}) copy-start(s32[12,4]{0,1:T(4,128)} %param.11) | copy-start | bytes 580
  0.7 13.9 %copy-start.9 = (s32[12,4]{0,1:T(4,128)S(1)}, s32[12,4]{0,1:T(4,128)}, u32[]{:S(2)}) copy-start(s32[12,4]{0,1:T(4,128)} %param.12) | copy-start | bytes 580
  2.4 12.8 %collective-permute-start.1 = (bf16[12,2,8,256]{3,0,2,1:T(8,128)(2,1)S(1)}, bf16[12,2,8,256]{3,0,2,1:T(8,128)(2,1)S(1)}, u32[]{:S(2)}, u32[]{:S(2)}) collective-permute-start(bf16[12,2,8,256]{3,0,2,1:T(8,128)(2,1)S(1)} %get-tuple-element.33), channel_id=1, source_target_pairs={{32,0},{64,32},{96,64},{128,96},{160,128},{192,160},{224,192},{256... | collective-permute-start | bytes 294920 | tf_op jit(solution)/shard_map/ppermute | solution.py:31
  11.2 4.8 %collective-permute-start = (bf16[12,2,8,256]{3,0,2,1:T(8,128)(2,1)S(1)}, bf16[12,2,8,256]{3,0,2,1:T(8,128)(2,1)S(1)}, u32[]{:S(2)}, u32[]{:S(2)}) collective-permute-start(bf16[12,2,8,256]{3,0,2,1:T(8,128)(2,1)S(1)} %get-tuple-element.32), channel_id=1, source_target_pairs={{0,32},{32,64},{64,96},{96,128},{128,160},{160,192},{192,224},{224... | collective-permute-start | bytes 294920 | tf_op jit(solution)/shard_map/ppermute | solution.py:30
  16.1 1.4 collective-permute-start.3
  16.8 0.8 collective-permute-start.2
  18.5 11.8 %copy-start.2 = (bf16[12,2,8,256]{3,0,2,1:T(8,128)(2,1)}, bf16[12,2,8,256]{3,0,2,1:T(8,128)(2,1)S(1)}, u32[]{:S(2)}) copy-start(bf16[12,2,8,256]{3,0,2,1:T(8,128)(2,1)S(1)} %reverse_select_fusion.2) | copy-start | bytes 294916
  19.4 16.0 %collective-permute-start.5 = (bf16[12,20,2,256]{3,0,2,1:T(8,128)(2,1)}, bf16[12,20,2,256]{3,0,2,1:T(8,128)(2,1)S(1)}, u32[]{:S(2)}, u32[]{:S(2)}) collective-permute-start(bf16[12,20,2,256]{3,0,2,1:T(8,128)(2,1)} %get-tuple-element.31), channel_id=1, source_target_pairs={{1,0},{2,1},{3,2},{4,3},{5,4},{6,5},{7,6},{8,7},{9,8},{10,9},{11,1... | collective-permute-start | bytes 737288 | tf_op jit(solution)/shard_map/ppermute | solution.py:58
  30.4 11.8 %collective-permute-start.4 = (bf16[12,20,2,256]{3,0,2,1:T(8,128)(2,1)S(1)}, bf16[12,20,2,256]{3,0,2,1:T(8,128)(2,1)S(1)}, u32[]{:S(2)}, u32[]{:S(2)}) collective-permute-start(bf16[12,20,2,256]{3,0,2,1:T(8,128)(2,1)S(1)} %get-tuple-element.30), channel_id=1, source_target_pairs={{0,1},{1,2},{2,3},{3,4},{4,5},{5,6},{6,7},{7,8},{8,9},{9,10},{10,1... | collective-permute-start | bytes 737288 | tf_op jit(solution)/shard_map/ppermute | solution.py:57
  43.4 14.2 %collective-permute-start.7 = (bf16[12,20,2,256]{3,0,2,1:T(8,128)(2,1)S(1)}, bf16[12,20,2,256]{3,0,2,1:T(8,128)(2,1)S(1)}, u32[]{:S(2)}, u32[]{:S(2)}) collective-permute-start(bf16[12,20,2,256]{3,0,2,1:T(8,128)(2,1)S(1)} %get-tuple-element.20), channel_id=1, source_target_pairs={{0,511},{31,480},{32,479},{63,448},{64,447},{95,416},{96,415},{127... | collective-permute-start | bytes 737288 | tf_op jit(solution)/shard_map/ppermute | solution.py:64
  45.9 17.2 %collective-permute-start.6 = (bf16[12,20,2,256]{3,0,2,1:T(8,128)(2,1)S(1)}, bf16[12,20,2,256]{3,0,2,1:T(8,128)(2,1)S(1)}, u32[]{:S(2)}, u32[]{:S(2)}) collective-permute-start(bf16[12,20,2,256]{3,0,2,1:T(8,128)(2,1)S(1)} %get-tuple-element.20), channel_id=1, source_target_pairs={{0,480},{31,511},{32,448},{63,479},{64,416},{95,447},{96,384},{127... | collective-permute-start | bytes 737288 | tf_op jit(solution)/shard_map/ppermute | solution.py:63
  63.5 5.9 %copy-start.3 = (bf16[12,2,8,256]{3,0,2,1:T(8,128)(2,1)S(1)}, bf16[12,2,8,256]{3,0,2,1:T(8,128)(2,1)}, u32[]{:S(2)}) copy-start(bf16[12,2,8,256]{3,0,2,1:T(8,128)(2,1)} %copy-done.2) | copy-start | bytes 294916
  69.5 3.8 %copy-start.11 = (bf16[12,16,8,128]{3,2,1,0:T(8,128)(2,1)S(1)}, bf16[12,16,8,128]{3,2,1,0:T(8,128)(2,1)}, u32[]{:S(2)}) copy-start(bf16[12,16,8,128]{3,2,1,0:T(8,128)(2,1)} %param.10) | copy-start | bytes 1179652
  77.8 1.1 copy-start.4
  77.8 1.1 copy-start.7
  85.1 1.3 copy-start.6
  102.5 27.1 %collective-permute-start.8 = (f32[2,2,4,4,36,128]{5,3,4,2,1,0:T(4,128)S(1)}, f32[2,2,4,4,36,128]{5,3,4,2,1,0:T(4,128)S(1)}, u32[]{:S(2)}, u32[]{:S(2)}) collective-permute-start(f32[2,2,4,4,36,128]{5,3,4,2,1,0:T(4,128)S(1)} %bitcast.240), channel_id=1, source_target_pairs={{0,32},{32,0},{1,33},{33,1},{2,34},{34,2},{3,35},{35,3},{4,36},{36... | collective-permute-start | bytes 3538952 | tf_op jit(solution)/shard_map/ppermute | solution.py:135
  130.2 30.2 %copy-start.5 = (bf16[12,16,8,128]{3,0,2,1:T(8,128)(2,1)S(1)}, bf16[12,16,8,128]{3,0,2,1:T(8,128)(2,1)}, u32[]{:S(2)}) copy-start(bf16[12,16,8,128]{3,0,2,1:T(8,128)(2,1)} %get-tuple-element.28) | copy-start | bytes 1179652
  151.3 20.5 %all-to-all-start.1 = ((f32[16,16,128]{2,1,0:T(8,128)}), f32[16,16,128]{2,1,0:T(8,128)S(1)}, u32[]{:S(2)}, u32[]{:S(2)}) async-start(f32[16,16,128]{2,1,0:T(8,128)} %pad.4.clone), calls=%async_computation.1 | async-start | bytes 262144 | tf_op jit(solution)/shard_map/all_to_all | solution.py:145

commit v2 on v1

v2 whole, which is shorter than its diff:
```python
import jax
import jax.numpy as jnp
from jax import lax
from jax.experimental import pallas as pl
from jax.experimental.pallas import tpu as pltpu
from jax.sharding import Mesh
from jax.sharding import PartitionSpec as P

ROWS = ("yh", "x", "c")
COLS = ("yl", "z")


def turned(cells):
    return jnp.transpose(cells, (0, 2, 1, 3))


def halos(state, seam_face, seam_code, corner_mask):
    count, height, width, _ = state.shape
    n_row = lax.axis_size(ROWS)
    n_col = lax.axis_size(COLS)
    r = lax.axis_index(ROWS)
    k = lax.axis_index(COLS)
    row_last = n_row - 1
    col_last = n_col - 1
    everywhere = ROWS + COLS
    top, bottom = r == 0, r == row_last
    west_end, east_end = k == 0, k == col_last

    def place(i, j):
        return i * n_col + j

    north, south = state[:, :2], state[:, height - 2 :]
    west, east = state[:, :, :2], state[:, :, width - 2 :]
    own_row = turned(jnp.where(top, north, jnp.flip(south, 1)))
    own_col = jnp.where(west_end, west, jnp.flip(east, 2))
    own = jnp.concatenate([own_row, own_col], axis=1)
    edges = [
        (i, j) for i in range(n_row) for j in range(n_col) if i in (0, row_last) or j in (0, col_last)
    ]

    def image(flip_row, flip_col):
        pairs = [
            (place(i, j), place(row_last - i if flip_row else i, col_last - j if flip_col else j))
            for i, j in edges
        ]
        got = lax.ppermute(own, everywhere, pairs)
        return got[:, :width], got[:, width:]

    from_above = lax.ppermute(south, ROWS, [(i, i + 1) for i in range(row_last)])
    from_below = lax.ppermute(north, ROWS, [(i + 1, i) for i in range(row_last)])
    row_x, col_x = image(False, True)
    row_y, col_y = image(True, False)
    row_xy, col_xy = image(True, True)

    def picked(options, index):
        options = jnp.stack(options)
        return jnp.take(options.reshape((4 * count,) + options.shape[2:]), index, axis=0)

    flip_x, flip_xy = jnp.flip(row_x, 1), jnp.flip(row_xy, 1)
    row_index = jnp.where(
        top, seam_code[:, 0] * count + seam_face[:, 0], seam_code[:, 1] * count + seam_face[:, 1]
    )
    row_pick = picked(
        [
            jnp.where(top, own_row, row_y),
            jnp.where(top, flip_x, flip_xy),
            jnp.where(top, row_y, own_row),
            jnp.where(top, flip_xy, flip_x),
        ],
        row_index,
    )
    row_pick = turned(row_pick)
    above = jnp.where(top, jnp.flip(row_pick, 1), from_above)
    below = jnp.where(bottom, row_pick, from_below)

    col_index = jnp.where(
        west_end, seam_code[:, 2] * count + seam_face[:, 2], seam_code[:, 3] * count + seam_face[:, 3]
    )
    flip_y, flip_xy = jnp.flip(col_y, 1), jnp.flip(col_xy, 1)
    col_pick = picked(
        [
            jnp.where(west_end, own_col, col_x),
            jnp.where(west_end, flip_y, flip_xy),
            jnp.where(west_end, col_x, own_col),
            jnp.where(west_end, flip_xy, flip_y),
        ],
        col_index,
    )

    to_right = jnp.concatenate([above[:, :, width - 2 :], east, below[:, :, width - 2 :]], axis=1)
    to_left = jnp.concatenate([above[:, :, :2], west, below[:, :, :2]], axis=1)
    from_left = lax.ppermute(to_right, COLS, [(j, j + 1) for j in range(col_last)])
    from_right = lax.ppermute(to_left, COLS, [(j + 1, j) for j in range(col_last)])
    half = n_row // 2
    along = [(i, j) for i in range(row_last) if i != half - 1 for j in (0, col_last)]
    end_above = lax.ppermute(
        col_pick[:, height - 2 :], everywhere, [(place(i, j), place(i + 1, j)) for i, j in along]
    )
    end_below = lax.ppermute(
        col_pick[:, :2], everywhere, [(place(i + 1, j), place(i, j)) for i, j in along]
    )

    def rows_of(cols):
        return jnp.where(r == half, cols[:, height - 2 :], cols[:, :2])

    back, back_x = jnp.flip(own_col, 1), jnp.flip(col_x, 1)
    middle = [
        jnp.where(west_end, rows_of(col_y), rows_of(col_xy)),
        jnp.where(west_end, rows_of(back), rows_of(back_x)),
        jnp.where(west_end, rows_of(col_xy), rows_of(col_y)),
        jnp.where(west_end, rows_of(back_x), rows_of(back)),
    ]

    def block(rows, is_west):
        cells = jnp.where(is_west, rows[:, :2], jnp.flip(rows[:, width - 2 :], 1))
        return turned(cells)

    corner = [
        block(own_row, west_end),
        block(row_x, ~west_end),
        block(row_y, west_end),
        block(row_xy, ~west_end),
    ]
    down = bottom.astype(jnp.int32)
    right = east_end.astype(jnp.int32)
    code = jnp.where(west_end, seam_code[:, 2], seam_code[:, 3])
    face = jnp.where(west_end, seam_face[:, 2], seam_face[:, 3])
    side = down ^ (code & 1)
    inner_code = jnp.where(side == 0, seam_code[face, 0], seam_code[face, 1])
    inner_face = jnp.where(side == 0, seam_face[face, 0], seam_face[face, 1])
    column = (code >> 1) ^ (inner_code & 1)
    which = 2 * ((inner_code >> 1) ^ down) + (column ^ right)
    corner_index = which * count + inner_face

    in_corner = top | bottom
    ends = picked(
        [jnp.where(in_corner, a, b) for a, b in zip(corner, middle)],
        jnp.where(in_corner, corner_index, col_index),
    )
    mask = jnp.where(
        top,
        jnp.where(west_end, corner_mask[:, 0], corner_mask[:, 1]),
        jnp.where(west_end, corner_mask[:, 2], corner_mask[:, 3]),
    )
    ends = jnp.where((in_corner & (mask == 0))[:, None, None, None], 0, ends)
    end_above = jnp.where(top, jnp.flip(ends, 1), jnp.where(r == half, ends, end_above))
    end_below = jnp.where(bottom | (r == half - 1), ends, end_below)
    edge = jnp.concatenate([end_above, col_pick, end_below], axis=1)
    left = turned(jnp.where(west_end, jnp.flip(edge, 2), from_left))
    right = turned(jnp.where(east_end, edge, from_right))

    upper = jnp.concatenate([left[:, :, :2], turned(above), right[:, :, :2]], axis=1)
    lower = jnp.concatenate([left[:, :, height + 2 :], turned(below), right[:, :, height + 2 :]], axis=1)
    return left[:, :, 2 : height + 2], right[:, :, 2 : height + 2], upper, lower


def compute_kernel(st_ref, lf_ref, rt_ref, up_ref, lo_ref, wg_ref, wd_ref, hg_ref, hidden_ref, out_ref, x_ref, dg_ref, dv_ref):
    _, faces, wide, height, c_in = x_ref.shape
    width = wide - 4
    c_out = hg_ref.shape[-1]
    dg_ref[...] = jnp.zeros(dg_ref.shape, dg_ref.dtype)
    dv_ref[...] = jnp.zeros(dv_ref.shape, dv_ref.dtype)
    step = 1
    cells = step * width * height

    def forward(n, _):
        f = n * step
        here = pl.ds(f, step)

        mid = jnp.concatenate([lf_ref[here], st_ref[here], rt_ref[here]], axis=1)
        x_ref[2, here] = mid
        mid = mid.astype(jnp.float32)
        above = up_ref[here].astype(jnp.float32)
        below = lo_ref[here].astype(jnp.float32)
        for shift, parts in (
            (0, [above, mid[:, :, : height - 2]]),
            (1, [above[:, :, 1:], mid[:, :, : height - 1]]),
            (3, [mid[:, :, 1:], below[:, :, :1]]),
            (4, [mid[:, :, 2:], below]),
        ):
            x_ref[shift, here] = jnp.concatenate(parts, axis=2).astype(jnp.bfloat16)

        def windows(spacing, first):
            return jnp.concatenate(
                [
                    x_ref[first + a * spacing, here, pl.ds(first + b * spacing, width)].reshape(cells, c_in)
                    for a in range(3)
                    for b in range(3)
                ],
                axis=1,
            )

        gate = jnp.dot(windows(1, 1), wg_ref[...], preferred_element_type=jnp.float32)
        value = jnp.dot(windows(2, 0), wd_ref[...], preferred_element_type=jnp.float32)
        root = (2.0 / jnp.pi) ** 0.5
        square = gate * gate
        t = jnp.tanh(root * gate * (1.0 + 0.044715 * square))
        half = 0.5 * (1.0 + t)
        act = gate * half
        slope = half + 0.5 * gate * (1.0 - t * t) * (root * (1.0 + 3 * 0.044715 * square))
        shape = (step, width, height, c_out)
        up = hg_ref[here].astype(jnp.float32).reshape(cells, c_out)
        hidden_ref[here] = (act * value).astype(jnp.bfloat16).reshape(shape)
        dgate = (up * value * slope).astype(jnp.bfloat16).reshape(shape)
        dvalue = (up * act).astype(jnp.bfloat16).reshape(shape)
        for b in range(3):
            lanes = pl.ds(b * c_out, c_out)
            dg_ref[here, pl.ds(b, width), :, lanes] = dgate
            dv_ref[here, pl.ds(2 * b, width), :, lanes] = dvalue
        return 0

    lax.fori_loop(0, faces // step, forward, 0, unroll=True)

    span = out_ref.shape[3]

    def put(grad, tap, block):
        start, end = tap * c_in, (tap + 1) * c_in
        at = start
        while at < end:
            chunk = at // span
            stop = min(end, (chunk + 1) * span)
            out_ref[chunk % 2, chunk // 2, grad, pl.ds(at - chunk * span, stop - at)] = block[at - start : stop - start]
            at = stop

    for a in range(3):
        for grad, row, cols, delta in ((0, 1 + a, pl.ds(1, wide - 2), dg_ref), (1, 2 * a, pl.ds(0, wide), dv_ref)):
            x = x_ref[row, :, cols].reshape(-1, c_in)
            d = delta[...].reshape(-1, 3 * c_out)
            sums = lax.dot_general(x, d, (((0,), (0,)), ((), ())), preferred_element_type=jnp.float32)
            for b in range(3):
                put(grad, a * 3 + b, sums[:, b * c_out : (b + 1) * c_out])


def compute(st, lf, rt, up, lo, wg, wd, hg):
    faces, width, height, c_in = st.shape
    wide = width + 4
    c_out = wg.shape[-1]
    vm = pl.BlockSpec(memory_space=pltpu.VMEM)
    return pl.pallas_call(
        compute_kernel,
        in_specs=[vm] * 8,
        out_specs=[vm] * 2,
        out_shape=[
            jax.ShapeDtypeStruct(hg.shape, jnp.bfloat16),
            jax.ShapeDtypeStruct((2, 8, 2, 9 * c_in // 16, c_out), jnp.float32),
        ],
        scratch_shapes=[
            pltpu.VMEM((5, faces, wide, height, c_in), jnp.bfloat16),
            pltpu.VMEM((faces, wide - 2, height, 3 * c_out), jnp.bfloat16),
            pltpu.VMEM((faces, wide, height, 3 * c_out), jnp.bfloat16),
        ],
        compiler_params=pltpu.CompilerParams(vmem_limit_bytes=56 * 2**20),
        name="gated_conv",
    )(st, lf, rt, up, lo, wg.reshape(-1, c_out), wd.reshape(-1, c_out), hg)


def on_device(state, gate_kernel, dilated_kernel, hidden_grad, seam_face, seam_code, corner_mask):
    count, height, width, _ = state.shape
    left, right, upper, lower = halos(state, seam_face, seam_code, corner_mask)
    hidden, terms = compute(
        turned(state), left, right, upper, lower, gate_kernel, dilated_kernel, turned(hidden_grad)
    )
    cells = count * height * width * lax.axis_size(ROWS) * lax.axis_size(COLS)
    gate_part, dilated_part = scattered_sum(terms, cells ** (-0.5))
    return (turned(hidden), gate_part, dilated_part)


def scattered_sum(terms, scale):
    _, spots, grads, span, lanes = terms.shape
    halves = lax.all_to_all(terms, "c", 0, 0)
    sends = (halves[0] + halves[1]).astype(jnp.bfloat16).reshape(spots, grads * span, lanes)
    arrived = lax.all_to_all(sends, ("yh", "x"), 0, 0)
    part = jnp.sum(arrived.astype(jnp.float32), axis=0).reshape(grads, span, lanes)
    takers = lax.axis_size(COLS)
    share = span * lanes // takers
    tall = -(-(share + lanes // 2) // lanes)
    starts = [i * share // lanes for i in range(takers)]
    sends = jnp.stack([part[:, s : s + tall].reshape(grads * tall, lanes) for s in starts])
    sends = jnp.pad(sends, ((0, 0), (0, -grads * tall % 8), (0, 0)))
    arrived = lax.all_to_all(sends, COLS, 0, 0)
    total = jnp.sum(arrived[:, : grads * tall], axis=0).reshape(grads, tall * lanes) * scale
    skip = lax.axis_index(COLS) * share % lanes
    total = lax.dynamic_slice_in_dim(total, skip, share, axis=1)
    return total[0], total[1]


def solution(mesh):
    fine = Mesh(mesh.devices.reshape(2, 4, 2, 4, 8), ROWS + COLS)
    cells = P(None, ROWS, COLS, None)
    return jax.shard_map(
        on_device,
        mesh=fine,
        in_specs=(cells, P(), P(), cells, P(), P(), P()),
        out_specs=(cells, P(ROWS + COLS), P(ROWS + COLS)),
        check_vma=False,
    )
```

time: 174 us -> 131 us (0.75)
  the two profiles are of different devices: /device:TPU:1 before, /device:TPU:56 now
where the time goes in v2:
time: 131 us
  starting transfers between devices  45.8 us (35%)
  blocking collectives  35.1 us (27%)
  local copies, waits for them, and re-layouts  16.8 us (13%)
  Pallas kernels  10.9 us (8%)
  other arithmetic  10.2 us (8%)
  waiting for transfers between devices  9.79 us (7%)
  between operations  2.01 us (2%)
    all_to_all x1, blocking collectives, scattered_sum(): arrived = lax.all_to_all(sends, ('yh', 'x'), 0, 0)  28.2 us
    all_to_all x1, starting transfers between devices, scattered_sum(): arrived = lax.all_to_all(sends, COLS, 0, 0)  17 us
    pallas_call x1, Pallas kernels, compute(): pl.pallas_call(compute_kernel, in_specs=[vm] * 8, out_specs=[vm] * 2, out...  10.9 us
    all_to_all x1, waiting for transfers between devices, scattered_sum(): arrived = lax.all_to_all(sends, COLS, 0, 0)  9.77 us
    ppermute x1, starting transfers between devices, halos(): lax.ppermute(north, ROWS, [(i + 1, i) for i in range(row_last)])  9.66 us
    ppermute x1, starting transfers between devices, halos(): lax.ppermute(to_left, COLS, [(j + 1, j) for j in range(col_last)])  9.37 us
    all_to_all x1, blocking collectives, scattered_sum(): halves = lax.all_to_all(terms, 'c', 0, 0)  6.85 us
    another operation x12, other arithmetic, picked(): options = jnp.stack(options)  4.34 us
  transfers between devices with their start and end apart: 10, of which 1 were waited for; matrix products, arithmetic and copies ran while one was open for 15% of the time, Pallas kernels for 0%

profile of v2, /device:TPU:56, one launch (start us, length us, event | category | flops | bytes accessed | tf_op | source)
XLA Modules:
  0.0 130.6 jit_solution(8284351989840002916)
XLA Ops:
  0.6 1.3 copy.147
  2.9 1.5 %fusion.21 = (bf16[12,16,2,256]{3,2,1,0:T(2,128)(2,1)S(1)}, bf16[12,16,2,256]{3,2,1,0:T(2,128)(2,1)S(1)}) fusion(bf16[12,16,8,256]{3,2,1,0:T(8,128)(2,1)} %param.7, bf16[12,16,2,256]{3,1,2,0:T(8,128)(2,1)S(1)} %rev.49, pred[]{:T(512)S(6)} %eq.42), kind=kLoop, calls=%fused_computation.137 | loop fusion | flops 98304 | bytes 786433 | tf_op jit(solution)/shard_map/slice | solution.py:33
  4.6 0.7 collective-permute-start.1
  6.0 0.7 collective-permute-start
  6.7 1.9 %collective-permute-start.5 = (bf16[12,2,8,256]{3,1,2,0:T(2,128)(2,1)S(1)}, bf16[12,2,8,256]{3,1,2,0:T(2,128)(2,1)S(1)}, u32[]{:S(2)}, u32[]{:S(2)}) collective-permute-start(bf16[12,2,8,256]{3,1,2,0:T(2,128)(2,1)S(1)} %slice.403), channel_id=1, source_target_pairs={{0,32},{32,64},{64,96},{96,128},{128,160},{160,192},{192,224},{224... | collective-permute-start | bytes 294920 | tf_op jit(solution)/shard_map/ppermute | solution.py:49
  8.6 9.7 %collective-permute-start.6 = (bf16[12,2,8,256]{3,1,2,0:T(2,128)(2,1)S(1)}, bf16[12,2,8,256]{3,1,2,0:T(2,128)(2,1)S(1)}, u32[]{:S(2)}, u32[]{:S(2)}) collective-permute-start(bf16[12,2,8,256]{3,1,2,0:T(2,128)(2,1)S(1)} %get-tuple-element.32), channel_id=1, source_target_pairs={{32,0},{64,32},{96,64},{128,96},{160,128},{192,160},{224,192},{256... | collective-permute-start | bytes 294920 | tf_op jit(solution)/shard_map/ppermute | solution.py:50
  18.9 0.7 gather_fusion.3
  19.6 0.7 gather_fusion.1
  20.4 0.7 gather_fusion.2
  21.1 0.7 gather_fusion
  22.0 0.8 slice.318
  22.7 0.8 slice.320
  23.5 0.8 rev.48
  24.3 0.8 copy.146
  26.8 0.7 pad_maximum_fusion.1
  27.5 0.7 gather_fusion.6
  29.4 4.3 %collective-permute-start.7 = (bf16[12,20,2,256]{3,1,2,0:T(8,128)(2,1)S(1)}, bf16[12,20,2,256]{3,1,2,0:T(8,128)(2,1)S(1)}, u32[]{:S(2)}, u32[]{:S(2)}) collective-permute-start(bf16[12,20,2,256]{3,1,2,0:T(8,128)(2,1)S(1)} %pad_maximum_fusion.3), channel_id=1, source_target_pairs={{0,1},{1,2},{2,3},{3,4},{4,5},{5,6},{6,7},{7,8},{8,9},{9,10},{10,1... | collective-permute-start | bytes 737288 | tf_op jit(solution)/shard_map/ppermute | solution.py:92
  33.9 9.4 %collective-permute-start.8 = (bf16[12,20,2,256]{3,1,2,0:T(8,128)(2,1)S(1)}, bf16[12,20,2,256]{3,1,2,0:T(8,128)(2,1)S(1)}, u32[]{:S(2)}, u32[]{:S(2)}) collective-permute-start(bf16[12,20,2,256]{3,1,2,0:T(8,128)(2,1)S(1)} %pad_maximum_fusion.4), channel_id=1, source_target_pairs={{1,0},{2,1},{3,2},{4,3},{5,4},{6,5},{7,6},{8,7},{9,8},{10,9},{11,1... | collective-permute-start | bytes 737288 | tf_op jit(solution)/shard_map/ppermute | solution.py:93
  44.6 1.5 %pad_maximum_fusion = bf16[4,12,16,2,256]{4,3,2,1,0:T(2,128)(2,1)S(1)} fusion(bf16[1,12,16,2,256]{4,3,2,1,0:T(2,128)(2,1)S(1)} %fusion.3, bf16[1,12,16,2,256]{4,3,2,1,0:T(2,128)(2,1)S(1)} %get-tuple-element.36, bf16[1,12,16,2,256]{4,3,2,1,0:T(2,128)(2,1)S(1)} %copy.95, bf16[1,12,16,2,256]{4,3,2,1,0:T(2,128)(2,1)S(1)} %get-tuple-element.35), kind=kLoop, calls=%fused_computation.10 | loop fusion | flops 1179648 | bytes 1572864 | tf_op jit(solution)/shard_map/stack | solution.py:56
  48.2 0.8 collective-permute-start.3
  49.2 1.0 fusion.15
  51.7 0.7 slice.434.rt_ref
  52.6 0.7 slice.431.lf_ref
  53.4 1.1 pad_maximum_fusion.5
  54.5 10.9 %gated_conv.1 = (bf16[12,8,16,128]{3,2,1,0:T(8,128)(2,1)}, f32[2,8,2,144,128]{4,3,2,1,0:T(8,128)}) custom-call(bf16[12,8,16,256]{3,2,1,0:T(8,128)(2,1)} %bitcast.100, bf16[12,2,16,256]{3,2,1,0:T(8,128)(2,1)} %slice.431.lf_ref, bf16[12,2,16,256]{3,2,1,0:T(8,128)(2,1)} %slice.434.rt_ref, bf16[12,12,2,256]{3,2,1,0:T(2,128)(2,1)} %get-tuple-element.102.up_ref, ...), custom_call_target="tpu_custom_call" | custom-call | tf_op jit(solution)/shard_map/gated_conv/pallas_call | solution.py:239
  65.4 6.8 %all_to_all.15 = f32[2,8,2,144,128]{4,3,2,1,0:T(8,128)S(1)} all-to-all(f32[2,8,2,144,128]{4,3,2,1,0:T(8,128)} %get-tuple-element.6), channel_id=1, replica_groups=mesh['yh'=2,'x'=4,'c'=2,'yl'=4,'z'=8] {'c'}, dimensions={0} | all-to-all | bytes 4718592 | tf_op jit(solution)/shard_map/all_to_all | solution.py:270
  72.4 28.2 %all_to_all.16 = bf16[8,288,128]{2,1,0:T(8,128)(2,1)S(1)} all-to-all(bf16[8,288,128]{2,1,0:T(8,128)(2,1)S(1)} %bitcast.102), channel_id=1, replica_groups=mesh['yh'=2,'x'=4,'c'=2,'yl'=4,'z'=8] {'yh','x'}, dimensions={0} | all-to-all | bytes 1179648 | tf_op jit(solution)/shard_map/all_to_all | solution.py:272
  101.5 0.7 pad.6
  102.2 17.0 %all-to-all-start.2 = ((f32[32,16,128]{2,1,0:T(8,128)}), f32[32,16,128]{2,1,0:T(8,128)S(1)}, u32[]{:S(2)}, u32[]{:S(2)}) async-start(f32[32,16,128]{2,1,0:T(8,128)} %pad.6), calls=%async_computation.2 | async-start | bytes 524288 | tf_op jit(solution)/shard_map/all_to_all | solution.py:280
  119.3 0.8 copy.105
  120.1 9.8 %all-to-all-done.2 = f32[32,16,128]{2,1,0:T(8,128)S(1)} async-done(((f32[32,16,128]{2,1,0:T(8,128)}), f32[32,16,128]{2,1,0:T(8,128)S(1)}, u32[]{:S(2)}, u32[]{:S(2)}) %all-to-all-start.2) | async-done | bytes 262176 | tf_op jit(solution)/shard_map/all_to_all | solution.py:280
  129.9 0.7 dynamic-slice_reduce_fusion
  (173 shorter events, 10.8 us)
Async XLA Ops:
  1.9 2.4 %copy-start.2 = (bf16[12,16,8,256]{3,1,2,0:T(8,128)(2,1)}, bf16[12,16,8,256]{3,1,2,0:T(8,128)(2,1)S(1)}, u32[]{:S(2)}) copy-start(bf16[12,16,8,256]{3,1,2,0:T(8,128)(2,1)S(1)} %copy.147) | copy-start | bytes 2359300
  2.8 20.7 %copy-start.5 = (bf16[12,8,2,256]{3,1,2,0:T(8,128)(2,1)}, bf16[12,8,2,256]{3,1,2,0:T(8,128)(2,1)S(1)}, u32[]{:S(2)}) copy-start(bf16[12,8,2,256]{3,1,2,0:T(8,128)(2,1)S(1)} %get-tuple-element.96) | copy-start | bytes 294916
  2.8 15.5 %copy-start = (s32[12,4]{0,1:T(4,128)S(1)}, s32[12,4]{0,1:T(4,128)}, u32[]{:S(2)}) copy-start(s32[12,4]{0,1:T(4,128)} %param.11) | copy-start | bytes 580
  2.8 15.5 %copy-start.1 = (s32[12,4]{0,1:T(4,128)S(1)}, s32[12,4]{0,1:T(4,128)}, u32[]{:S(2)}) copy-start(s32[12,4]{0,1:T(4,128)} %param.12) | copy-start | bytes 580
  4.6 21.7 %collective-permute-start.1 = (bf16[12,24,2,256]{3,2,1,0:T(2,128)(2,1)S(1)}, bf16[12,24,2,256]{3,2,1,0:T(2,128)(2,1)S(1)}, u32[]{:S(2)}, u32[]{:S(2)}) collective-permute-start(bf16[12,24,2,256]{3,2,1,0:T(2,128)(2,1)S(1)} %copy.70), channel_id=1, source_target_pairs={{0,511},{1,510},{2,509},{3,508},{4,507},{5,506},{6,505},{7,504},{8... | collective-permute-start | bytes 884744 | tf_op jit(solution)/shard_map/ppermute | solution.py:46
  5.3 21.3 %collective-permute-start.2 = (bf16[12,24,2,256]{3,2,1,0:T(2,128)(2,1)S(1)}, bf16[12,24,2,256]{3,2,1,0:T(2,128)(2,1)S(1)}, u32[]{:S(2)}, u32[]{:S(2)}) collective-permute-start(bf16[12,24,2,256]{3,2,1,0:T(2,128)(2,1)S(1)} %copy.70), channel_id=1, source_target_pairs={{0,31},{1,30},{2,29},{3,28},{4,27},{5,26},{6,25},{7,24},{8,23},{9,... | collective-permute-start | bytes 884744 | tf_op jit(solution)/shard_map/ppermute | solution.py:46
  6.0 20.2 %collective-permute-start = (bf16[12,24,2,256]{3,1,2,0:T(8,128)(2,1)S(1)}, bf16[12,24,2,256]{3,1,2,0:T(8,128)(2,1)S(1)}, u32[]{:S(2)}, u32[]{:S(2)}) collective-permute-start(bf16[12,24,2,256]{3,1,2,0:T(8,128)(2,1)S(1)} %constant_dynamic-update-slice_fusion), channel_id=1, source_target_pairs={{0,480},{1,481},{2,482},{3,483},{4,484},{5,485},{6,486},{7,487},{8... | collective-permute-start | bytes 884744 | tf_op jit(solution)/shard_map/ppermute | solution.py:46
  6.7 22.5 %collective-permute-start.5 = (bf16[12,2,8,256]{3,1,2,0:T(2,128)(2,1)S(1)}, bf16[12,2,8,256]{3,1,2,0:T(2,128)(2,1)S(1)}, u32[]{:S(2)}, u32[]{:S(2)}) collective-permute-start(bf16[12,2,8,256]{3,1,2,0:T(2,128)(2,1)S(1)} %slice.403), channel_id=1, source_target_pairs={{0,32},{32,64},{64,96},{96,128},{128,160},{160,192},{192,224},{224... | collective-permute-start | bytes 294920 | tf_op jit(solution)/shard_map/ppermute | solution.py:49
  8.6 19.7 %collective-permute-start.6 = (bf16[12,2,8,256]{3,1,2,0:T(2,128)(2,1)S(1)}, bf16[12,2,8,256]{3,1,2,0:T(2,128)(2,1)S(1)}, u32[]{:S(2)}, u32[]{:S(2)}) collective-permute-start(bf16[12,2,8,256]{3,1,2,0:T(2,128)(2,1)S(1)} %get-tuple-element.32), channel_id=1, source_target_pairs={{32,0},{64,32},{96,64},{128,96},{160,128},{192,160},{224,192},{256... | collective-permute-start | bytes 294920 | tf_op jit(solution)/shard_map/ppermute | solution.py:50
  19.6 4.7 %copy-start.3 = (bf16[12,16,8,128]{3,2,1,0:T(8,128)(2,1)S(1)}, bf16[12,16,8,128]{3,2,1,0:T(8,128)(2,1)}, u32[]{:S(2)}) copy-start(bf16[12,16,8,128]{3,2,1,0:T(8,128)(2,1)} %param.10) | copy-start | bytes 1179652
  20.4 5.3 %copy-start.12 = (s32[12,4]{0,1:T(4,128)S(1)}, s32[12,4]{0,1:T(4,128)}, u32[]{:S(2)}) copy-start(s32[12,4]{0,1:T(4,128)} %param.13) | copy-start | bytes 580
  29.4 23.1 %collective-permute-start.7 = (bf16[12,20,2,256]{3,1,2,0:T(8,128)(2,1)S(1)}, bf16[12,20,2,256]{3,1,2,0:T(8,128)(2,1)S(1)}, u32[]{:S(2)}, u32[]{:S(2)}) collective-permute-start(bf16[12,20,2,256]{3,1,2,0:T(8,128)(2,1)S(1)} %pad_maximum_fusion.3), channel_id=1, source_target_pairs={{0,1},{1,2},{2,3},{3,4},{4,5},{5,6},{6,7},{7,8},{8,9},{9,10},{10,1... | collective-permute-start | bytes 737288 | tf_op jit(solution)/shard_map/ppermute | solution.py:92
  33.9 17.6 %collective-permute-start.8 = (bf16[12,20,2,256]{3,1,2,0:T(8,128)(2,1)S(1)}, bf16[12,20,2,256]{3,1,2,0:T(8,128)(2,1)S(1)}, u32[]{:S(2)}, u32[]{:S(2)}) collective-permute-start(bf16[12,20,2,256]{3,1,2,0:T(8,128)(2,1)S(1)} %pad_maximum_fusion.4), channel_id=1, source_target_pairs={{1,0},{2,1},{3,2},{4,3},{5,4},{6,5},{7,6},{8,7},{9,8},{10,9},{11,1... | collective-permute-start | bytes 737288 | tf_op jit(solution)/shard_map/ppermute | solution.py:93
  46.0 0.8 copy-start.9
  46.0 2.0 %copy-start.7 = (bf16[12,2,2,256]{3,1,2,0:T(2,128)(2,1)S(1)}, bf16[12,2,2,256]{3,1,2,0:T(2,128)(2,1)}, u32[]{:S(2)}) copy-start(bf16[12,2,2,256]{3,1,2,0:T(2,128)(2,1)} %slice.318) | copy-start | bytes 73732
  46.1 2.0 %copy-start.8 = (bf16[12,2,2,256]{3,1,2,0:T(2,128)(2,1)S(1)}, bf16[12,2,2,256]{3,1,2,0:T(2,128)(2,1)}, u32[]{:S(2)}) copy-start(bf16[12,2,2,256]{3,1,2,0:T(2,128)(2,1)} %slice.320) | copy-start | bytes 73732
  46.2 3.0 %copy-start.6 = (bf16[12,2,2,256]{3,1,2,0:T(2,128)(2,1)S(1)}, bf16[12,2,2,256]{3,1,2,0:T(2,128)(2,1)}, u32[]{:S(2)}) copy-start(bf16[12,2,2,256]{3,1,2,0:T(2,128)(2,1)} %rev.48) | copy-start | bytes 73732
  46.2 4.8 %copy-start.10 = (pred[12]{0:T(512)(128)(4,1)S(1)}, pred[12]{0:T(512)(128)(4,1)}, u32[]{:S(2)}) copy-start(pred[12]{0:T(512)(128)(4,1)} %get-tuple-element.19) | copy-start | bytes 40
  46.2 4.8 %copy-start.11 = (pred[12]{0:T(512)(128)(4,1)S(1)}, pred[12]{0:T(512)(128)(4,1)}, u32[]{:S(2)}) copy-start(pred[12]{0:T(512)(128)(4,1)} %and_bitcast_fusion.3) | copy-start | bytes 40
  47.0 4.0 %collective-permute-start.4 = (bf16[12,2,2,256]{3,1,2,0:T(2,128)(2,1)S(1)}, bf16[12,2,2,256]{3,1,2,0:T(2,128)(2,1)S(1)}, u32[]{:S(2)}, u32[]{:S(2)}) collective-permute-start(bf16[12,2,2,256]{3,1,2,0:T(2,128)(2,1)S(1)} %get-tuple-element.55), channel_id=1, source_target_pairs={{32,0},{63,31},{64,32},{95,63},{96,64},{127,95},{128,96},{159,127}... | collective-permute-start | bytes 73736 | tf_op jit(solution)/shard_map/ppermute | solution.py:99
  48.2 3.2 %collective-permute-start.3 = (bf16[12,2,2,256]{3,1,2,0:T(2,128)(2,1)S(1)}, bf16[12,2,2,256]{3,1,2,0:T(2,128)(2,1)S(1)}, u32[]{:S(2)}, u32[]{:S(2)}) collective-permute-start(bf16[12,2,2,256]{3,1,2,0:T(2,128)(2,1)S(1)} %get-tuple-element.54), channel_id=1, source_target_pairs={{0,32},{31,63},{32,64},{63,95},{64,96},{95,127},{96,128},{127,159}... | collective-permute-start | bytes 73736 | tf_op jit(solution)/shard_map/ppermute | solution.py:96
  100.8 18.5 %copy-start.4 = (bf16[12,8,16,128]{3,2,1,0:T(8,128)(2,1)S(1)}, bf16[12,8,16,128]{3,2,1,0:T(8,128)(2,1)}, u32[]{:S(2)}) copy-start(bf16[12,8,16,128]{3,2,1,0:T(8,128)(2,1)} %get-tuple-element.5) | copy-start | bytes 1179652
  102.2 27.7 %all-to-all-start.2 = ((f32[32,16,128]{2,1,0:T(8,128)}), f32[32,16,128]{2,1,0:T(8,128)S(1)}, u32[]{:S(2)}, u32[]{:S(2)}) async-start(f32[32,16,128]{2,1,0:T(8,128)} %pad.6), calls=%async_computation.2 | async-start | bytes 524288 | tf_op jit(solution)/shard_map/all_to_all | solution.py:280

commit v3 on v2

v3 whole, which is shorter than its diff:
```python
import jax
import jax.numpy as jnp
from jax import lax
from jax.experimental import pallas as pl
from jax.experimental.pallas import tpu as pltpu
from jax.sharding import Mesh
from jax.sharding import PartitionSpec as P

ROWS = ("yh", "x", "c")
COLS = ("yl", "z")


def turned(cells):
    return jnp.transpose(cells, (0, 2, 1, 3))


def chosen(table, index):
    return table.at[index].get(mode="promise_in_bounds")


def looked_up(table, index):
    spots = jnp.arange(table.shape[0])
    return jnp.sum(jnp.where(index[:, None] == spots[None, :], table[None, :], 0), axis=1)


def per_face(condition, yes, no):
    return jnp.where(condition[:, None, None, None], yes, no)


def halos(cells, seam_face, seam_code, corner_mask):
    count, width, height, _ = cells.shape
    n_row = lax.axis_size(ROWS)
    n_col = lax.axis_size(COLS)
    r = lax.axis_index(ROWS)
    k = lax.axis_index(COLS)
    row_last = n_row - 1
    col_last = n_col - 1
    everywhere = ROWS + COLS
    top, bottom = r == 0, r == row_last
    west_end, east_end = k == 0, k == col_last
    down = bottom.astype(jnp.int32)
    right = east_end.astype(jnp.int32)
    in_corner = (top | bottom) & (west_end | east_end)
    corners = [(i, j) for i in (0, row_last) for j in (0, col_last)]
    edge_rows = [(i, j) for i in (0, row_last) for j in range(1, col_last)]
    edge_cols = [(i, j) for i in range(1, row_last) for j in (0, col_last)]

    def swap(x, where, image):
        pairs = []
        for i, j in where:
            other = (row_last - i if image & 2 else i) * n_col + (col_last - j if image & 1 else j)
            pairs.append((i * n_col + j, other))
        return lax.ppermute(x, everywhere, pairs)

    north, south = cells[:, :, :2], cells[:, :, height - 2 :]
    from_above = lax.ppermute(south, ROWS, [(i, i + 1) for i in range(row_last)])
    from_below = lax.ppermute(north, ROWS, [(i + 1, i) for i in range(row_last)])

    own_row = jnp.where(top, north, jnp.flip(south, 2))

    def side_columns(above, below, columns):
        return jnp.concatenate([above[:, columns], cells[:, columns], below[:, columns]], axis=2)

    west, east = slice(0, 2), slice(width - 2, width)
    own_col = jnp.where(
        west_end,
        side_columns(from_above, from_below, west),
        jnp.flip(side_columns(from_above, from_below, east), 1),
    )
    tall = height + 4
    row_image = swap(own_row, edge_rows, 1)
    col_image = swap(own_col, edge_cols, 3)
    both_image = swap(jnp.concatenate([own_col, turned(own_row)], axis=2), corners, 3)
    row_image = jnp.where(in_corner, turned(both_image[:, :, tall:]), row_image)
    col_image = jnp.where(in_corner, both_image[:, :, :tall], col_image)

    def row_seam(is_top):
        code = jnp.where(is_top, seam_code[:, 0], seam_code[:, 1])
        face = jnp.where(is_top, seam_face[:, 0], seam_face[:, 1])
        side = jnp.where(is_top, 0, 1)
        return 2 * ((code >> 1) ^ side) + (code & 1), face

    row_first = jnp.where(in_corner, 3, 1)
    row_next = jnp.where(in_corner, 1, 2)
    row_from, row_face = row_seam(top)
    give_from, give_face = row_seam(jnp.where(in_corner, top, ~top))

    def column_seam(is_west):
        code = jnp.where(is_west, seam_code[:, 2], seam_code[:, 3])
        face = jnp.where(is_west, seam_face[:, 2], seam_face[:, 3])
        at = jnp.where(is_west, 0, 1)
        side = down ^ (code & 1)
        inner = jnp.where(side == 0, looked_up(seam_code[:, 0], face), looked_up(seam_code[:, 1], face))
        inner_face = jnp.where(side == 0, looked_up(seam_face[:, 0], face), looked_up(seam_face[:, 1], face))
        inner_east = (code >> 1) ^ (inner & 1)
        inner_from = 2 * ((inner >> 1) ^ down) + (inner_east ^ at)
        return 2 * (code & 1) + ((code >> 1) ^ at), face, inner_from, inner_face, inner_east

    col_from, col_face, block_from, block_face, block_east = column_seam(west_end)
    give_col, give_col_face, give_block, give_block_face, give_east = column_seam(~west_end)

    def spot(comes_from, first, face):
        return jnp.where(comes_from == first, count, 0) + face

    row_all = chosen(
        jnp.concatenate([own_row, row_image]),
        jnp.concatenate(
            [
                spot(row_from, row_first, row_face),
                spot(give_from ^ row_next, row_first, give_face),
                spot(block_from, 3, block_face),
                spot(give_block ^ 1, 3, give_block_face),
            ]
        ),
    )
    col_all = chosen(
        jnp.concatenate([own_col, col_image]),
        jnp.concatenate([spot(col_from, 3, col_face), spot(give_col ^ 1, 3, give_col_face)]),
    )

    def block(rows, is_east):
        return per_face(is_east == 0, rows[:, west], jnp.flip(rows[:, east], 1))

    row_here, row_gift = row_all[:count], row_all[count : 2 * count]
    block_here = block(row_all[2 * count : 3 * count], block_east)
    col_here = col_all[:count]
    col_gift, block_gift = col_all[count:], block(row_all[3 * count :], give_east)
    row_given = swap(row_gift, edge_rows, 2)
    col_given = swap(col_gift, edge_cols, 1)
    both_given = swap(jnp.concatenate([col_gift, turned(row_gift), block_gift], axis=2), corners, 1)
    row_given = jnp.where(in_corner, turned(both_given[:, :, tall : tall + width]), row_given)
    col_given = jnp.where(in_corner, both_given[:, :, :tall], col_given)
    block_given = both_given[:, :, tall + width :]

    def at_hand(comes_from, first):
        return (comes_from == 0) | (comes_from == first)

    row_pick = per_face(at_hand(row_from, row_first), row_here, row_given)
    row_pick = per_face(row_from & 1 == 1, jnp.flip(row_pick, 1), row_pick)
    above = jnp.where(top, jnp.flip(row_pick, 2), from_above)
    below = jnp.where(bottom, row_pick, from_below)
    from_left = lax.ppermute(side_columns(above, below, east), COLS, [(j, j + 1) for j in range(col_last)])
    from_right = lax.ppermute(side_columns(above, below, west), COLS, [(j + 1, j) for j in range(col_last)])

    col_pick = per_face(at_hand(col_from, 3), col_here, col_given)
    col_pick = per_face(col_from & 2 == 2, jnp.flip(col_pick, 2), col_pick)
    corner = per_face(at_hand(block_from, 3), block_here, block_given)
    mask = jnp.where(
        top,
        jnp.where(west_end, corner_mask[:, 0], corner_mask[:, 1]),
        jnp.where(west_end, corner_mask[:, 2], corner_mask[:, 3]),
    )
    corner = per_face(mask == 0, 0, corner)
    edge = jnp.concatenate(
        [
            jnp.where(top, jnp.flip(corner, 2), col_pick[:, :, :2]),
            col_pick[:, :, 2 : height + 2],
            jnp.where(bottom, corner, col_pick[:, :, height + 2 :]),
        ],
        axis=2,
    )
    left_cols = jnp.where(west_end, jnp.flip(edge, 1), from_left)
    right_cols = jnp.where(east_end, edge, from_right)
    return left_cols, right_cols, above, below


def compute_kernel(
    core_ref,
    st_ref,
    lf_ref,
    rt_ref,
    up_ref,
    lo_ref,
    wg_ref,
    wd_ref,
    hg_ref,
    hidden_ref,
    mine_ref,
    theirs_ref,
    x_ref,
    dg_ref,
    dv_ref,
    sums_ref,
    sems,
):
    _, faces, wide, height, c_in = x_ref.shape
    width = wide - 4
    c_out = hg_ref.shape[-1]
    dg_ref[...] = jnp.zeros(dg_ref.shape, dg_ref.dtype)
    dv_ref[...] = jnp.zeros(dv_ref.shape, dv_ref.dtype)
    step = 1
    cells = step * width * height

    def forward(n, _):
        f = n * step
        here = pl.ds(f, step)

        inside = pl.ds(2, width)
        mid = st_ref[here]
        x_ref[2, here, inside] = mid
        mid = mid.astype(jnp.float32)
        above = up_ref[here].astype(jnp.float32)
        below = lo_ref[here].astype(jnp.float32)
        left = lf_ref[here].astype(jnp.float32)
        right = rt_ref[here].astype(jnp.float32)
        for shift in range(5):
            rows = slice(shift, shift + height)
            x_ref[shift, here, pl.ds(0, 2)] = left[:, :, rows].astype(jnp.bfloat16)
            x_ref[shift, here, pl.ds(width + 2, 2)] = right[:, :, rows].astype(jnp.bfloat16)
        for shift, parts in (
            (0, [above, mid[:, :, : height - 2]]),
            (1, [above[:, :, 1:], mid[:, :, : height - 1]]),
            (3, [mid[:, :, 1:], below[:, :, :1]]),
            (4, [mid[:, :, 2:], below]),
        ):
            x_ref[shift, here, inside] = jnp.concatenate(parts, axis=2).astype(jnp.bfloat16)

        def windows(spacing, first):
            return jnp.concatenate(
                [
                    x_ref[first + a * spacing, here, pl.ds(first + b * spacing, width)].reshape(cells, c_in)
                    for a in range(3)
                    for b in range(3)
                ],
                axis=1,
            )

        gate = jnp.dot(windows(1, 1), wg_ref[...], preferred_element_type=jnp.float32)
        value = jnp.dot(windows(2, 0), wd_ref[...], preferred_element_type=jnp.float32)
        root = (2.0 / jnp.pi) ** 0.5
        square = gate * gate
        t = jnp.tanh(root * gate * (1.0 + 0.044715 * square))
        half = 0.5 * (1.0 + t)
        act = gate * half
        slope = half + 0.5 * gate * (1.0 - t * t) * (root * (1.0 + 3 * 0.044715 * square))
        shape = (step, width, height, c_out)
        up = hg_ref[here].astype(jnp.float32).reshape(cells, c_out)
        hidden_ref[here] = (act * value).astype(jnp.bfloat16).reshape(shape)
        dgate = (up * value * slope).astype(jnp.bfloat16).reshape(shape)
        dvalue = (up * act).astype(jnp.bfloat16).reshape(shape)
        for b in range(3):
            lanes = pl.ds(b * c_out, c_out)
            dg_ref[here, pl.ds(b, width), :, lanes] = dgate
            dv_ref[here, pl.ds(2 * b, width), :, lanes] = dvalue
        return 0

    lax.fori_loop(0, faces // step, forward, 0, unroll=True)

    grads, _, across, along, span, _ = sums_ref.shape

    def put(grad, tap, block):
        start, end = tap * c_in, (tap + 1) * c_in
        at = start
        while at < end:
            n = at // span
            stop = min(end, (n + 1) * span)
            spot = n // 2 % across, n // 2 // across
            sums_ref[grad, n % 2, spot[0], spot[1], pl.ds(at - n * span, stop - at)] = block[at - start : stop - start]
            at = stop

    core = core_ref[0]
    copies = []
    for grad, first, cols, delta in ((0, 1, pl.ds(1, wide - 2), dg_ref), (1, 0, pl.ds(0, wide), dv_ref)):
        d = delta[...].reshape(-1, 3 * c_out)
        for a in range(3):
            x = x_ref[first + a * (grad + 1), :, cols].reshape(-1, c_in)
            sums = lax.dot_general(x, d, (((0,), (0,)), ((), ())), preferred_element_type=jnp.float32)
            for b in range(3):
                put(grad, a * 3 + b, sums[:, b * c_out : (b + 1) * c_out])
        for n, target in ((core, mine_ref), (1 - core, theirs_ref)):
            copy = pltpu.make_async_copy(sums_ref.at[grad, n], target.at[grad], sems.at[len(copies)])
            copy.start()
            copies.append(copy)
    for copy in copies:
        copy.wait()


def compute(core, st, lf, rt, up, lo, wg, wd, hg):
    faces, width, height, c_in = st.shape
    wide = width + 4
    c_out = wg.shape[-1]
    across, along = lax.axis_size("x"), lax.axis_size("yh")
    shares = (2, across, along, 9 * c_in // (2 * across * along), c_out)
    vm = pl.BlockSpec(memory_space=pltpu.VMEM)
    anywhere = pl.BlockSpec(memory_space=pl.ANY)
    return pl.pallas_call(
        compute_kernel,
        in_specs=[pl.BlockSpec(memory_space=pltpu.SMEM)] + [vm] * 8,
        out_specs=[vm, anywhere, anywhere],
        out_shape=[
            jax.ShapeDtypeStruct(hg.shape, jnp.bfloat16),
            jax.ShapeDtypeStruct(shares, jnp.float32),
            jax.ShapeDtypeStruct(shares, jnp.float32),
        ],
        scratch_shapes=[
            pltpu.VMEM((5, faces, wide, height, c_in), jnp.bfloat16),
            pltpu.VMEM((faces, wide - 2, height, 3 * c_out), jnp.bfloat16),
            pltpu.VMEM((faces, wide, height, 3 * c_out), jnp.bfloat16),
            pltpu.VMEM((2,) + shares, jnp.float32),
            pltpu.SemaphoreType.DMA((4,)),
        ],
        compiler_params=pltpu.CompilerParams(vmem_limit_bytes=56 * 2**20),
        name="gated_conv",
    )(core, st, lf, rt, up, lo, wg.reshape(-1, c_out), wd.reshape(-1, c_out), hg)


def on_device(state, gate_kernel, dilated_kernel, hidden_grad, seam_face, seam_code, corner_mask):
    count, height, width, _ = state.shape
    cells = turned(state)
    left, right, above, below = halos(cells, seam_face, seam_code, corner_mask)
    core = lax.axis_index("c").reshape(1)
    hidden, mine, theirs = compute(
        core, cells, left, right, above, below, gate_kernel, dilated_kernel, turned(hidden_grad)
    )
    total_cells = count * height * width * lax.axis_size(ROWS) * lax.axis_size(COLS)
    gate_part, dilated_part = scattered_sum(mine, theirs, total_cells ** (-0.5))
    return (turned(hidden), gate_part, dilated_part)


def scattered_sum(mine, theirs, scale):
    both = mine + lax.ppermute(theirs, "c", [(0, 1), (1, 0)])
    grads, across, along, span, lanes = both.shape
    sends = jnp.transpose(both.astype(jnp.bfloat16), (1, 0, 2, 3, 4))
    arrived = lax.all_to_all(sends.reshape(across, -1, lanes), "x", 0, 0)
    part = jnp.sum(arrived.astype(jnp.float32), axis=0).reshape(grads, along, span, lanes)
    takers = lax.axis_size(COLS)
    share = span * lanes // takers
    tall = -(-(share + lanes // 2) // lanes)
    starts = [i * share // lanes for i in range(takers)]
    sends = jnp.stack([part[:, :, s : s + tall] for s in starts])
    sends = jnp.transpose(sends, (2, 0, 3, 1, 4)).reshape(along * takers, tall, grads, lanes)
    arrived = lax.all_to_all(sends, ("yh",) + COLS, 0, 0)
    total = jnp.transpose(jnp.sum(arrived, axis=0) * scale, (1, 0, 2)).reshape(grads, tall * lanes)
    skip = lax.axis_index(COLS) * share % lanes
    total = lax.dynamic_slice_in_dim(total, skip, share, axis=1)
    return total[0], total[1]


def solution(mesh):
    fine = Mesh(mesh.devices.reshape(2, 4, 2, 4, 8), ROWS + COLS)
    cells = P(None, ROWS, COLS, None)
    return jax.shard_map(
        on_device,
        mesh=fine,
        in_specs=(cells, P(), P(), cells, P(), P(), P()),
        out_specs=(cells, P(ROWS + COLS), P(ROWS + COLS)),
        check_vma=False,
    )
```

time: 131 us -> 123 us (0.939)
  the two profiles are of different devices: /device:TPU:56 before, /device:TPU:1 now
where the time goes in v3:
time: 123 us; the launch traced here: 121 us
  starting transfers between devices  53.5 us (43%)
  waiting for transfers between devices  24.2 us (20%)
  blocking collectives  15.1 us (12%)
  Pallas kernels  11.3 us (9%)
  local copies, waits for them, and re-layouts  9.25 us (8%)
  other arithmetic  6.44 us (5%)
  between operations  1.58 us (1%)
    ppermute x6, starting transfers between devices, swap(): return lax.ppermute(x, everywhere, pairs)  23.8 us
    all_to_all x1, blocking collectives, scattered_sum(): arrived = lax.all_to_all(sends.reshape(across, -1, lanes), 'x', 0, 0)  15.1 us
    all_to_all x1, waiting for transfers between devices, scattered_sum(): arrived = lax.all_to_all(sends, ('yh',) + COLS, 0, 0)  12.2 us
    pallas_call x1, Pallas kernels, compute(): pl.pallas_call(compute_kernel, in_specs=[pl.BlockSpec(memory_space=pltpu....  11.3 us
    all_to_all x1, starting transfers between devices, scattered_sum(): arrived = lax.all_to_all(sends, ('yh',) + COLS, 0, 0)  8.2 us
    ppermute x6, waiting for transfers between devices, swap(): return lax.ppermute(x, everywhere, pairs)  6.9 us
    ppermute x1, starting transfers between devices, scattered_sum(): both = mine + lax.ppermute(theirs, 'c', [(0, 1), (1, 0)])  5.97 us
    ppermute x1, starting transfers between devices, halos(): lax.ppermute(north, ROWS, [(i + 1, i) for i in range(row_last)])  5.57 us
  transfers between devices with their start and end apart: 12, of which 6 were waited for; matrix products, arithmetic and copies ran while one was open for 6% of the time, Pallas kernels for 0%

profile of v3, /device:TPU:1, one launch (start us, length us, event | category | flops | bytes accessed | tf_op | source)
XLA Modules:
  0.0 121.4 jit_solution(15459895453284403690)
XLA Ops:
  0.6 1.3 %copy.104 = bf16[12,16,8,256]{3,1,2,0:T(8,128)(2,1)S(1)} copy(bf16[12,16,8,256]{3,2,1,0:T(8,128)(2,1)} %param.7) | data formatting | bytes 1572864 | tf_op args[0]
  2.1 4.5 %collective-permute-start = (bf16[12,8,2,256]{3,2,1,0:T(2,128)(2,1)S(1)}, bf16[12,8,2,256]{3,2,1,0:T(2,128)(2,1)S(1)}, u32[]{:S(2)}, u32[]{:S(2)}) collective-permute-start(bf16[12,8,2,256]{3,2,1,0:T(2,128)(2,1)S(1)} %slice.325), channel_id=1, source_target_pairs={{0,32},{32,64},{64,96},{96,128},{128,160},{160,192},{192,224},{224... | collective-permute-start | bytes 294920 | tf_op jit(solution)/shard_map/ppermute | solution.py:56
  6.6 0.5 rev.33
  7.3 5.6 %collective-permute-start.1 = (bf16[12,8,2,256]{3,2,1,0:T(2,128)(2,1)S(1)}, bf16[12,8,2,256]{3,2,1,0:T(2,128)(2,1)S(1)}, u32[]{:S(2)}, u32[]{:S(2)}) collective-permute-start(bf16[12,8,2,256]{3,2,1,0:T(2,128)(2,1)S(1)} %get-tuple-element.48), channel_id=1, source_target_pairs={{32,0},{64,32},{96,64},{128,96},{160,128},{192,160},{224,192},{256... | collective-permute-start | bytes 294920 | tf_op jit(solution)/shard_map/ppermute | solution.py:57
  12.9 0.7 collective-permute-start.3
  14.8 0.7 collective-permute-start.2
  15.6 13.5 %collective-permute-start.4 = (bf16[12,2,20,256]{3,2,1,0:T(8,128)(2,1)S(1)}, bf16[12,2,20,256]{3,2,1,0:T(8,128)(2,1)S(1)}, u32[]{:S(2)}, u32[]{:S(2)}) collective-permute-start(bf16[12,2,20,256]{3,2,1,0:T(8,128)(2,1)S(1)} %fusion.4), channel_id=1, source_target_pairs={{32,479},{63,448},{64,447},{95,416},{96,415},{127,384},{128,383},{... | collective-permute-start | bytes 737288 | tf_op jit(solution)/shard_map/ppermute | solution.py:53
  29.5 1.3 %gather_fusion = bf16[48,8,2,256]{3,2,1,0:T(2,128)(2,1)S(1)} fusion(bf16[24,8,2,256]{3,2,1,0:T(2,128)(2,1)S(1)} %pad_maximum_fusion.8, s32[1024]{0:T(1024)S(1)} %pad_clamp_fusion.1), kind=kCustom, calls=%fused_computation | custom fusion | bytes 786624 | tf_op jit(solution)/shard_map/gather | solution.py:18
  31.0 3.3 %collective-permute-done.4 = bf16[12,2,20,256]{3,2,1,0:T(8,128)(2,1)S(1)} collective-permute-done((bf16[12,2,20,256]{3,2,1,0:T(8,128)(2,1)S(1)}, bf16[12,2,20,256]{3,2,1,0:T(8,128)(2,1)S(1)}, u32[]{:S(2)}, u32[]{:S(2)}) %collective-permute-start.4) | collective-permute-done | bytes 245792 | tf_op jit(solution)/shard_map/ppermute | solution.py:53
  34.4 0.6 gather_fusion.1
  35.0 7.6 %collective-permute-start.6 = (bf16[12,2,20,256]{3,2,1,0:T(8,128)(2,1)S(1)}, bf16[12,2,20,256]{3,2,1,0:T(8,128)(2,1)S(1)}, u32[]{:S(2)}, u32[]{:S(2)}) collective-permute-start(bf16[12,2,20,256]{3,2,1,0:T(8,128)(2,1)S(1)} %slice.336), channel_id=1, source_target_pairs={{32,63},{63,32},{64,95},{95,64},{96,127},{127,96},{128,159},{159,1... | collective-permute-start | bytes 737288 | tf_op jit(solution)/shard_map/ppermute | solution.py:53
  42.8 0.7 collective-permute-start.5
  43.5 0.8 copy.105
  44.3 0.7 collective-permute-start.7
  45.0 3.6 %collective-permute-done.6 = bf16[12,2,20,256]{3,2,1,0:T(8,128)(2,1)S(1)} collective-permute-done((bf16[12,2,20,256]{3,2,1,0:T(8,128)(2,1)S(1)}, bf16[12,2,20,256]{3,2,1,0:T(8,128)(2,1)S(1)}, u32[]{:S(2)}, u32[]{:S(2)}) %collective-permute-start.6) | collective-permute-done | bytes 245792 | tf_op jit(solution)/shard_map/ppermute | solution.py:53
  49.7 0.5 rev.41
  50.5 1.3 %collective-permute-start.9 = (bf16[12,2,20,256]{3,2,1,0:T(8,128)(2,1)S(1)}, bf16[12,2,20,256]{3,2,1,0:T(8,128)(2,1)S(1)}, u32[]{:S(2)}, u32[]{:S(2)}) collective-permute-start(bf16[12,2,20,256]{3,2,1,0:T(8,128)(2,1)S(1)} %fusion.5), channel_id=1, source_target_pairs={{1,0},{2,1},{3,2},{4,3},{5,4},{6,5},{7,6},{8,7},{9,8},{10,9},{11,1... | collective-permute-start | bytes 737288 | tf_op jit(solution)/shard_map/ppermute | solution.py:143
  52.6 4.2 %collective-permute-start.8 = (bf16[12,2,20,256]{3,2,1,0:T(8,128)(2,1)S(1)}, bf16[12,2,20,256]{3,2,1,0:T(8,128)(2,1)S(1)}, u32[]{:S(2)}, u32[]{:S(2)}) collective-permute-start(bf16[12,2,20,256]{3,2,1,0:T(8,128)(2,1)S(1)} %fusion.2), channel_id=1, source_target_pairs={{0,1},{1,2},{2,3},{3,4},{4,5},{5,6},{6,7},{7,8},{8,9},{9,10},{10,1... | collective-permute-start | bytes 737288 | tf_op jit(solution)/shard_map/ppermute | solution.py:142
  56.8 1.2 collective-permute-done.9
  58.0 0.9 broadcast_select_fusion.1
  58.9 1.3 %collective-permute-done.8 = bf16[12,2,20,256]{3,2,1,0:T(8,128)(2,1)S(1)} collective-permute-done((bf16[12,2,20,256]{3,2,1,0:T(8,128)(2,1)S(1)}, bf16[12,2,20,256]{3,2,1,0:T(8,128)(2,1)S(1)}, u32[]{:S(2)}, u32[]{:S(2)}) %collective-permute-start.8) | collective-permute-done | bytes 245792 | tf_op jit(solution)/shard_map/ppermute | solution.py:142
  60.2 0.8 reverse_select_fusion.lf_ref
  61.1 11.3 %gated_conv.1 = (bf16[12,8,16,128]{3,2,1,0:T(8,128)(2,1)}, f32[2,4,2,144,128]{4,3,2,1,0:T(8,128)}, f32[2,4,2,144,128]{4,3,2,1,0:T(8,128)}) custom-call(s32[1]{0:T(128)} %bitcast.core_ref, bf16[12,8,16,256]{3,2,1,0:T(8,128)(2,1)} %bitcast.249, bf16[12,2,20,256]{3,2,1,0:T(8,128)(2,1)} %reverse_select_fusion.lf_ref, ...), custom_call_target="tpu_custom_call" | custom-call | tf_op jit(solution)/shard_map/gated_conv/pallas_call | solution.py:286
  72.3 6.0 %collective-permute-start.10 = (f32[2,4,2,144,128]{4,3,2,1,0:T(8,128)}, f32[2,4,2,144,128]{4,3,2,1,0:T(8,128)S(1)}, u32[]{:S(2)}, u32[]{:S(2)}) collective-permute-start(f32[2,4,2,144,128]{4,3,2,1,0:T(8,128)} %get-tuple-element.8), channel_id=1, source_target_pairs={{0,32},{32,0},{1,33},{33,1},{2,34},{34,2},{3,35},{35,3},{4,36},{36... | collective-permute-start | bytes 3538952 | tf_op jit(solution)/shard_map/ppermute | solution.py:321
  78.3 2.7 %collective-permute-done.10 = f32[2,4,2,144,128]{4,3,2,1,0:T(8,128)S(1)} collective-permute-done((f32[2,4,2,144,128]{4,3,2,1,0:T(8,128)}, f32[2,4,2,144,128]{4,3,2,1,0:T(8,128)S(1)}, u32[]{:S(2)}, u32[]{:S(2)}) %collective-permute-start.10) | collective-permute-done | bytes 1179680 | tf_op jit(solution)/shard_map/ppermute | solution.py:321
  81.0 1.4 %fusion = bf16[4,2,2,144,128]{4,3,2,0,1:T(8,128)(2,1)S(1)} fusion(f32[2,4,2,144,128]{4,3,2,1,0:T(8,128)} %get-tuple-element.7, f32[2,4,2,144,128]{4,3,2,1,0:T(8,128)S(1)} %collective-permute-done.10), kind=kLoop, calls=%fused_computation.5 | loop fusion | flops 589824 | bytes 2949120 | tf_op jit(solution)/shard_map/transpose | solution.py:323
  82.5 15.1 %all_to_all.10 = bf16[4,576,128]{2,1,0:T(8,128)(2,1)S(1)} all-to-all(bf16[4,576,128]{2,1,0:T(8,128)(2,1)S(1)} %bitcast.250), channel_id=1, replica_groups=mesh['yh'=2,'x'=4,'c'=2,'yl'=4,'z'=8] {'x'}, dimensions={0} | all-to-all | bytes 1179648 | tf_op jit(solution)/shard_map/all_to_all | solution.py:324
  98.3 1.0 copy.93
  99.3 8.2 %all-to-all-start.1 = ((f32[64,5,2,128]{3,2,1,0:T(2,128)}), f32[64,5,2,128]{3,2,1,0:T(2,128)S(1)}, u32[]{:S(2)}, u32[]{:S(2)}) async-start(f32[64,5,2,128]{3,2,1,0:T(2,128)} %copy.93), calls=%async_computation.1 | async-start | bytes 655360 | tf_op jit(solution)/shard_map/all_to_all | solution.py:332
  107.5 0.8 copy.94
  108.4 12.2 %all-to-all-done.1 = f32[64,5,2,128]{3,2,1,0:T(2,128)S(1)} async-done(((f32[64,5,2,128]{3,2,1,0:T(2,128)}), f32[64,5,2,128]{3,2,1,0:T(2,128)S(1)}, u32[]{:S(2)}, u32[]{:S(2)}) %all-to-all-start.1) | async-done | bytes 327712 | tf_op jit(solution)/shard_map/all_to_all | solution.py:332
  120.7 0.7 dynamic-slice_reduce_fusion
  (108 shorter events, 4.9 us)
Async XLA Ops:
  1.9 12.5 %copy-start = (bf16[12,16,8,256]{3,1,2,0:T(8,128)(2,1)}, bf16[12,16,8,256]{3,1,2,0:T(8,128)(2,1)S(1)}, u32[]{:S(2)}) copy-start(bf16[12,16,8,256]{3,1,2,0:T(8,128)(2,1)S(1)} %copy.104) | copy-start | bytes 2359300
  1.9 11.7 %copy-start.5 = (s32[12,4]{0,1:T(4,128)S(1)}, s32[12,4]{0,1:T(4,128)}, u32[]{:S(2)}) copy-start(s32[12,4]{0,1:T(4,128)} %param.12) | copy-start | bytes 580
  2.0 11.8 %copy-start.6 = (s32[12,4]{0,1:T(4,128)S(1)}, s32[12,4]{0,1:T(4,128)}, u32[]{:S(2)}) copy-start(s32[12,4]{0,1:T(4,128)} %param.11) | copy-start | bytes 580
  2.1 12.2 %collective-permute-start = (bf16[12,8,2,256]{3,2,1,0:T(2,128)(2,1)S(1)}, bf16[12,8,2,256]{3,2,1,0:T(2,128)(2,1)S(1)}, u32[]{:S(2)}, u32[]{:S(2)}) collective-permute-start(bf16[12,8,2,256]{3,2,1,0:T(2,128)(2,1)S(1)} %slice.325), channel_id=1, source_target_pairs={{0,32},{32,64},{64,96},{96,128},{128,160},{160,192},{192,224},{224... | collective-permute-start | bytes 294920 | tf_op jit(solution)/shard_map/ppermute | solution.py:56
  7.3 6.9 %collective-permute-start.1 = (bf16[12,8,2,256]{3,2,1,0:T(2,128)(2,1)S(1)}, bf16[12,8,2,256]{3,2,1,0:T(2,128)(2,1)S(1)}, u32[]{:S(2)}, u32[]{:S(2)}) collective-permute-start(bf16[12,8,2,256]{3,2,1,0:T(2,128)(2,1)S(1)} %get-tuple-element.48), channel_id=1, source_target_pairs={{32,0},{64,32},{96,64},{128,96},{160,128},{192,160},{224,192},{256... | collective-permute-start | bytes 294920 | tf_op jit(solution)/shard_map/ppermute | solution.py:57
  12.9 16.2 %collective-permute-start.3 = (bf16[12,8,2,256]{3,1,2,0:T(8,128)(2,1)S(1)}, bf16[12,8,2,256]{3,1,2,0:T(8,128)(2,1)S(1)}, u32[]{:S(2)}, u32[]{:S(2)}) collective-permute-start(bf16[12,8,2,256]{3,1,2,0:T(8,128)(2,1)S(1)} %copy.107), channel_id=1, source_target_pairs={{1,30},{2,29},{3,28},{4,27},{5,26},{6,25},{7,24},{8,23},{9,22},{10... | collective-permute-start | bytes 294920 | tf_op jit(solution)/shard_map/ppermute | solution.py:53
  14.8 14.3 %collective-permute-start.2 = (bf16[12,2,28,256]{3,2,1,0:T(8,128)(2,1)S(1)}, bf16[12,2,28,256]{3,2,1,0:T(8,128)(2,1)S(1)}, u32[]{:S(2)}, u32[]{:S(2)}) collective-permute-start(bf16[12,2,28,256]{3,2,1,0:T(8,128)(2,1)S(1)} %pad_maximum_fusion.1), channel_id=1, source_target_pairs={{0,511},{31,480},{480,31},{511,0}} | collective-permute-start | bytes 1032200 | tf_op jit(solution)/shard_map/ppermute | solution.py:53
  15.6 18.7 %collective-permute-start.4 = (bf16[12,2,20,256]{3,2,1,0:T(8,128)(2,1)S(1)}, bf16[12,2,20,256]{3,2,1,0:T(8,128)(2,1)S(1)}, u32[]{:S(2)}, u32[]{:S(2)}) collective-permute-start(bf16[12,2,20,256]{3,2,1,0:T(8,128)(2,1)S(1)} %fusion.4), channel_id=1, source_target_pairs={{32,479},{63,448},{64,447},{95,416},{96,415},{127,384},{128,383},{... | collective-permute-start | bytes 737288 | tf_op jit(solution)/shard_map/ppermute | solution.py:53
  34.3 9.2 %copy-start.3 = (bf16[12,16,8,128]{3,2,1,0:T(8,128)(2,1)S(1)}, bf16[12,16,8,128]{3,2,1,0:T(8,128)(2,1)}, u32[]{:S(2)}) copy-start(bf16[12,16,8,128]{3,2,1,0:T(8,128)(2,1)} %param.10) | copy-start | bytes 1179652
  34.9 9.4 %copy-start.7 = (s32[12,4]{0,1:T(4,128)S(1)}, s32[12,4]{0,1:T(4,128)}, u32[]{:S(2)}) copy-start(s32[12,4]{0,1:T(4,128)} %param.13) | copy-start | bytes 580
  35.0 13.6 %collective-permute-start.6 = (bf16[12,2,20,256]{3,2,1,0:T(8,128)(2,1)S(1)}, bf16[12,2,20,256]{3,2,1,0:T(8,128)(2,1)S(1)}, u32[]{:S(2)}, u32[]{:S(2)}) collective-permute-start(bf16[12,2,20,256]{3,2,1,0:T(8,128)(2,1)S(1)} %slice.336), channel_id=1, source_target_pairs={{32,63},{63,32},{64,95},{95,64},{96,127},{127,96},{128,159},{159,1... | collective-permute-start | bytes 737288 | tf_op jit(solution)/shard_map/ppermute | solution.py:53
  42.8 5.9 %collective-permute-start.5 = (bf16[12,2,30,256]{3,2,1,0:T(8,128)(2,1)S(1)}, bf16[12,2,30,256]{3,2,1,0:T(8,128)(2,1)S(1)}, u32[]{:S(2)}, u32[]{:S(2)}) collective-permute-start(bf16[12,2,30,256]{3,2,1,0:T(8,128)(2,1)S(1)} %pad_maximum_fusion.2), channel_id=1, source_target_pairs={{0,31},{31,0},{480,511},{511,480}} | collective-permute-start | bytes 1105928 | tf_op jit(solution)/shard_map/ppermute | solution.py:53
  44.3 4.8 %collective-permute-start.7 = (bf16[12,8,2,256]{3,2,1,0:T(2,128)(2,1)S(1)}, bf16[12,8,2,256]{3,2,1,0:T(2,128)(2,1)S(1)}, u32[]{:S(2)}, u32[]{:S(2)}) collective-permute-start(bf16[12,8,2,256]{3,2,1,0:T(2,128)(2,1)S(1)} %slice.337), channel_id=1, source_target_pairs={{1,481},{2,482},{3,483},{4,484},{5,485},{6,486},{7,487},{8,488},{9... | collective-permute-start | bytes 294920 | tf_op jit(solution)/shard_map/ppermute | solution.py:53
  49.7 2.7 %copy-start.1 = (bf16[12,8,2,256]{3,2,1,0:T(2,128)(2,1)}, bf16[12,8,2,256]{3,2,1,0:T(2,128)(2,1)S(1)}, u32[]{:S(2)}) copy-start(bf16[12,8,2,256]{3,2,1,0:T(2,128)(2,1)S(1)} %get-tuple-element.39.lo_ref) | copy-start | bytes 294916
  50.2 2.1 %copy-start.2 = (bf16[12,2,8,256]{3,2,1,0:T(8,128)(2,1)}, bf16[12,2,8,256]{3,2,1,0:T(8,128)(2,1)S(1)}, u32[]{:S(2)}) copy-start(bf16[12,2,8,256]{3,2,1,0:T(8,128)(2,1)S(1)} %broadcast_select_fusion.6) | copy-start | bytes 294916
  50.5 7.5 %collective-permute-start.9 = (bf16[12,2,20,256]{3,2,1,0:T(8,128)(2,1)S(1)}, bf16[12,2,20,256]{3,2,1,0:T(8,128)(2,1)S(1)}, u32[]{:S(2)}, u32[]{:S(2)}) collective-permute-start(bf16[12,2,20,256]{3,2,1,0:T(8,128)(2,1)S(1)} %fusion.5), channel_id=1, source_target_pairs={{1,0},{2,1},{3,2},{4,3},{5,4},{6,5},{7,6},{8,7},{9,8},{10,9},{11,1... | collective-permute-start | bytes 737288 | tf_op jit(solution)/shard_map/ppermute | solution.py:143
  52.6 7.6 %collective-permute-start.8 = (bf16[12,2,20,256]{3,2,1,0:T(8,128)(2,1)S(1)}, bf16[12,2,20,256]{3,2,1,0:T(8,128)(2,1)S(1)}, u32[]{:S(2)}, u32[]{:S(2)}) collective-permute-start(bf16[12,2,20,256]{3,2,1,0:T(8,128)(2,1)S(1)} %fusion.2), channel_id=1, source_target_pairs={{0,1},{1,2},{2,3},{3,4},{4,5},{5,6},{6,7},{7,8},{8,9},{9,10},{10,1... | collective-permute-start | bytes 737288 | tf_op jit(solution)/shard_map/ppermute | solution.py:142
  72.3 8.6 %collective-permute-start.10 = (f32[2,4,2,144,128]{4,3,2,1,0:T(8,128)}, f32[2,4,2,144,128]{4,3,2,1,0:T(8,128)S(1)}, u32[]{:S(2)}, u32[]{:S(2)}) collective-permute-start(f32[2,4,2,144,128]{4,3,2,1,0:T(8,128)} %get-tuple-element.8), channel_id=1, source_target_pairs={{0,32},{32,0},{1,33},{33,1},{2,34},{34,2},{3,35},{35,3},{4,36},{36... | collective-permute-start | bytes 3538952 | tf_op jit(solution)/shard_map/ppermute | solution.py:321
  98.0 9.5 %copy-start.4 = (bf16[12,8,16,128]{3,2,1,0:T(8,128)(2,1)S(1)}, bf16[12,8,16,128]{3,2,1,0:T(8,128)(2,1)}, u32[]{:S(2)}) copy-start(bf16[12,8,16,128]{3,2,1,0:T(8,128)(2,1)} %get-tuple-element.6) | copy-start | bytes 1179652
  99.3 21.3 %all-to-all-start.1 = ((f32[64,5,2,128]{3,2,1,0:T(2,128)}), f32[64,5,2,128]{3,2,1,0:T(2,128)S(1)}, u32[]{:S(2)}, u32[]{:S(2)}) async-start(f32[64,5,2,128]{3,2,1,0:T(2,128)} %copy.93), calls=%async_computation.1 | async-start | bytes 655360 | tf_op jit(solution)/shard_map/all_to_all | solution.py:332

commit v4 on v3

--- a/solution.py
+++ b/solution.py
@@ -45,10 +45,14 @@
     edge_rows = [(i, j) for i in (0, row_last) for j in range(1, col_last)]
     edge_cols = [(i, j) for i in range(1, row_last) for j in (0, col_last)]
 
-    def swap(x, where, image):
+    def late(i):
+        return i % 2 ^ i // (n_row // 2)
+
+    def swap(x, where, image, late_image=None):
         pairs = []
         for i, j in where:
-            other = (row_last - i if image & 2 else i) * n_col + (col_last - j if image & 1 else j)
+            to = late_image if late_image and late(i) else image
+            other = (row_last - i if to & 2 else i) * n_col + (col_last - j if to & 1 else j)
             pairs.append((i * n_col + j, other))
         return lax.ppermute(x, everywhere, pairs)
 
@@ -56,12 +60,21 @@
     from_above = lax.ppermute(south, ROWS, [(i, i + 1) for i in range(row_last)])
     from_below = lax.ppermute(north, ROWS, [(i + 1, i) for i in range(row_last)])
 
-    own_row = jnp.where(top, north, jnp.flip(south, 2))
-
     def side_columns(above, below, columns):
         return jnp.concatenate([above[:, columns], cells[:, columns], below[:, columns]], axis=2)
 
     west, east = slice(0, 2), slice(width - 2, width)
+
+    def sideways(above, below, rows):
+        steps = [(i * n_col + j, i * n_col + j + 1) for i in rows for j in range(col_last)]
+        from_left = lax.ppermute(side_columns(above, below, east), everywhere, steps)
+        from_right = lax.ppermute(side_columns(above, below, west), everywhere, [(b, a) for a, b in steps])
+        return from_left, from_right
+
+    left_inner, right_inner = sideways(from_above, from_below, range(1, row_last))
+
+    own_row = jnp.where(top, north, jnp.flip(south, 2))
+
     own_col = jnp.where(
         west_end,
         side_columns(from_above, from_below, west),
@@ -69,7 +82,7 @@
     )
     tall = height + 4
     row_image = swap(own_row, edge_rows, 1)
-    col_image = swap(own_col, edge_cols, 3)
+    col_image = swap(own_col, edge_cols, 3, 1)
     both_image = swap(jnp.concatenate([own_col, turned(own_row)], axis=2), corners, 3)
     row_image = jnp.where(in_corner, turned(both_image[:, :, tall:]), row_image)
     col_image = jnp.where(in_corner, both_image[:, :, :tall], col_image)
@@ -80,6 +93,9 @@
         side = jnp.where(is_top, 0, 1)
         return 2 * ((code >> 1) ^ side) + (code & 1), face
 
+    col_late = ~in_corner & (late(r) == 1)
+    col_first = jnp.where(col_late, 1, 3)
+    col_next = jnp.where(col_late, 3, 1)
     row_first = jnp.where(in_corner, 3, 1)
     row_next = jnp.where(in_corner, 1, 2)
     row_from, row_face = row_seam(top)
@@ -115,7 +131,7 @@
     )
     col_all = chosen(
         jnp.concatenate([own_col, col_image]),
-        jnp.concatenate([spot(col_from, 3, col_face), spot(give_col ^ 1, 3, give_col_face)]),
+        jnp.concatenate([spot(col_from, col_first, col_face), spot(give_col ^ col_next, col_first, give_col_face)]),
     )
 
     def block(rows, is_east):
@@ -126,7 +142,7 @@
     col_here = col_all[:count]
     col_gift, block_gift = col_all[count:], block(row_all[3 * count :], give_east)
     row_given = swap(row_gift, edge_rows, 2)
-    col_given = swap(col_gift, edge_cols, 1)
+    col_given = swap(col_gift, edge_cols, 1, 3)
     both_given = swap(jnp.concatenate([col_gift, turned(row_gift), block_gift], axis=2), corners, 1)
     row_given = jnp.where(in_corner, turned(both_given[:, :, tall : tall + width]), row_given)
     col_given = jnp.where(in_corner, both_given[:, :, :tall], col_given)
@@ -139,10 +155,11 @@
     row_pick = per_face(row_from & 1 == 1, jnp.flip(row_pick, 1), row_pick)
     above = jnp.where(top, jnp.flip(row_pick, 2), from_above)
     below = jnp.where(bottom, row_pick, from_below)
-    from_left = lax.ppermute(side_columns(above, below, east), COLS, [(j, j + 1) for j in range(col_last)])
-    from_right = lax.ppermute(side_columns(above, below, west), COLS, [(j + 1, j) for j in range(col_last)])
-
-    col_pick = per_face(at_hand(col_from, 3), col_here, col_given)
+    left_edge, right_edge = sideways(above, below, (0, row_last))
+    from_left = jnp.where(top | bottom, left_edge, left_inner)
+    from_right = jnp.where(top | bottom, right_edge, right_inner)
+
+    col_pick = per_face(at_hand(col_from, col_first), col_here, col_given)
     col_pick = per_face(col_from & 2 == 2, jnp.flip(col_pick, 2), col_pick)
     corner = per_face(at_hand(block_from, 3), block_here, block_given)
     mask = jnp.where(
@@ -327,10 +344,11 @@
     share = span * lanes // takers
     tall = -(-(share + lanes // 2) // lanes)
     starts = [i * share // lanes for i in range(takers)]
+    part = part.astype(jnp.bfloat16)
     sends = jnp.stack([part[:, :, s : s + tall] for s in starts])
     sends = jnp.transpose(sends, (2, 0, 3, 1, 4)).reshape(along * takers, tall, grads, lanes)
     arrived = lax.all_to_all(sends, ("yh",) + COLS, 0, 0)
-    total = jnp.transpose(jnp.sum(arrived, axis=0) * scale, (1, 0, 2)).reshape(grads, tall * lanes)
+    total = jnp.transpose(jnp.sum(arrived.astype(jnp.float32), axis=0) * scale, (1, 0, 2)).reshape(grads, tall * lanes)
     skip = lax.axis_index(COLS) * share % lanes
     total = lax.dynamic_slice_in_dim(total, skip, share, axis=1)
     return total[0], total[1]

time: 123 us -> 118 us (0.959)
  waiting for transfers between devices: 24.2 us -> 19 us
  other arithmetic: 6.44 us -> 9.84 us
  blocking collectives: 15.1 us -> 12.8 us
    ppermute x2 -> x4, waiting for transfers between devices: 2.48 us -> 0.05 us  [the longest x2 0.05 us: sideways(): lax.ppermute(side_columns(above, below, west), everywhere, [(b, a) for a,...]
    all_to_all x1, blocking collectives: 15.1 us -> 12.8 us  [scattered_sum(): arrived = lax.all_to_all(sends.reshape(across, -1, lanes), 'x', 0, 0)]
    ppermute x6, waiting for transfers between devices: 6.9 us -> 5.41 us  [swap(): return lax.ppermute(x, everywhere, pairs)]
    all_to_all x1, waiting for transfers between devices: 12.2 us -> 10.8 us  [scattered_sum(): arrived = lax.all_to_all(sends, ('yh',) + COLS, 0, 0)]
    ppermute x2 -> x4, starting transfers between devices: 5.48 us -> 4.97 us  [the longest x2 2.8 us: sideways(): lax.ppermute(side_columns(above, below, west), everywhere, [(b, a) for a,...]
    unnamed x50 -> x62, local copies, waits for them, and re-layouts: 3.17 us -> 3.42 us
  transfers between devices with their start and end apart: 12 -> 14, of which waited for: 6 -> 4; matrix products, arithmetic and copies ran while one was open for 6% -> 11% of each run, Pallas kernels for 0% -> 0%
where the time goes in v4:
time: 118 us; the launch traced here: 117 us
  starting transfers between devices  52.9 us (45%)
  waiting for transfers between devices  19 us (16%)
  blocking collectives  12.8 us (11%)
  Pallas kernels  11.3 us (10%)
  local copies, waits for them, and re-layouts  9.85 us (8%)
  other arithmetic  9.84 us (8%)
  between operations  1.49 us (1%)
    ppermute x6, starting transfers between devices, swap(): return lax.ppermute(x, everywhere, pairs)  23.5 us
    all_to_all x1, blocking collectives, scattered_sum(): arrived = lax.all_to_all(sends.reshape(across, -1, lanes), 'x', 0, 0)  12.8 us
    pallas_call x1, Pallas kernels, compute(): pl.pallas_call(compute_kernel, in_specs=[pl.BlockSpec(memory_space=pltpu....  11.3 us
    all_to_all x1, waiting for transfers between devices, scattered_sum(): arrived = lax.all_to_all(sends, ('yh',) + COLS, 0, 0)  10.8 us
    all_to_all x1, starting transfers between devices, scattered_sum(): arrived = lax.all_to_all(sends, ('yh',) + COLS, 0, 0)  8.1 us
    ppermute x1, starting transfers between devices, scattered_sum(): both = mine + lax.ppermute(theirs, 'c', [(0, 1), (1, 0)])  6.28 us
    ppermute x1, starting transfers between devices, halos(): lax.ppermute(north, ROWS, [(i + 1, i) for i in range(row_last)])  5.57 us
    ppermute x6, waiting for transfers between devices, swap(): return lax.ppermute(x, everywhere, pairs)  5.41 us
  transfers between devices with their start and end apart: 14, of which 4 were waited for; matrix products, arithmetic and copies ran while one was open for 11% of the time, Pallas kernels for 0%

profile of v4, /device:TPU:1, one launch (start us, length us, event | category | flops | bytes accessed | tf_op | source)
XLA Modules:
  0.0 117.1 jit_solution(4955406484230831178)
XLA Ops:
  0.6 1.3 %copy.112 = bf16[12,16,8,256]{3,1,2,0:T(8,128)(2,1)S(1)} copy(bf16[12,16,8,256]{3,2,1,0:T(8,128)(2,1)} %param.7) | data formatting | bytes 1572864 | tf_op args[0]
  2.1 4.5 %collective-permute-start = (bf16[12,8,2,256]{3,2,1,0:T(2,128)(2,1)S(1)}, bf16[12,8,2,256]{3,2,1,0:T(2,128)(2,1)S(1)}, u32[]{:S(2)}, u32[]{:S(2)}) collective-permute-start(bf16[12,8,2,256]{3,2,1,0:T(2,128)(2,1)S(1)} %slice.331), channel_id=1, source_target_pairs={{0,32},{32,64},{64,96},{96,128},{128,160},{160,192},{192,224},{224... | collective-permute-start | bytes 294920 | tf_op jit(solution)/shard_map/ppermute | solution.py:60
  7.3 5.6 %collective-permute-start.1 = (bf16[12,8,2,256]{3,2,1,0:T(2,128)(2,1)S(1)}, bf16[12,8,2,256]{3,2,1,0:T(2,128)(2,1)S(1)}, u32[]{:S(2)}, u32[]{:S(2)}) collective-permute-start(bf16[12,8,2,256]{3,2,1,0:T(2,128)(2,1)S(1)} %get-tuple-element.48), channel_id=1, source_target_pairs={{32,0},{64,32},{96,64},{128,96},{160,128},{192,160},{224,192},{256... | collective-permute-start | bytes 294920 | tf_op jit(solution)/shard_map/ppermute | solution.py:61
  12.9 0.7 collective-permute-start.3
  15.6 0.9 fusion.3
  16.6 0.7 collective-permute-start.2
  17.3 0.6 compare_or_fusion.2
  18.0 11.7 %collective-permute-start.4 = (bf16[12,2,20,256]{3,2,1,0:T(8,128)(2,1)S(1)}, bf16[12,2,20,256]{3,2,1,0:T(8,128)(2,1)S(1)}, u32[]{:S(2)}, u32[]{:S(2)}) collective-permute-start(bf16[12,2,20,256]{3,2,1,0:T(8,128)(2,1)S(1)} %get-tuple-element.54), channel_id=1, source_target_pairs={{32,63},{63,32},{64,447},{95,416},{96,127},{127,96},{128,383},{159... | collective-permute-start | bytes 737288 | tf_op jit(solution)/shard_map/ppermute | solution.py:57
  30.1 1.3 %gather_fusion = bf16[48,8,2,256]{3,2,1,0:T(2,128)(2,1)S(1)} fusion(bf16[24,8,2,256]{3,2,1,0:T(2,128)(2,1)S(1)} %pad_maximum_fusion.8, s32[1024]{0:T(1024)S(1)} %pad_clamp_fusion.1), kind=kCustom, calls=%fused_computation | custom fusion | bytes 786624 | tf_op jit(solution)/shard_map/gather | solution.py:18
  31.5 0.6 fusion.21
  32.1 4.6 %collective-permute-done.4 = bf16[12,2,20,256]{3,2,1,0:T(8,128)(2,1)S(1)} collective-permute-done((bf16[12,2,20,256]{3,2,1,0:T(8,128)(2,1)S(1)}, bf16[12,2,20,256]{3,2,1,0:T(8,128)(2,1)S(1)}, u32[]{:S(2)}, u32[]{:S(2)}) %collective-permute-start.4) | collective-permute-done | bytes 245792 | tf_op jit(solution)/shard_map/ppermute | solution.py:57
  37.5 9.1 %collective-permute-start.6 = (bf16[12,2,20,256]{3,2,1,0:T(8,128)(2,1)S(1)}, bf16[12,2,20,256]{3,2,1,0:T(8,128)(2,1)S(1)}, u32[]{:S(2)}, u32[]{:S(2)}) collective-permute-start(bf16[12,2,20,256]{3,2,1,0:T(8,128)(2,1)S(1)} %slice.342), channel_id=1, source_target_pairs={{32,479},{63,448},{64,95},{95,64},{96,415},{127,384},{128,159},{15... | collective-permute-start | bytes 737288 | tf_op jit(solution)/shard_map/ppermute | solution.py:57
  46.9 0.7 collective-permute-start.5
  47.6 0.8 copy.113
  48.4 1.3 %collective-permute-start.9 = (bf16[12,2,20,256]{3,2,1,0:T(8,128)(2,1)S(1)}, bf16[12,2,20,256]{3,2,1,0:T(8,128)(2,1)S(1)}, u32[]{:S(2)}, u32[]{:S(2)}) collective-permute-start(bf16[12,2,20,256]{3,2,1,0:T(8,128)(2,1)S(1)} %fusion.1), channel_id=1, source_target_pairs={{32,33},{33,34},{34,35},{35,36},{36,37},{37,38},{38,39},{39,40},{4... | collective-permute-start | bytes 737288 | tf_op jit(solution)/shard_map/ppermute | solution.py:70
  49.7 1.4 %collective-permute-start.11 = (bf16[12,2,20,256]{3,2,1,0:T(8,128)(2,1)}, bf16[12,2,20,256]{3,2,1,0:T(8,128)(2,1)}, u32[]{:S(2)}, u32[]{:S(2)}) collective-permute-start(bf16[12,2,20,256]{3,2,1,0:T(8,128)(2,1)} %get-tuple-element.53), channel_id=1, source_target_pairs={{33,32},{34,33},{35,34},{36,35},{37,36},{38,37},{39,38},{40,39},{4... | collective-permute-start | bytes 737288 | tf_op jit(solution)/shard_map/ppermute | solution.py:71
  51.2 0.7 collective-permute-start.7
  51.9 0.8 collective-permute-done.6
  54.5 1.4 %collective-permute-start.10 = (bf16[12,2,20,256]{3,2,1,0:T(8,128)(2,1)S(1)}, bf16[12,2,20,256]{3,2,1,0:T(8,128)(2,1)}, u32[]{:S(2)}, u32[]{:S(2)}) collective-permute-start(bf16[12,2,20,256]{3,2,1,0:T(8,128)(2,1)S(1)} %fusion.4), channel_id=1, source_target_pairs={{1,0},{2,1},{3,2},{4,3},{5,4},{6,5},{7,6},{8,7},{9,8},{10,9},{11,1... | collective-permute-start | bytes 737288 | tf_op jit(solution)/shard_map/ppermute | solution.py:71
  56.7 0.9 collective-permute-start.8
  57.7 1.9 %select_select_fusion = (bf16[12,2,20,256]{3,2,1,0:T(8,128)(2,1)}, bf16[12,2,20,256]{3,2,1,0:T(8,128)(2,1)S(1)}) fusion(bf16[12,2,20,256]{3,2,1,0:T(8,128)(2,1)} %collective-permute-done.10, bf16[12,2,20,256]{3,2,1,0:T(8,128)(2,1)} %collective-permute-done.11, pred[]{:T(512)S(6)} %eq.249, pred[]{:T(512)S(6)} %or.30, ...), kind=kLoop, calls=%fused_computation.22 | loop fusion | flops 983040 | bytes 1228802 | tf_op jit(solution)/shard_map/jit(_where)/select_n | solution.py:180
  59.6 0.8 select_select_fusion.1.lf_ref
  60.4 11.3 %gated_conv.1 = (bf16[12,8,16,128]{3,2,1,0:T(8,128)(2,1)}, f32[2,4,2,144,128]{4,3,2,1,0:T(8,128)}, f32[2,4,2,144,128]{4,3,2,1,0:T(8,128)}) custom-call(s32[1]{0:T(128)} %bitcast.core_ref, bf16[12,8,16,256]{3,2,1,0:T(8,128)(2,1)} %bitcast.249, bf16[12,2,20,256]{3,2,1,0:T(8,128)(2,1)} %select_select_fusion.1.lf_ref, ...), custom_call_target="tpu_custom_call" | custom-call | tf_op jit(solution)/shard_map/gated_conv/pallas_call | solution.py:303
  71.7 6.3 %collective-permute-start.12 = (f32[2,4,2,144,128]{4,3,2,1,0:T(8,128)}, f32[2,4,2,144,128]{4,3,2,1,0:T(8,128)S(1)}, u32[]{:S(2)}, u32[]{:S(2)}) collective-permute-start(f32[2,4,2,144,128]{4,3,2,1,0:T(8,128)} %get-tuple-element.8), channel_id=1, source_target_pairs={{0,32},{32,0},{1,33},{33,1},{2,34},{34,2},{3,35},{35,3},{4,36},{36... | collective-permute-start | bytes 3538952 | tf_op jit(solution)/shard_map/ppermute | solution.py:338
  78.0 2.7 %collective-permute-done.12 = f32[2,4,2,144,128]{4,3,2,1,0:T(8,128)S(1)} collective-permute-done((f32[2,4,2,144,128]{4,3,2,1,0:T(8,128)}, f32[2,4,2,144,128]{4,3,2,1,0:T(8,128)S(1)}, u32[]{:S(2)}, u32[]{:S(2)}) %collective-permute-start.12) | collective-permute-done | bytes 1179680 | tf_op jit(solution)/shard_map/ppermute | solution.py:338
  80.6 1.4 %fusion = bf16[4,2,2,144,128]{4,3,2,0,1:T(8,128)(2,1)S(1)} fusion(f32[2,4,2,144,128]{4,3,2,1,0:T(8,128)} %get-tuple-element.7, f32[2,4,2,144,128]{4,3,2,1,0:T(8,128)S(1)} %collective-permute-done.12), kind=kLoop, calls=%fused_computation.4 | loop fusion | flops 589824 | bytes 2949120 | tf_op jit(solution)/shard_map/transpose | solution.py:340
  82.1 12.8 %all_to_all.10 = bf16[4,576,128]{2,1,0:T(8,128)(2,1)S(1)} all-to-all(bf16[4,576,128]{2,1,0:T(8,128)(2,1)S(1)} %bitcast.250), channel_id=1, replica_groups=mesh['yh'=2,'x'=4,'c'=2,'yl'=4,'z'=8] {'x'}, dimensions={0} | all-to-all | bytes 1179648 | tf_op jit(solution)/shard_map/all_to_all | solution.py:341
  95.6 0.8 copy.99
  96.4 8.1 %all-to-all-start.1 = ((bf16[64,5,2,128]{3,2,1,0:T(2,128)(2,1)}), bf16[64,5,2,128]{3,2,1,0:T(2,128)(2,1)S(1)}, u32[]{:S(2)}, u32[]{:S(2)}) async-start(bf16[64,5,2,128]{3,2,1,0:T(2,128)(2,1)} %copy.99), calls=%async_computation.1 | async-start | bytes 327680 | tf_op jit(solution)/shard_map/all_to_all | solution.py:350
  104.5 0.8 copy.100
  105.4 10.8 %all-to-all-done.1 = bf16[64,5,2,128]{3,2,1,0:T(2,128)(2,1)S(1)} async-done(((bf16[64,5,2,128]{3,2,1,0:T(2,128)(2,1)}), bf16[64,5,2,128]{3,2,1,0:T(2,128)(2,1)S(1)}, u32[]{:S(2)}, u32[]{:S(2)}) %all-to-all-start.1) | async-done | bytes 163872 | tf_op jit(solution)/shard_map/all_to_all | solution.py:350
  116.4 0.7 dynamic-slice_reduce_fusion
  (124 shorter events, 7.6 us)
Async XLA Ops:
  1.9 13.6 %copy-start = (bf16[12,16,8,256]{3,1,2,0:T(8,128)(2,1)}, bf16[12,16,8,256]{3,1,2,0:T(8,128)(2,1)S(1)}, u32[]{:S(2)}) copy-start(bf16[12,16,8,256]{3,1,2,0:T(8,128)(2,1)S(1)} %copy.112) | copy-start | bytes 2359300
  1.9 11.8 %copy-start.8 = (s32[12,4]{0,1:T(4,128)S(1)}, s32[12,4]{0,1:T(4,128)}, u32[]{:S(2)}) copy-start(s32[12,4]{0,1:T(4,128)} %param.12) | copy-start | bytes 580
  2.0 12.8 %copy-start.9 = (s32[12,4]{0,1:T(4,128)S(1)}, s32[12,4]{0,1:T(4,128)}, u32[]{:S(2)}) copy-start(s32[12,4]{0,1:T(4,128)} %param.11) | copy-start | bytes 580
  2.1 13.2 %collective-permute-start = (bf16[12,8,2,256]{3,2,1,0:T(2,128)(2,1)S(1)}, bf16[12,8,2,256]{3,2,1,0:T(2,128)(2,1)S(1)}, u32[]{:S(2)}, u32[]{:S(2)}) collective-permute-start(bf16[12,8,2,256]{3,2,1,0:T(2,128)(2,1)S(1)} %slice.331), channel_id=1, source_target_pairs={{0,32},{32,64},{64,96},{96,128},{128,160},{160,192},{192,224},{224... | collective-permute-start | bytes 294920 | tf_op jit(solution)/shard_map/ppermute | solution.py:60
  7.3 7.9 %collective-permute-start.1 = (bf16[12,8,2,256]{3,2,1,0:T(2,128)(2,1)S(1)}, bf16[12,8,2,256]{3,2,1,0:T(2,128)(2,1)S(1)}, u32[]{:S(2)}, u32[]{:S(2)}) collective-permute-start(bf16[12,8,2,256]{3,2,1,0:T(2,128)(2,1)S(1)} %get-tuple-element.48), channel_id=1, source_target_pairs={{32,0},{64,32},{96,64},{128,96},{160,128},{192,160},{224,192},{256... | collective-permute-start | bytes 294920 | tf_op jit(solution)/shard_map/ppermute | solution.py:61
  12.9 16.7 %collective-permute-start.3 = (bf16[12,8,2,256]{3,1,2,0:T(8,128)(2,1)S(1)}, bf16[12,8,2,256]{3,1,2,0:T(8,128)(2,1)S(1)}, u32[]{:S(2)}, u32[]{:S(2)}) collective-permute-start(bf16[12,8,2,256]{3,1,2,0:T(8,128)(2,1)S(1)} %copy.115), channel_id=1, source_target_pairs={{1,30},{2,29},{3,28},{4,27},{5,26},{6,25},{7,24},{8,23},{9,22},{10... | collective-permute-start | bytes 294920 | tf_op jit(solution)/shard_map/ppermute | solution.py:57
  15.3 1.2 %copy-start.5 = (bf16[12,8,2,256]{3,2,1,0:T(2,128)(2,1)}, bf16[12,8,2,256]{3,2,1,0:T(2,128)(2,1)S(1)}, u32[]{:S(2)}) copy-start(bf16[12,8,2,256]{3,2,1,0:T(2,128)(2,1)S(1)} %collective-permute-done.1) | copy-start | bytes 294916
  16.6 13.1 %collective-permute-start.2 = (bf16[12,2,28,256]{3,2,1,0:T(8,128)(2,1)S(1)}, bf16[12,2,28,256]{3,2,1,0:T(8,128)(2,1)S(1)}, u32[]{:S(2)}, u32[]{:S(2)}) collective-permute-start(bf16[12,2,28,256]{3,2,1,0:T(8,128)(2,1)S(1)} %pad_maximum_fusion.1), channel_id=1, source_target_pairs={{0,511},{31,480},{480,31},{511,0}} | collective-permute-start | bytes 1032200 | tf_op jit(solution)/shard_map/ppermute | solution.py:57
  18.0 18.8 %collective-permute-start.4 = (bf16[12,2,20,256]{3,2,1,0:T(8,128)(2,1)S(1)}, bf16[12,2,20,256]{3,2,1,0:T(8,128)(2,1)S(1)}, u32[]{:S(2)}, u32[]{:S(2)}) collective-permute-start(bf16[12,2,20,256]{3,2,1,0:T(8,128)(2,1)S(1)} %get-tuple-element.54), channel_id=1, source_target_pairs={{32,63},{63,32},{64,447},{95,416},{96,127},{127,96},{128,383},{159... | collective-permute-start | bytes 737288 | tf_op jit(solution)/shard_map/ppermute | solution.py:57
  36.9 10.7 %copy-start.13 = (s32[12]{0:T(128)S(1)}, s32[12]{0:T(128)}, u32[]{:S(2)}) copy-start(s32[12]{0:T(128)} %get-tuple-element.73) | copy-start | bytes 148
  36.9 10.7 %copy-start.3 = (bf16[12,16,8,128]{3,2,1,0:T(8,128)(2,1)S(1)}, bf16[12,16,8,128]{3,2,1,0:T(8,128)(2,1)}, u32[]{:S(2)}) copy-start(bf16[12,16,8,128]{3,2,1,0:T(8,128)(2,1)} %param.10) | copy-start | bytes 1179652
  37.5 10.9 %copy-start.11 = (s32[12,4]{0,1:T(4,128)S(1)}, s32[12,4]{0,1:T(4,128)}, u32[]{:S(2)}) copy-start(s32[12,4]{0,1:T(4,128)} %param.13) | copy-start | bytes 580
  37.5 15.1 %copy-start.12 = (pred[12]{0:T(512)(128)(4,1)S(1)}, pred[12]{0:T(512)(128)(4,1)}, u32[]{:S(2)}) copy-start(pred[12]{0:T(512)(128)(4,1)} %compare_or_fusion.1) | copy-start | bytes 40
  37.5 15.1 %collective-permute-start.6 = (bf16[12,2,20,256]{3,2,1,0:T(8,128)(2,1)S(1)}, bf16[12,2,20,256]{3,2,1,0:T(8,128)(2,1)S(1)}, u32[]{:S(2)}, u32[]{:S(2)}) collective-permute-start(bf16[12,2,20,256]{3,2,1,0:T(8,128)(2,1)S(1)} %slice.342), channel_id=1, source_target_pairs={{32,479},{63,448},{64,95},{95,64},{96,415},{127,384},{128,159},{15... | collective-permute-start | bytes 737288 | tf_op jit(solution)/shard_map/ppermute | solution.py:57
  46.9 5.8 %collective-permute-start.5 = (bf16[12,2,30,256]{3,2,1,0:T(8,128)(2,1)S(1)}, bf16[12,2,30,256]{3,2,1,0:T(8,128)(2,1)S(1)}, u32[]{:S(2)}, u32[]{:S(2)}) collective-permute-start(bf16[12,2,30,256]{3,2,1,0:T(8,128)(2,1)S(1)} %pad_maximum_fusion.2), channel_id=1, source_target_pairs={{0,31},{31,0},{480,511},{511,480}} | collective-permute-start | bytes 1105928 | tf_op jit(solution)/shard_map/ppermute | solution.py:57
  48.4 11.2 %collective-permute-start.9 = (bf16[12,2,20,256]{3,2,1,0:T(8,128)(2,1)S(1)}, bf16[12,2,20,256]{3,2,1,0:T(8,128)(2,1)S(1)}, u32[]{:S(2)}, u32[]{:S(2)}) collective-permute-start(bf16[12,2,20,256]{3,2,1,0:T(8,128)(2,1)S(1)} %fusion.1), channel_id=1, source_target_pairs={{32,33},{33,34},{34,35},{35,36},{36,37},{37,38},{38,39},{39,40},{4... | collective-permute-start | bytes 737288 | tf_op jit(solution)/shard_map/ppermute | solution.py:70
  49.7 3.6 %copy-start.6 = (bf16[12,8,2,256]{3,2,1,0:T(2,128)(2,1)S(1)}, bf16[12,8,2,256]{3,2,1,0:T(2,128)(2,1)}, u32[]{:S(2)}) copy-start(bf16[12,8,2,256]{3,2,1,0:T(2,128)(2,1)} %copy-done.5) | copy-start | bytes 294916
  49.7 7.9 %collective-permute-start.11 = (bf16[12,2,20,256]{3,2,1,0:T(8,128)(2,1)}, bf16[12,2,20,256]{3,2,1,0:T(8,128)(2,1)}, u32[]{:S(2)}, u32[]{:S(2)}) collective-permute-start(bf16[12,2,20,256]{3,2,1,0:T(8,128)(2,1)} %get-tuple-element.53), channel_id=1, source_target_pairs={{33,32},{34,33},{35,34},{36,35},{37,36},{38,37},{39,38},{40,39},{4... | collective-permute-start | bytes 737288 | tf_op jit(solution)/shard_map/ppermute | solution.py:71
  51.2 2.0 %collective-permute-start.7 = (bf16[12,8,2,256]{3,2,1,0:T(2,128)(2,1)S(1)}, bf16[12,8,2,256]{3,2,1,0:T(2,128)(2,1)S(1)}, u32[]{:S(2)}, u32[]{:S(2)}) collective-permute-start(bf16[12,8,2,256]{3,2,1,0:T(2,128)(2,1)S(1)} %slice.343), channel_id=1, source_target_pairs={{1,481},{2,482},{3,483},{4,484},{5,485},{6,486},{7,487},{8,488},{9... | collective-permute-start | bytes 294920 | tf_op jit(solution)/shard_map/ppermute | solution.py:57
  53.4 2.6 %copy-start.7 = (bf16[12,2,2,256]{3,2,1,0:T(2,128)(2,1)S(1)}, bf16[12,2,2,256]{3,2,1,0:T(2,128)(2,1)}, u32[]{:S(2)}) copy-start(bf16[12,2,2,256]{3,2,1,0:T(2,128)(2,1)} %get-tuple-element.49) | copy-start | bytes 73732
  53.4 2.6 %copy-start.10 = (pred[12]{0:T(512)(128)(4,1)S(1)}, pred[12]{0:T(512)(128)(4,1)}, u32[]{:S(2)}) copy-start(pred[12]{0:T(512)(128)(4,1)} %get-tuple-element.77) | copy-start | bytes 40
  53.7 2.7 %copy-start.1 = (bf16[12,8,2,256]{3,2,1,0:T(2,128)(2,1)}, bf16[12,8,2,256]{3,2,1,0:T(2,128)(2,1)S(1)}, u32[]{:S(2)}) copy-start(bf16[12,8,2,256]{3,2,1,0:T(2,128)(2,1)S(1)} %get-tuple-element.39.lo_ref) | copy-start | bytes 294916
  54.3 2.2 %copy-start.2 = (bf16[12,2,8,256]{3,2,1,0:T(8,128)(2,1)}, bf16[12,2,8,256]{3,2,1,0:T(8,128)(2,1)S(1)}, u32[]{:S(2)}) copy-start(bf16[12,2,8,256]{3,2,1,0:T(8,128)(2,1)S(1)} %broadcast_select_fusion.5) | copy-start | bytes 294916
  54.5 3.1 %collective-permute-start.10 = (bf16[12,2,20,256]{3,2,1,0:T(8,128)(2,1)S(1)}, bf16[12,2,20,256]{3,2,1,0:T(8,128)(2,1)}, u32[]{:S(2)}, u32[]{:S(2)}) collective-permute-start(bf16[12,2,20,256]{3,2,1,0:T(8,128)(2,1)S(1)} %fusion.4), channel_id=1, source_target_pairs={{1,0},{2,1},{3,2},{4,3},{5,4},{6,5},{7,6},{8,7},{9,8},{10,9},{11,1... | collective-permute-start | bytes 737288 | tf_op jit(solution)/shard_map/ppermute | solution.py:71
  56.7 2.9 %collective-permute-start.8 = (bf16[12,2,20,256]{3,2,1,0:T(8,128)(2,1)S(1)}, bf16[12,2,20,256]{3,2,1,0:T(8,128)(2,1)S(1)}, u32[]{:S(2)}, u32[]{:S(2)}) collective-permute-start(bf16[12,2,20,256]{3,2,1,0:T(8,128)(2,1)S(1)} %fusion.2), channel_id=1, source_target_pairs={{0,1},{1,2},{2,3},{3,4},{4,5},{5,6},{6,7},{7,8},{8,9},{9,10},{10,1... | collective-permute-start | bytes 737288 | tf_op jit(solution)/shard_map/ppermute | solution.py:70
  71.7 8.9 %collective-permute-start.12 = (f32[2,4,2,144,128]{4,3,2,1,0:T(8,128)}, f32[2,4,2,144,128]{4,3,2,1,0:T(8,128)S(1)}, u32[]{:S(2)}, u32[]{:S(2)}) collective-permute-start(f32[2,4,2,144,128]{4,3,2,1,0:T(8,128)} %get-tuple-element.8), channel_id=1, source_target_pairs={{0,32},{32,0},{1,33},{33,1},{2,34},{34,2},{3,35},{35,3},{4,36},{36... | collective-permute-start | bytes 3538952 | tf_op jit(solution)/shard_map/ppermute | solution.py:338
  94.9 9.6 %copy-start.4 = (bf16[12,8,16,128]{3,2,1,0:T(8,128)(2,1)S(1)}, bf16[12,8,16,128]{3,2,1,0:T(8,128)(2,1)}, u32[]{:S(2)}) copy-start(bf16[12,8,16,128]{3,2,1,0:T(8,128)(2,1)} %get-tuple-element.6) | copy-start | bytes 1179652
  96.4 19.8 %all-to-all-start.1 = ((bf16[64,5,2,128]{3,2,1,0:T(2,128)(2,1)}), bf16[64,5,2,128]{3,2,1,0:T(2,128)(2,1)S(1)}, u32[]{:S(2)}, u32[]{:S(2)}) async-start(bf16[64,5,2,128]{3,2,1,0:T(2,128)(2,1)} %copy.99), calls=%async_computation.1 | async-start | bytes 327680 | tf_op jit(solution)/shard_map/all_to_all | solution.py:350

commit v5 on v4

--- a/solution.py
+++ b/solution.py
@@ -263,7 +263,7 @@
 
     lax.fori_loop(0, faces // step, forward, 0, unroll=True)
 
-    grads, _, across, along, span, _ = sums_ref.shape
+    _, across, _, along, span, _ = sums_ref.shape
 
     def put(grad, tap, block):
         start, end = tap * c_in, (tap + 1) * c_in
@@ -272,7 +272,7 @@
             n = at // span
             stop = min(end, (n + 1) * span)
             spot = n // 2 % across, n // 2 // across
-            sums_ref[grad, n % 2, spot[0], spot[1], pl.ds(at - n * span, stop - at)] = block[at - start : stop - start]
+            sums_ref[n % 2, spot[0], grad, spot[1], pl.ds(at - n * span, stop - at)] = block[at - start : stop - start]
             at = stop
 
     core = core_ref[0]
@@ -285,7 +285,7 @@
             for b in range(3):
                 put(grad, a * 3 + b, sums[:, b * c_out : (b + 1) * c_out])
         for n, target in ((core, mine_ref), (1 - core, theirs_ref)):
-            copy = pltpu.make_async_copy(sums_ref.at[grad, n], target.at[grad], sems.at[len(copies)])
+            copy = pltpu.make_async_copy(sums_ref.at[n, :, grad], target.at[:, grad], sems.at[len(copies)])
             copy.start()
             copies.append(copy)
     for copy in copies:
@@ -297,7 +297,7 @@
     wide = width + 4
     c_out = wg.shape[-1]
     across, along = lax.axis_size("x"), lax.axis_size("yh")
-    shares = (2, across, along, 9 * c_in // (2 * across * along), c_out)
+    shares = (across, 2, along, 9 * c_in // (2 * across * along), c_out)
     vm = pl.BlockSpec(memory_space=pltpu.VMEM)
     anywhere = pl.BlockSpec(memory_space=pl.ANY)
     return pl.pallas_call(
@@ -336,9 +336,8 @@
 
 def scattered_sum(mine, theirs, scale):
     both = mine + lax.ppermute(theirs, "c", [(0, 1), (1, 0)])
-    grads, across, along, span, lanes = both.shape
-    sends = jnp.transpose(both.astype(jnp.bfloat16), (1, 0, 2, 3, 4))
-    arrived = lax.all_to_all(sends.reshape(across, -1, lanes), "x", 0, 0)
+    across, grads, along, span, lanes = both.shape
+    arrived = lax.all_to_all(both.astype(jnp.bfloat16).reshape(across, -1, lanes), "x", 0, 0)
     part = jnp.sum(arrived.astype(jnp.float32), axis=0).reshape(grads, along, span, lanes)
     takers = lax.axis_size(COLS)
     share = span * lanes // takers

time: 118 us -> 118 us (level)
    transpose x1 -> x0, other arithmetic: 1.44 us -> none  [scattered_sum(): sends = jnp.transpose(both.astype(jnp.bfloat16), (1, 0, 2, 3, 4))]
    convert_element_type x0 -> x1, other arithmetic: none -> 1.44 us  [scattered_sum(): both.astype(jnp.bfloat16).reshape(across, -1, lanes)]
where the time goes in v5:
time: 118 us; the launch traced here: 117 us
  starting transfers between devices  52.9 us (45%)
  waiting for transfers between devices  19 us (16%)
  blocking collectives  12.8 us (11%)
  Pallas kernels  11.2 us (9%)
  other arithmetic  9.84 us (8%)
  local copies, waits for them, and re-layouts  9.81 us (8%)
  between operations  1.48 us (1%)
    ppermute x6, starting transfers between devices, swap(): return lax.ppermute(x, everywhere, pairs)  23.5 us
    all_to_all x1, blocking collectives, scattered_sum(): lax.all_to_all(both.astype(jnp.bfloat16).reshape(across, -1, lanes), 'x',...  12.8 us
    pallas_call x1, Pallas kernels, compute(): pl.pallas_call(compute_kernel, in_specs=[pl.BlockSpec(memory_space=pltpu....  11.2 us
    all_to_all x1, waiting for transfers between devices, scattered_sum(): arrived = lax.all_to_all(sends, ('yh',) + COLS, 0, 0)  10.8 us
    all_to_all x1, starting transfers between devices, scattered_sum(): arrived = lax.all_to_all(sends, ('yh',) + COLS, 0, 0)  8.1 us
    ppermute x1, starting transfers between devices, scattered_sum(): both = mine + lax.ppermute(theirs, 'c', [(0, 1), (1, 0)])  6.28 us
    ppermute x1, starting transfers between devices, halos(): lax.ppermute(north, ROWS, [(i + 1, i) for i in range(row_last)])  5.57 us
    ppermute x6, waiting for transfers between devices, swap(): return lax.ppermute(x, everywhere, pairs)  5.41 us
  transfers between devices with their start and end apart: 14, of which 4 were waited for; matrix products, arithmetic and copies ran while one was open for 11% of the time, Pallas kernels for 0%

profile of v5, /device:TPU:1, one launch (start us, length us, event | category | flops | bytes accessed | tf_op | source)
XLA Modules:
  0.0 117.0 jit_solution(2436340528084477652)
XLA Ops:
  0.6 1.3 %copy.108 = bf16[12,16,8,256]{3,1,2,0:T(8,128)(2,1)S(1)} copy(bf16[12,16,8,256]{3,2,1,0:T(8,128)(2,1)} %param.7) | data formatting | bytes 1572864 | tf_op args[0]
  2.1 4.5 %collective-permute-start = (bf16[12,8,2,256]{3,2,1,0:T(2,128)(2,1)S(1)}, bf16[12,8,2,256]{3,2,1,0:T(2,128)(2,1)S(1)}, u32[]{:S(2)}, u32[]{:S(2)}) collective-permute-start(bf16[12,8,2,256]{3,2,1,0:T(2,128)(2,1)S(1)} %slice.331), channel_id=1, source_target_pairs={{0,32},{32,64},{64,96},{96,128},{128,160},{160,192},{192,224},{224... | collective-permute-start | bytes 294920 | tf_op jit(solution)/shard_map/ppermute | solution.py:60
  7.3 5.6 %collective-permute-start.1 = (bf16[12,8,2,256]{3,2,1,0:T(2,128)(2,1)S(1)}, bf16[12,8,2,256]{3,2,1,0:T(2,128)(2,1)S(1)}, u32[]{:S(2)}, u32[]{:S(2)}) collective-permute-start(bf16[12,8,2,256]{3,2,1,0:T(2,128)(2,1)S(1)} %get-tuple-element.48), channel_id=1, source_target_pairs={{32,0},{64,32},{96,64},{128,96},{160,128},{192,160},{224,192},{256... | collective-permute-start | bytes 294920 | tf_op jit(solution)/shard_map/ppermute | solution.py:61
  12.9 0.7 collective-permute-start.3
  15.6 0.9 fusion.2
  16.6 0.7 collective-permute-start.2
  17.3 0.6 compare_or_fusion.2
  18.0 11.7 %collective-permute-start.4 = (bf16[12,2,20,256]{3,2,1,0:T(8,128)(2,1)S(1)}, bf16[12,2,20,256]{3,2,1,0:T(8,128)(2,1)S(1)}, u32[]{:S(2)}, u32[]{:S(2)}) collective-permute-start(bf16[12,2,20,256]{3,2,1,0:T(8,128)(2,1)S(1)} %get-tuple-element.54), channel_id=1, source_target_pairs={{32,63},{63,32},{64,447},{95,416},{96,127},{127,96},{128,383},{159... | collective-permute-start | bytes 737288 | tf_op jit(solution)/shard_map/ppermute | solution.py:57
  30.1 1.3 %gather_fusion = bf16[48,8,2,256]{3,2,1,0:T(2,128)(2,1)S(1)} fusion(bf16[24,8,2,256]{3,2,1,0:T(2,128)(2,1)S(1)} %pad_maximum_fusion.8, s32[1024]{0:T(1024)S(1)} %pad_clamp_fusion.1), kind=kCustom, calls=%fused_computation | custom fusion | bytes 786624 | tf_op jit(solution)/shard_map/gather | solution.py:18
  31.5 0.6 fusion.20
  32.1 4.6 %collective-permute-done.4 = bf16[12,2,20,256]{3,2,1,0:T(8,128)(2,1)S(1)} collective-permute-done((bf16[12,2,20,256]{3,2,1,0:T(8,128)(2,1)S(1)}, bf16[12,2,20,256]{3,2,1,0:T(8,128)(2,1)S(1)}, u32[]{:S(2)}, u32[]{:S(2)}) %collective-permute-start.4) | collective-permute-done | bytes 245792 | tf_op jit(solution)/shard_map/ppermute | solution.py:57
  37.5 9.1 %collective-permute-start.6 = (bf16[12,2,20,256]{3,2,1,0:T(8,128)(2,1)S(1)}, bf16[12,2,20,256]{3,2,1,0:T(8,128)(2,1)S(1)}, u32[]{:S(2)}, u32[]{:S(2)}) collective-permute-start(bf16[12,2,20,256]{3,2,1,0:T(8,128)(2,1)S(1)} %slice.342), channel_id=1, source_target_pairs={{32,479},{63,448},{64,95},{95,64},{96,415},{127,384},{128,159},{15... | collective-permute-start | bytes 737288 | tf_op jit(solution)/shard_map/ppermute | solution.py:57
  46.9 0.7 collective-permute-start.5
  47.6 0.8 copy.109
  48.4 1.3 %collective-permute-start.9 = (bf16[12,2,20,256]{3,2,1,0:T(8,128)(2,1)S(1)}, bf16[12,2,20,256]{3,2,1,0:T(8,128)(2,1)S(1)}, u32[]{:S(2)}, u32[]{:S(2)}) collective-permute-start(bf16[12,2,20,256]{3,2,1,0:T(8,128)(2,1)S(1)} %fusion), channel_id=1, source_target_pairs={{32,33},{33,34},{34,35},{35,36},{36,37},{37,38},{38,39},{39,40},{4... | collective-permute-start | bytes 737288 | tf_op jit(solution)/shard_map/ppermute | solution.py:70
  49.7 1.4 %collective-permute-start.11 = (bf16[12,2,20,256]{3,2,1,0:T(8,128)(2,1)}, bf16[12,2,20,256]{3,2,1,0:T(8,128)(2,1)}, u32[]{:S(2)}, u32[]{:S(2)}) collective-permute-start(bf16[12,2,20,256]{3,2,1,0:T(8,128)(2,1)} %get-tuple-element.53), channel_id=1, source_target_pairs={{33,32},{34,33},{35,34},{36,35},{37,36},{38,37},{39,38},{40,39},{4... | collective-permute-start | bytes 737288 | tf_op jit(solution)/shard_map/ppermute | solution.py:71
  51.2 0.7 collective-permute-start.7
  51.9 0.8 collective-permute-done.6
  54.5 1.4 %collective-permute-start.10 = (bf16[12,2,20,256]{3,2,1,0:T(8,128)(2,1)S(1)}, bf16[12,2,20,256]{3,2,1,0:T(8,128)(2,1)}, u32[]{:S(2)}, u32[]{:S(2)}) collective-permute-start(bf16[12,2,20,256]{3,2,1,0:T(8,128)(2,1)S(1)} %fusion.3), channel_id=1, source_target_pairs={{1,0},{2,1},{3,2},{4,3},{5,4},{6,5},{7,6},{8,7},{9,8},{10,9},{11,1... | collective-permute-start | bytes 737288 | tf_op jit(solution)/shard_map/ppermute | solution.py:71
  56.7 0.9 collective-permute-start.8
  57.7 1.9 %select_select_fusion = (bf16[12,2,20,256]{3,2,1,0:T(8,128)(2,1)}, bf16[12,2,20,256]{3,2,1,0:T(8,128)(2,1)S(1)}) fusion(bf16[12,2,20,256]{3,2,1,0:T(8,128)(2,1)} %collective-permute-done.10, bf16[12,2,20,256]{3,2,1,0:T(8,128)(2,1)} %collective-permute-done.11, pred[]{:T(512)S(6)} %eq.249, pred[]{:T(512)S(6)} %or.30, ...), kind=kLoop, calls=%fused_computation.21 | loop fusion | flops 983040 | bytes 1228802 | tf_op jit(solution)/shard_map/jit(_where)/select_n | solution.py:180
  59.6 0.8 select_select_fusion.1.lf_ref
  60.4 11.2 %gated_conv.1 = (bf16[12,8,16,128]{3,2,1,0:T(8,128)(2,1)}, f32[4,2,2,144,128]{4,3,2,1,0:T(8,128)}, f32[4,2,2,144,128]{4,3,2,1,0:T(8,128)}) custom-call(s32[1]{0:T(128)} %bitcast.core_ref, bf16[12,8,16,256]{3,2,1,0:T(8,128)(2,1)} %bitcast.247, bf16[12,2,20,256]{3,2,1,0:T(8,128)(2,1)} %select_select_fusion.1.lf_ref, ...), custom_call_target="tpu_custom_call" | custom-call | tf_op jit(solution)/shard_map/gated_conv/pallas_call | solution.py:303
  71.6 6.3 %collective-permute-start.12 = (f32[4,2,2,144,128]{4,3,2,1,0:T(8,128)}, f32[4,2,2,144,128]{4,3,2,1,0:T(8,128)S(1)}, u32[]{:S(2)}, u32[]{:S(2)}) collective-permute-start(f32[4,2,2,144,128]{4,3,2,1,0:T(8,128)} %get-tuple-element.8), channel_id=1, source_target_pairs={{0,32},{32,0},{1,33},{33,1},{2,34},{34,2},{3,35},{35,3},{4,36},{36... | collective-permute-start | bytes 3538952 | tf_op jit(solution)/shard_map/ppermute | solution.py:338
  77.9 2.7 %collective-permute-done.12 = f32[4,2,2,144,128]{4,3,2,1,0:T(8,128)S(1)} collective-permute-done((f32[4,2,2,144,128]{4,3,2,1,0:T(8,128)}, f32[4,2,2,144,128]{4,3,2,1,0:T(8,128)S(1)}, u32[]{:S(2)}, u32[]{:S(2)}) %collective-permute-start.12) | collective-permute-done | bytes 1179680 | tf_op jit(solution)/shard_map/ppermute | solution.py:338
  80.6 1.4 %add_convert_fusion = bf16[4,2,2,144,128]{4,3,2,1,0:T(8,128)(2,1)S(1)} fusion(f32[4,2,2,144,128]{4,3,2,1,0:T(8,128)} %get-tuple-element.7, f32[4,2,2,144,128]{4,3,2,1,0:T(8,128)S(1)} %collective-permute-done.12), kind=kLoop, calls=%fused_computation.2 | loop fusion | flops 589824 | bytes 2949120 | tf_op jit(solution)/shard_map/convert_element_type | solution.py:340
  82.0 12.8 %all_to_all.10 = bf16[4,576,128]{2,1,0:T(8,128)(2,1)S(1)} all-to-all(bf16[4,576,128]{2,1,0:T(8,128)(2,1)S(1)} %bitcast.248), channel_id=1, replica_groups=mesh['yh'=2,'x'=4,'c'=2,'yl'=4,'z'=8] {'x'}, dimensions={0} | all-to-all | bytes 1179648 | tf_op jit(solution)/shard_map/all_to_all | solution.py:340
  95.5 0.8 copy.95
  96.3 8.1 %all-to-all-start.1 = ((bf16[64,5,2,128]{3,2,1,0:T(2,128)(2,1)}), bf16[64,5,2,128]{3,2,1,0:T(2,128)(2,1)S(1)}, u32[]{:S(2)}, u32[]{:S(2)}) async-start(bf16[64,5,2,128]{3,2,1,0:T(2,128)(2,1)} %copy.95), calls=%async_computation.1 | async-start | bytes 327680 | tf_op jit(solution)/shard_map/all_to_all | solution.py:349
  104.4 0.8 copy.96
  105.3 10.8 %all-to-all-done.1 = bf16[64,5,2,128]{3,2,1,0:T(2,128)(2,1)S(1)} async-done(((bf16[64,5,2,128]{3,2,1,0:T(2,128)(2,1)}), bf16[64,5,2,128]{3,2,1,0:T(2,128)(2,1)S(1)}, u32[]{:S(2)}, u32[]{:S(2)}) %all-to-all-start.1) | async-done | bytes 163872 | tf_op jit(solution)/shard_map/all_to_all | solution.py:349
  116.3 0.7 dynamic-slice_reduce_fusion
  (123 shorter events, 7.5 us)
Async XLA Ops:
  1.9 13.6 %copy-start = (bf16[12,16,8,256]{3,1,2,0:T(8,128)(2,1)}, bf16[12,16,8,256]{3,1,2,0:T(8,128)(2,1)S(1)}, u32[]{:S(2)}) copy-start(bf16[12,16,8,256]{3,1,2,0:T(8,128)(2,1)S(1)} %copy.108) | copy-start | bytes 2359300
  1.9 11.8 %copy-start.8 = (s32[12,4]{0,1:T(4,128)S(1)}, s32[12,4]{0,1:T(4,128)}, u32[]{:S(2)}) copy-start(s32[12,4]{0,1:T(4,128)} %param.12) | copy-start | bytes 580
  2.0 12.8 %copy-start.9 = (s32[12,4]{0,1:T(4,128)S(1)}, s32[12,4]{0,1:T(4,128)}, u32[]{:S(2)}) copy-start(s32[12,4]{0,1:T(4,128)} %param.11) | copy-start | bytes 580
  2.1 13.2 %collective-permute-start = (bf16[12,8,2,256]{3,2,1,0:T(2,128)(2,1)S(1)}, bf16[12,8,2,256]{3,2,1,0:T(2,128)(2,1)S(1)}, u32[]{:S(2)}, u32[]{:S(2)}) collective-permute-start(bf16[12,8,2,256]{3,2,1,0:T(2,128)(2,1)S(1)} %slice.331), channel_id=1, source_target_pairs={{0,32},{32,64},{64,96},{96,128},{128,160},{160,192},{192,224},{224... | collective-permute-start | bytes 294920 | tf_op jit(solution)/shard_map/ppermute | solution.py:60
  7.3 7.9 %collective-permute-start.1 = (bf16[12,8,2,256]{3,2,1,0:T(2,128)(2,1)S(1)}, bf16[12,8,2,256]{3,2,1,0:T(2,128)(2,1)S(1)}, u32[]{:S(2)}, u32[]{:S(2)}) collective-permute-start(bf16[12,8,2,256]{3,2,1,0:T(2,128)(2,1)S(1)} %get-tuple-element.48), channel_id=1, source_target_pairs={{32,0},{64,32},{96,64},{128,96},{160,128},{192,160},{224,192},{256... | collective-permute-start | bytes 294920 | tf_op jit(solution)/shard_map/ppermute | solution.py:61
  12.9 16.7 %collective-permute-start.3 = (bf16[12,8,2,256]{3,1,2,0:T(8,128)(2,1)S(1)}, bf16[12,8,2,256]{3,1,2,0:T(8,128)(2,1)S(1)}, u32[]{:S(2)}, u32[]{:S(2)}) collective-permute-start(bf16[12,8,2,256]{3,1,2,0:T(8,128)(2,1)S(1)} %copy.111), channel_id=1, source_target_pairs={{1,30},{2,29},{3,28},{4,27},{5,26},{6,25},{7,24},{8,23},{9,22},{10... | collective-permute-start | bytes 294920 | tf_op jit(solution)/shard_map/ppermute | solution.py:57
  15.3 1.2 %copy-start.5 = (bf16[12,8,2,256]{3,2,1,0:T(2,128)(2,1)}, bf16[12,8,2,256]{3,2,1,0:T(2,128)(2,1)S(1)}, u32[]{:S(2)}) copy-start(bf16[12,8,2,256]{3,2,1,0:T(2,128)(2,1)S(1)} %collective-permute-done.1) | copy-start | bytes 294916
  16.6 13.1 %collective-permute-start.2 = (bf16[12,2,28,256]{3,2,1,0:T(8,128)(2,1)S(1)}, bf16[12,2,28,256]{3,2,1,0:T(8,128)(2,1)S(1)}, u32[]{:S(2)}, u32[]{:S(2)}) collective-permute-start(bf16[12,2,28,256]{3,2,1,0:T(8,128)(2,1)S(1)} %pad_maximum_fusion.1), channel_id=1, source_target_pairs={{0,511},{31,480},{480,31},{511,0}} | collective-permute-start | bytes 1032200 | tf_op jit(solution)/shard_map/ppermute | solution.py:57
  18.0 18.8 %collective-permute-start.4 = (bf16[12,2,20,256]{3,2,1,0:T(8,128)(2,1)S(1)}, bf16[12,2,20,256]{3,2,1,0:T(8,128)(2,1)S(1)}, u32[]{:S(2)}, u32[]{:S(2)}) collective-permute-start(bf16[12,2,20,256]{3,2,1,0:T(8,128)(2,1)S(1)} %get-tuple-element.54), channel_id=1, source_target_pairs={{32,63},{63,32},{64,447},{95,416},{96,127},{127,96},{128,383},{159... | collective-permute-start | bytes 737288 | tf_op jit(solution)/shard_map/ppermute | solution.py:57
  36.9 10.7 %copy-start.13 = (s32[12]{0:T(128)S(1)}, s32[12]{0:T(128)}, u32[]{:S(2)}) copy-start(s32[12]{0:T(128)} %get-tuple-element.73) | copy-start | bytes 148
  36.9 10.7 %copy-start.3 = (bf16[12,16,8,128]{3,2,1,0:T(8,128)(2,1)S(1)}, bf16[12,16,8,128]{3,2,1,0:T(8,128)(2,1)}, u32[]{:S(2)}) copy-start(bf16[12,16,8,128]{3,2,1,0:T(8,128)(2,1)} %param.10) | copy-start | bytes 1179652
  37.5 10.9 %copy-start.11 = (s32[12,4]{0,1:T(4,128)S(1)}, s32[12,4]{0,1:T(4,128)}, u32[]{:S(2)}) copy-start(s32[12,4]{0,1:T(4,128)} %param.13) | copy-start | bytes 580
  37.5 15.1 %copy-start.12 = (pred[12]{0:T(512)(128)(4,1)S(1)}, pred[12]{0:T(512)(128)(4,1)}, u32[]{:S(2)}) copy-start(pred[12]{0:T(512)(128)(4,1)} %compare_or_fusion.1) | copy-start | bytes 40
  37.5 15.1 %collective-permute-start.6 = (bf16[12,2,20,256]{3,2,1,0:T(8,128)(2,1)S(1)}, bf16[12,2,20,256]{3,2,1,0:T(8,128)(2,1)S(1)}, u32[]{:S(2)}, u32[]{:S(2)}) collective-permute-start(bf16[12,2,20,256]{3,2,1,0:T(8,128)(2,1)S(1)} %slice.342), channel_id=1, source_target_pairs={{32,479},{63,448},{64,95},{95,64},{96,415},{127,384},{128,159},{15... | collective-permute-start | bytes 737288 | tf_op jit(solution)/shard_map/ppermute | solution.py:57
  46.9 5.8 %collective-permute-start.5 = (bf16[12,2,30,256]{3,2,1,0:T(8,128)(2,1)S(1)}, bf16[12,2,30,256]{3,2,1,0:T(8,128)(2,1)S(1)}, u32[]{:S(2)}, u32[]{:S(2)}) collective-permute-start(bf16[12,2,30,256]{3,2,1,0:T(8,128)(2,1)S(1)} %pad_maximum_fusion.2), channel_id=1, source_target_pairs={{0,31},{31,0},{480,511},{511,480}} | collective-permute-start | bytes 1105928 | tf_op jit(solution)/shard_map/ppermute | solution.py:57
  48.4 11.2 %collective-permute-start.9 = (bf16[12,2,20,256]{3,2,1,0:T(8,128)(2,1)S(1)}, bf16[12,2,20,256]{3,2,1,0:T(8,128)(2,1)S(1)}, u32[]{:S(2)}, u32[]{:S(2)}) collective-permute-start(bf16[12,2,20,256]{3,2,1,0:T(8,128)(2,1)S(1)} %fusion), channel_id=1, source_target_pairs={{32,33},{33,34},{34,35},{35,36},{36,37},{37,38},{38,39},{39,40},{4... | collective-permute-start | bytes 737288 | tf_op jit(solution)/shard_map/ppermute | solution.py:70
  49.7 3.6 %copy-start.6 = (bf16[12,8,2,256]{3,2,1,0:T(2,128)(2,1)S(1)}, bf16[12,8,2,256]{3,2,1,0:T(2,128)(2,1)}, u32[]{:S(2)}) copy-start(bf16[12,8,2,256]{3,2,1,0:T(2,128)(2,1)} %copy-done.5) | copy-start | bytes 294916
  49.7 7.9 %collective-permute-start.11 = (bf16[12,2,20,256]{3,2,1,0:T(8,128)(2,1)}, bf16[12,2,20,256]{3,2,1,0:T(8,128)(2,1)}, u32[]{:S(2)}, u32[]{:S(2)}) collective-permute-start(bf16[12,2,20,256]{3,2,1,0:T(8,128)(2,1)} %get-tuple-element.53), channel_id=1, source_target_pairs={{33,32},{34,33},{35,34},{36,35},{37,36},{38,37},{39,38},{40,39},{4... | collective-permute-start | bytes 737288 | tf_op jit(solution)/shard_map/ppermute | solution.py:71
  51.2 2.0 %collective-permute-start.7 = (bf16[12,8,2,256]{3,2,1,0:T(2,128)(2,1)S(1)}, bf16[12,8,2,256]{3,2,1,0:T(2,128)(2,1)S(1)}, u32[]{:S(2)}, u32[]{:S(2)}) collective-permute-start(bf16[12,8,2,256]{3,2,1,0:T(2,128)(2,1)S(1)} %slice.343), channel_id=1, source_target_pairs={{1,481},{2,482},{3,483},{4,484},{5,485},{6,486},{7,487},{8,488},{9... | collective-permute-start | bytes 294920 | tf_op jit(solution)/shard_map/ppermute | solution.py:57
  53.4 2.6 %copy-start.7 = (bf16[12,2,2,256]{3,2,1,0:T(2,128)(2,1)S(1)}, bf16[12,2,2,256]{3,2,1,0:T(2,128)(2,1)}, u32[]{:S(2)}) copy-start(bf16[12,2,2,256]{3,2,1,0:T(2,128)(2,1)} %get-tuple-element.49) | copy-start | bytes 73732
  53.4 2.6 %copy-start.10 = (pred[12]{0:T(512)(128)(4,1)S(1)}, pred[12]{0:T(512)(128)(4,1)}, u32[]{:S(2)}) copy-start(pred[12]{0:T(512)(128)(4,1)} %get-tuple-element.77) | copy-start | bytes 40
  53.7 2.7 %copy-start.1 = (bf16[12,8,2,256]{3,2,1,0:T(2,128)(2,1)}, bf16[12,8,2,256]{3,2,1,0:T(2,128)(2,1)S(1)}, u32[]{:S(2)}) copy-start(bf16[12,8,2,256]{3,2,1,0:T(2,128)(2,1)S(1)} %get-tuple-element.39.lo_ref) | copy-start | bytes 294916
  54.3 2.2 %copy-start.2 = (bf16[12,2,8,256]{3,2,1,0:T(8,128)(2,1)}, bf16[12,2,8,256]{3,2,1,0:T(8,128)(2,1)S(1)}, u32[]{:S(2)}) copy-start(bf16[12,2,8,256]{3,2,1,0:T(8,128)(2,1)S(1)} %broadcast_select_fusion.5) | copy-start | bytes 294916
  54.5 3.1 %collective-permute-start.10 = (bf16[12,2,20,256]{3,2,1,0:T(8,128)(2,1)S(1)}, bf16[12,2,20,256]{3,2,1,0:T(8,128)(2,1)}, u32[]{:S(2)}, u32[]{:S(2)}) collective-permute-start(bf16[12,2,20,256]{3,2,1,0:T(8,128)(2,1)S(1)} %fusion.3), channel_id=1, source_target_pairs={{1,0},{2,1},{3,2},{4,3},{5,4},{6,5},{7,6},{8,7},{9,8},{10,9},{11,1... | collective-permute-start | bytes 737288 | tf_op jit(solution)/shard_map/ppermute | solution.py:71
  56.7 2.9 %collective-permute-start.8 = (bf16[12,2,20,256]{3,2,1,0:T(8,128)(2,1)S(1)}, bf16[12,2,20,256]{3,2,1,0:T(8,128)(2,1)S(1)}, u32[]{:S(2)}, u32[]{:S(2)}) collective-permute-start(bf16[12,2,20,256]{3,2,1,0:T(8,128)(2,1)S(1)} %fusion.1), channel_id=1, source_target_pairs={{0,1},{1,2},{2,3},{3,4},{4,5},{5,6},{6,7},{7,8},{8,9},{9,10},{10,1... | collective-permute-start | bytes 737288 | tf_op jit(solution)/shard_map/ppermute | solution.py:70
  71.6 8.9 %collective-permute-start.12 = (f32[4,2,2,144,128]{4,3,2,1,0:T(8,128)}, f32[4,2,2,144,128]{4,3,2,1,0:T(8,128)S(1)}, u32[]{:S(2)}, u32[]{:S(2)}) collective-permute-start(f32[4,2,2,144,128]{4,3,2,1,0:T(8,128)} %get-tuple-element.8), channel_id=1, source_target_pairs={{0,32},{32,0},{1,33},{33,1},{2,34},{34,2},{3,35},{35,3},{4,36},{36... | collective-permute-start | bytes 3538952 | tf_op jit(solution)/shard_map/ppermute | solution.py:338
  94.8 9.6 %copy-start.4 = (bf16[12,8,16,128]{3,2,1,0:T(8,128)(2,1)S(1)}, bf16[12,8,16,128]{3,2,1,0:T(8,128)(2,1)}, u32[]{:S(2)}) copy-start(bf16[12,8,16,128]{3,2,1,0:T(8,128)(2,1)} %get-tuple-element.6) | copy-start | bytes 1179652
  96.3 19.8 %all-to-all-start.1 = ((bf16[64,5,2,128]{3,2,1,0:T(2,128)(2,1)}), bf16[64,5,2,128]{3,2,1,0:T(2,128)(2,1)S(1)}, u32[]{:S(2)}, u32[]{:S(2)}) async-start(bf16[64,5,2,128]{3,2,1,0:T(2,128)(2,1)} %copy.95), calls=%async_computation.1 | async-start | bytes 327680 | tf_op jit(solution)/shard_map/all_to_all | solution.py:349

commit v6 on v5

--- a/solution.py
+++ b/solution.py
@@ -195,16 +195,13 @@
     mine_ref,
     theirs_ref,
     x_ref,
-    dg_ref,
-    dv_ref,
+    d_ref,
     sums_ref,
     sems,
 ):
     _, faces, wide, height, c_in = x_ref.shape
     width = wide - 4
     c_out = hg_ref.shape[-1]
-    dg_ref[...] = jnp.zeros(dg_ref.shape, dg_ref.dtype)
-    dv_ref[...] = jnp.zeros(dv_ref.shape, dv_ref.dtype)
     step = 1
     cells = step * width * height
 
@@ -255,10 +252,13 @@
         hidden_ref[here] = (act * value).astype(jnp.bfloat16).reshape(shape)
         dgate = (up * value * slope).astype(jnp.bfloat16).reshape(shape)
         dvalue = (up * act).astype(jnp.bfloat16).reshape(shape)
-        for b in range(3):
-            lanes = pl.ds(b * c_out, c_out)
-            dg_ref[here, pl.ds(b, width), :, lanes] = dgate
-            dv_ref[here, pl.ds(2 * b, width), :, lanes] = dvalue
+        for tap, (at, delta) in enumerate([(1 + b, dgate) for b in range(3)] + [(2 * b, dvalue) for b in range(3)]):
+            lanes = pl.ds(tap * c_out, c_out)
+            for start, size in ((0, at), (at + width, 4 - at)):
+                if size > 0:
+                    blank = jnp.zeros((step, size, height, c_out), jnp.bfloat16)
+                    d_ref[here, pl.ds(start, size), :, lanes] = blank
+            d_ref[here, pl.ds(at, width), :, lanes] = delta
         return 0
 
     lax.fori_loop(0, faces // step, forward, 0, unroll=True)
@@ -277,13 +277,20 @@
 
     core = core_ref[0]
     copies = []
-    for grad, first, cols, delta in ((0, 1, pl.ds(1, wide - 2), dg_ref), (1, 0, pl.ds(0, wide), dv_ref)):
-        d = delta[...].reshape(-1, 3 * c_out)
-        for a in range(3):
-            x = x_ref[first + a * (grad + 1), :, cols].reshape(-1, c_in)
+    half = 3 * c_out
+    everything, inner = pl.ds(0, wide), pl.ds(1, wide - 2)
+    for grad, parts in (
+        (1, ((0, everything, half, half), (4, everything, half, half), (2, everything, 0, 2 * half))),
+        (0, ((1, inner, 0, half), (3, inner, 0, half))),
+    ):
+        for shift, cols, lane, lanes in parts:
+            x = x_ref[shift, :, cols].reshape(-1, c_in)
+            d = d_ref[:, cols, :, pl.ds(lane, lanes)].reshape(-1, lanes)
             sums = lax.dot_general(x, d, (((0,), (0,)), ((), ())), preferred_element_type=jnp.float32)
-            for b in range(3):
-                put(grad, a * 3 + b, sums[:, b * c_out : (b + 1) * c_out])
+            for b in range(lanes // c_out):
+                which, tap = divmod(lane // c_out + b, 3)
+                a = shift // 2 if which == 1 else shift - 1
+                put(which, a * 3 + tap, sums[:, b * c_out : (b + 1) * c_out])
         for n, target in ((core, mine_ref), (1 - core, theirs_ref)):
             copy = pltpu.make_async_copy(sums_ref.at[n, :, grad], target.at[:, grad], sems.at[len(copies)])
             copy.start()
@@ -311,8 +318,7 @@
         ],
         scratch_shapes=[
             pltpu.VMEM((5, faces, wide, height, c_in), jnp.bfloat16),
-            pltpu.VMEM((faces, wide - 2, height, 3 * c_out), jnp.bfloat16),
-            pltpu.VMEM((faces, wide, height, 3 * c_out), jnp.bfloat16),
+            pltpu.VMEM((faces, wide, height, 6 * c_out), jnp.bfloat16),
             pltpu.VMEM((2,) + shares, jnp.float32),
             pltpu.SemaphoreType.DMA((4,)),
         ],

time: 118 us -> 118 us (level)
  no operation moved by 1% of the time
where the time goes in v6:
time: 118 us; the launch traced here: 117 us
  starting transfers between devices  52.9 us (45%)
  waiting for transfers between devices  19 us (16%)
  blocking collectives  12.8 us (11%)
  Pallas kernels  11 us (9%)
  other arithmetic  9.84 us (8%)
  local copies, waits for them, and re-layouts  9.81 us (8%)
  between operations  1.48 us (1%)
    ppermute x6, starting transfers between devices, swap(): return lax.ppermute(x, everywhere, pairs)  23.5 us
    all_to_all x1, blocking collectives, scattered_sum(): lax.all_to_all(both.astype(jnp.bfloat16).reshape(across, -1, lanes), 'x',...  12.8 us
    pallas_call x1, Pallas kernels, compute(): pl.pallas_call(compute_kernel, in_specs=[pl.BlockSpec(memory_space=pltpu....  11 us
    all_to_all x1, waiting for transfers between devices, scattered_sum(): arrived = lax.all_to_all(sends, ('yh',) + COLS, 0, 0)  10.8 us
    all_to_all x1, starting transfers between devices, scattered_sum(): arrived = lax.all_to_all(sends, ('yh',) + COLS, 0, 0)  8.1 us
    ppermute x1, starting transfers between devices, scattered_sum(): both = mine + lax.ppermute(theirs, 'c', [(0, 1), (1, 0)])  6.27 us
    ppermute x1, starting transfers between devices, halos(): lax.ppermute(north, ROWS, [(i + 1, i) for i in range(row_last)])  5.57 us
    ppermute x6, waiting for transfers between devices, swap(): return lax.ppermute(x, everywhere, pairs)  5.41 us
  transfers between devices with their start and end apart: 14, of which 4 were waited for; matrix products, arithmetic and copies ran while one was open for 11% of the time, Pallas kernels for 0%

profile of v6, /device:TPU:1, one launch (start us, length us, event | category | flops | bytes accessed | tf_op | source)
XLA Modules:
  0.0 116.8 jit_solution(12797078021198990624)
XLA Ops:
  0.6 1.3 %copy.108 = bf16[12,16,8,256]{3,1,2,0:T(8,128)(2,1)S(1)} copy(bf16[12,16,8,256]{3,2,1,0:T(8,128)(2,1)} %param.7) | data formatting | bytes 1572864 | tf_op args[0]
  2.1 4.5 %collective-permute-start = (bf16[12,8,2,256]{3,2,1,0:T(2,128)(2,1)S(1)}, bf16[12,8,2,256]{3,2,1,0:T(2,128)(2,1)S(1)}, u32[]{:S(2)}, u32[]{:S(2)}) collective-permute-start(bf16[12,8,2,256]{3,2,1,0:T(2,128)(2,1)S(1)} %slice.331), channel_id=1, source_target_pairs={{0,32},{32,64},{64,96},{96,128},{128,160},{160,192},{192,224},{224... | collective-permute-start | bytes 294920 | tf_op jit(solution)/shard_map/ppermute | solution.py:60
  7.3 5.6 %collective-permute-start.1 = (bf16[12,8,2,256]{3,2,1,0:T(2,128)(2,1)S(1)}, bf16[12,8,2,256]{3,2,1,0:T(2,128)(2,1)S(1)}, u32[]{:S(2)}, u32[]{:S(2)}) collective-permute-start(bf16[12,8,2,256]{3,2,1,0:T(2,128)(2,1)S(1)} %get-tuple-element.48), channel_id=1, source_target_pairs={{32,0},{64,32},{96,64},{128,96},{160,128},{192,160},{224,192},{256... | collective-permute-start | bytes 294920 | tf_op jit(solution)/shard_map/ppermute | solution.py:61
  12.9 0.7 collective-permute-start.3
  15.6 0.9 fusion.2
  16.6 0.7 collective-permute-start.2
  17.3 0.6 compare_or_fusion.2
  18.0 11.7 %collective-permute-start.4 = (bf16[12,2,20,256]{3,2,1,0:T(8,128)(2,1)S(1)}, bf16[12,2,20,256]{3,2,1,0:T(8,128)(2,1)S(1)}, u32[]{:S(2)}, u32[]{:S(2)}) collective-permute-start(bf16[12,2,20,256]{3,2,1,0:T(8,128)(2,1)S(1)} %get-tuple-element.54), channel_id=1, source_target_pairs={{32,63},{63,32},{64,447},{95,416},{96,127},{127,96},{128,383},{159... | collective-permute-start | bytes 737288 | tf_op jit(solution)/shard_map/ppermute | solution.py:57
  30.1 1.3 %gather_fusion = bf16[48,8,2,256]{3,2,1,0:T(2,128)(2,1)S(1)} fusion(bf16[24,8,2,256]{3,2,1,0:T(2,128)(2,1)S(1)} %pad_maximum_fusion.8, s32[1024]{0:T(1024)S(1)} %pad_clamp_fusion.1), kind=kCustom, calls=%fused_computation | custom fusion | bytes 786624 | tf_op jit(solution)/shard_map/gather | solution.py:18
  31.5 0.6 fusion.20
  32.1 4.6 %collective-permute-done.4 = bf16[12,2,20,256]{3,2,1,0:T(8,128)(2,1)S(1)} collective-permute-done((bf16[12,2,20,256]{3,2,1,0:T(8,128)(2,1)S(1)}, bf16[12,2,20,256]{3,2,1,0:T(8,128)(2,1)S(1)}, u32[]{:S(2)}, u32[]{:S(2)}) %collective-permute-start.4) | collective-permute-done | bytes 245792 | tf_op jit(solution)/shard_map/ppermute | solution.py:57
  37.5 9.1 %collective-permute-start.6 = (bf16[12,2,20,256]{3,2,1,0:T(8,128)(2,1)S(1)}, bf16[12,2,20,256]{3,2,1,0:T(8,128)(2,1)S(1)}, u32[]{:S(2)}, u32[]{:S(2)}) collective-permute-start(bf16[12,2,20,256]{3,2,1,0:T(8,128)(2,1)S(1)} %slice.342), channel_id=1, source_target_pairs={{32,479},{63,448},{64,95},{95,64},{96,415},{127,384},{128,159},{15... | collective-permute-start | bytes 737288 | tf_op jit(solution)/shard_map/ppermute | solution.py:57
  46.9 0.7 collective-permute-start.5
  47.6 0.8 copy.109
  48.4 1.3 %collective-permute-start.9 = (bf16[12,2,20,256]{3,2,1,0:T(8,128)(2,1)S(1)}, bf16[12,2,20,256]{3,2,1,0:T(8,128)(2,1)S(1)}, u32[]{:S(2)}, u32[]{:S(2)}) collective-permute-start(bf16[12,2,20,256]{3,2,1,0:T(8,128)(2,1)S(1)} %fusion), channel_id=1, source_target_pairs={{32,33},{33,34},{34,35},{35,36},{36,37},{37,38},{38,39},{39,40},{4... | collective-permute-start | bytes 737288 | tf_op jit(solution)/shard_map/ppermute | solution.py:70
  49.7 1.4 %collective-permute-start.11 = (bf16[12,2,20,256]{3,2,1,0:T(8,128)(2,1)}, bf16[12,2,20,256]{3,2,1,0:T(8,128)(2,1)}, u32[]{:S(2)}, u32[]{:S(2)}) collective-permute-start(bf16[12,2,20,256]{3,2,1,0:T(8,128)(2,1)} %get-tuple-element.53), channel_id=1, source_target_pairs={{33,32},{34,33},{35,34},{36,35},{37,36},{38,37},{39,38},{40,39},{4... | collective-permute-start | bytes 737288 | tf_op jit(solution)/shard_map/ppermute | solution.py:71
  51.2 0.7 collective-permute-start.7
  51.9 0.8 collective-permute-done.6
  54.5 1.4 %collective-permute-start.10 = (bf16[12,2,20,256]{3,2,1,0:T(8,128)(2,1)S(1)}, bf16[12,2,20,256]{3,2,1,0:T(8,128)(2,1)}, u32[]{:S(2)}, u32[]{:S(2)}) collective-permute-start(bf16[12,2,20,256]{3,2,1,0:T(8,128)(2,1)S(1)} %fusion.3), channel_id=1, source_target_pairs={{1,0},{2,1},{3,2},{4,3},{5,4},{6,5},{7,6},{8,7},{9,8},{10,9},{11,1... | collective-permute-start | bytes 737288 | tf_op jit(solution)/shard_map/ppermute | solution.py:71
  56.7 0.9 collective-permute-start.8
  57.7 1.9 %select_select_fusion = (bf16[12,2,20,256]{3,2,1,0:T(8,128)(2,1)}, bf16[12,2,20,256]{3,2,1,0:T(8,128)(2,1)S(1)}) fusion(bf16[12,2,20,256]{3,2,1,0:T(8,128)(2,1)} %collective-permute-done.10, bf16[12,2,20,256]{3,2,1,0:T(8,128)(2,1)} %collective-permute-done.11, pred[]{:T(512)S(6)} %eq.249, pred[]{:T(512)S(6)} %or.30, ...), kind=kLoop, calls=%fused_computation.21 | loop fusion | flops 983040 | bytes 1228802 | tf_op jit(solution)/shard_map/jit(_where)/select_n | solution.py:180
  59.6 0.8 select_select_fusion.1.lf_ref
  60.4 11.0 %gated_conv.1 = (bf16[12,8,16,128]{3,2,1,0:T(8,128)(2,1)}, f32[4,2,2,144,128]{4,3,2,1,0:T(8,128)}, f32[4,2,2,144,128]{4,3,2,1,0:T(8,128)}) custom-call(s32[1]{0:T(128)} %bitcast.core_ref, bf16[12,8,16,256]{3,2,1,0:T(8,128)(2,1)} %bitcast.247, bf16[12,2,20,256]{3,2,1,0:T(8,128)(2,1)} %select_select_fusion.1.lf_ref, ...), custom_call_target="tpu_custom_call" | custom-call | tf_op jit(solution)/shard_map/gated_conv/pallas_call | solution.py:310
  71.4 6.3 %collective-permute-start.12 = (f32[4,2,2,144,128]{4,3,2,1,0:T(8,128)}, f32[4,2,2,144,128]{4,3,2,1,0:T(8,128)S(1)}, u32[]{:S(2)}, u32[]{:S(2)}) collective-permute-start(f32[4,2,2,144,128]{4,3,2,1,0:T(8,128)} %get-tuple-element.8), channel_id=1, source_target_pairs={{0,32},{32,0},{1,33},{33,1},{2,34},{34,2},{3,35},{35,3},{4,36},{36... | collective-permute-start | bytes 3538952 | tf_op jit(solution)/shard_map/ppermute | solution.py:344
  77.7 2.7 %collective-permute-done.12 = f32[4,2,2,144,128]{4,3,2,1,0:T(8,128)S(1)} collective-permute-done((f32[4,2,2,144,128]{4,3,2,1,0:T(8,128)}, f32[4,2,2,144,128]{4,3,2,1,0:T(8,128)S(1)}, u32[]{:S(2)}, u32[]{:S(2)}) %collective-permute-start.12) | collective-permute-done | bytes 1179680 | tf_op jit(solution)/shard_map/ppermute | solution.py:344
  80.4 1.4 %add_convert_fusion = bf16[4,2,2,144,128]{4,3,2,1,0:T(8,128)(2,1)S(1)} fusion(f32[4,2,2,144,128]{4,3,2,1,0:T(8,128)} %get-tuple-element.7, f32[4,2,2,144,128]{4,3,2,1,0:T(8,128)S(1)} %collective-permute-done.12), kind=kLoop, calls=%fused_computation.2 | loop fusion | flops 589824 | bytes 2949120 | tf_op jit(solution)/shard_map/convert_element_type | solution.py:346
  81.8 12.8 %all_to_all.10 = bf16[4,576,128]{2,1,0:T(8,128)(2,1)S(1)} all-to-all(bf16[4,576,128]{2,1,0:T(8,128)(2,1)S(1)} %bitcast.248), channel_id=1, replica_groups=mesh['yh'=2,'x'=4,'c'=2,'yl'=4,'z'=8] {'x'}, dimensions={0} | all-to-all | bytes 1179648 | tf_op jit(solution)/shard_map/all_to_all | solution.py:346
  95.2 0.8 copy.95
  96.1 8.1 %all-to-all-start.1 = ((bf16[64,5,2,128]{3,2,1,0:T(2,128)(2,1)}), bf16[64,5,2,128]{3,2,1,0:T(2,128)(2,1)S(1)}, u32[]{:S(2)}, u32[]{:S(2)}) async-start(bf16[64,5,2,128]{3,2,1,0:T(2,128)(2,1)} %copy.95), calls=%async_computation.1 | async-start | bytes 327680 | tf_op jit(solution)/shard_map/all_to_all | solution.py:355
  104.2 0.8 copy.96
  105.1 10.8 %all-to-all-done.1 = bf16[64,5,2,128]{3,2,1,0:T(2,128)(2,1)S(1)} async-done(((bf16[64,5,2,128]{3,2,1,0:T(2,128)(2,1)}), bf16[64,5,2,128]{3,2,1,0:T(2,128)(2,1)S(1)}, u32[]{:S(2)}, u32[]{:S(2)}) %all-to-all-start.1) | async-done | bytes 163872 | tf_op jit(solution)/shard_map/all_to_all | solution.py:355
  116.1 0.7 dynamic-slice_reduce_fusion
  (123 shorter events, 7.5 us)
Async XLA Ops:
  1.9 13.6 %copy-start = (bf16[12,16,8,256]{3,1,2,0:T(8,128)(2,1)}, bf16[12,16,8,256]{3,1,2,0:T(8,128)(2,1)S(1)}, u32[]{:S(2)}) copy-start(bf16[12,16,8,256]{3,1,2,0:T(8,128)(2,1)S(1)} %copy.108) | copy-start | bytes 2359300
  1.9 11.8 %copy-start.8 = (s32[12,4]{0,1:T(4,128)S(1)}, s32[12,4]{0,1:T(4,128)}, u32[]{:S(2)}) copy-start(s32[12,4]{0,1:T(4,128)} %param.12) | copy-start | bytes 580
  2.0 12.8 %copy-start.9 = (s32[12,4]{0,1:T(4,128)S(1)}, s32[12,4]{0,1:T(4,128)}, u32[]{:S(2)}) copy-start(s32[12,4]{0,1:T(4,128)} %param.11) | copy-start | bytes 580
  2.1 13.2 %collective-permute-start = (bf16[12,8,2,256]{3,2,1,0:T(2,128)(2,1)S(1)}, bf16[12,8,2,256]{3,2,1,0:T(2,128)(2,1)S(1)}, u32[]{:S(2)}, u32[]{:S(2)}) collective-permute-start(bf16[12,8,2,256]{3,2,1,0:T(2,128)(2,1)S(1)} %slice.331), channel_id=1, source_target_pairs={{0,32},{32,64},{64,96},{96,128},{128,160},{160,192},{192,224},{224... | collective-permute-start | bytes 294920 | tf_op jit(solution)/shard_map/ppermute | solution.py:60
  7.3 7.9 %collective-permute-start.1 = (bf16[12,8,2,256]{3,2,1,0:T(2,128)(2,1)S(1)}, bf16[12,8,2,256]{3,2,1,0:T(2,128)(2,1)S(1)}, u32[]{:S(2)}, u32[]{:S(2)}) collective-permute-start(bf16[12,8,2,256]{3,2,1,0:T(2,128)(2,1)S(1)} %get-tuple-element.48), channel_id=1, source_target_pairs={{32,0},{64,32},{96,64},{128,96},{160,128},{192,160},{224,192},{256... | collective-permute-start | bytes 294920 | tf_op jit(solution)/shard_map/ppermute | solution.py:61
  12.9 16.7 %collective-permute-start.3 = (bf16[12,8,2,256]{3,1,2,0:T(8,128)(2,1)S(1)}, bf16[12,8,2,256]{3,1,2,0:T(8,128)(2,1)S(1)}, u32[]{:S(2)}, u32[]{:S(2)}) collective-permute-start(bf16[12,8,2,256]{3,1,2,0:T(8,128)(2,1)S(1)} %copy.111), channel_id=1, source_target_pairs={{1,30},{2,29},{3,28},{4,27},{5,26},{6,25},{7,24},{8,23},{9,22},{10... | collective-permute-start | bytes 294920 | tf_op jit(solution)/shard_map/ppermute | solution.py:57
  15.3 1.2 %copy-start.5 = (bf16[12,8,2,256]{3,2,1,0:T(2,128)(2,1)}, bf16[12,8,2,256]{3,2,1,0:T(2,128)(2,1)S(1)}, u32[]{:S(2)}) copy-start(bf16[12,8,2,256]{3,2,1,0:T(2,128)(2,1)S(1)} %collective-permute-done.1) | copy-start | bytes 294916
  16.6 13.1 %collective-permute-start.2 = (bf16[12,2,28,256]{3,2,1,0:T(8,128)(2,1)S(1)}, bf16[12,2,28,256]{3,2,1,0:T(8,128)(2,1)S(1)}, u32[]{:S(2)}, u32[]{:S(2)}) collective-permute-start(bf16[12,2,28,256]{3,2,1,0:T(8,128)(2,1)S(1)} %pad_maximum_fusion.1), channel_id=1, source_target_pairs={{0,511},{31,480},{480,31},{511,0}} | collective-permute-start | bytes 1032200 | tf_op jit(solution)/shard_map/ppermute | solution.py:57
  18.0 18.8 %collective-permute-start.4 = (bf16[12,2,20,256]{3,2,1,0:T(8,128)(2,1)S(1)}, bf16[12,2,20,256]{3,2,1,0:T(8,128)(2,1)S(1)}, u32[]{:S(2)}, u32[]{:S(2)}) collective-permute-start(bf16[12,2,20,256]{3,2,1,0:T(8,128)(2,1)S(1)} %get-tuple-element.54), channel_id=1, source_target_pairs={{32,63},{63,32},{64,447},{95,416},{96,127},{127,96},{128,383},{159... | collective-permute-start | bytes 737288 | tf_op jit(solution)/shard_map/ppermute | solution.py:57
  36.9 10.7 %copy-start.13 = (s32[12]{0:T(128)S(1)}, s32[12]{0:T(128)}, u32[]{:S(2)}) copy-start(s32[12]{0:T(128)} %get-tuple-element.73) | copy-start | bytes 148
  36.9 10.7 %copy-start.3 = (bf16[12,16,8,128]{3,2,1,0:T(8,128)(2,1)S(1)}, bf16[12,16,8,128]{3,2,1,0:T(8,128)(2,1)}, u32[]{:S(2)}) copy-start(bf16[12,16,8,128]{3,2,1,0:T(8,128)(2,1)} %param.10) | copy-start | bytes 1179652
  37.5 10.9 %copy-start.11 = (s32[12,4]{0,1:T(4,128)S(1)}, s32[12,4]{0,1:T(4,128)}, u32[]{:S(2)}) copy-start(s32[12,4]{0,1:T(4,128)} %param.13) | copy-start | bytes 580
  37.5 15.1 %copy-start.12 = (pred[12]{0:T(512)(128)(4,1)S(1)}, pred[12]{0:T(512)(128)(4,1)}, u32[]{:S(2)}) copy-start(pred[12]{0:T(512)(128)(4,1)} %compare_or_fusion.1) | copy-start | bytes 40
  37.5 15.1 %collective-permute-start.6 = (bf16[12,2,20,256]{3,2,1,0:T(8,128)(2,1)S(1)}, bf16[12,2,20,256]{3,2,1,0:T(8,128)(2,1)S(1)}, u32[]{:S(2)}, u32[]{:S(2)}) collective-permute-start(bf16[12,2,20,256]{3,2,1,0:T(8,128)(2,1)S(1)} %slice.342), channel_id=1, source_target_pairs={{32,479},{63,448},{64,95},{95,64},{96,415},{127,384},{128,159},{15... | collective-permute-start | bytes 737288 | tf_op jit(solution)/shard_map/ppermute | solution.py:57
  46.9 5.8 %collective-permute-start.5 = (bf16[12,2,30,256]{3,2,1,0:T(8,128)(2,1)S(1)}, bf16[12,2,30,256]{3,2,1,0:T(8,128)(2,1)S(1)}, u32[]{:S(2)}, u32[]{:S(2)}) collective-permute-start(bf16[12,2,30,256]{3,2,1,0:T(8,128)(2,1)S(1)} %pad_maximum_fusion.2), channel_id=1, source_target_pairs={{0,31},{31,0},{480,511},{511,480}} | collective-permute-start | bytes 1105928 | tf_op jit(solution)/shard_map/ppermute | solution.py:57
  48.4 11.2 %collective-permute-start.9 = (bf16[12,2,20,256]{3,2,1,0:T(8,128)(2,1)S(1)}, bf16[12,2,20,256]{3,2,1,0:T(8,128)(2,1)S(1)}, u32[]{:S(2)}, u32[]{:S(2)}) collective-permute-start(bf16[12,2,20,256]{3,2,1,0:T(8,128)(2,1)S(1)} %fusion), channel_id=1, source_target_pairs={{32,33},{33,34},{34,35},{35,36},{36,37},{37,38},{38,39},{39,40},{4... | collective-permute-start | bytes 737288 | tf_op jit(solution)/shard_map/ppermute | solution.py:70
  49.7 3.6 %copy-start.6 = (bf16[12,8,2,256]{3,2,1,0:T(2,128)(2,1)S(1)}, bf16[12,8,2,256]{3,2,1,0:T(2,128)(2,1)}, u32[]{:S(2)}) copy-start(bf16[12,8,2,256]{3,2,1,0:T(2,128)(2,1)} %copy-done.5) | copy-start | bytes 294916
  49.7 7.9 %collective-permute-start.11 = (bf16[12,2,20,256]{3,2,1,0:T(8,128)(2,1)}, bf16[12,2,20,256]{3,2,1,0:T(8,128)(2,1)}, u32[]{:S(2)}, u32[]{:S(2)}) collective-permute-start(bf16[12,2,20,256]{3,2,1,0:T(8,128)(2,1)} %get-tuple-element.53), channel_id=1, source_target_pairs={{33,32},{34,33},{35,34},{36,35},{37,36},{38,37},{39,38},{40,39},{4... | collective-permute-start | bytes 737288 | tf_op jit(solution)/shard_map/ppermute | solution.py:71
  51.2 2.0 %collective-permute-start.7 = (bf16[12,8,2,256]{3,2,1,0:T(2,128)(2,1)S(1)}, bf16[12,8,2,256]{3,2,1,0:T(2,128)(2,1)S(1)}, u32[]{:S(2)}, u32[]{:S(2)}) collective-permute-start(bf16[12,8,2,256]{3,2,1,0:T(2,128)(2,1)S(1)} %slice.343), channel_id=1, source_target_pairs={{1,481},{2,482},{3,483},{4,484},{5,485},{6,486},{7,487},{8,488},{9... | collective-permute-start | bytes 294920 | tf_op jit(solution)/shard_map/ppermute | solution.py:57
  53.4 2.6 %copy-start.7 = (bf16[12,2,2,256]{3,2,1,0:T(2,128)(2,1)S(1)}, bf16[12,2,2,256]{3,2,1,0:T(2,128)(2,1)}, u32[]{:S(2)}) copy-start(bf16[12,2,2,256]{3,2,1,0:T(2,128)(2,1)} %get-tuple-element.49) | copy-start | bytes 73732
  53.4 2.6 %copy-start.10 = (pred[12]{0:T(512)(128)(4,1)S(1)}, pred[12]{0:T(512)(128)(4,1)}, u32[]{:S(2)}) copy-start(pred[12]{0:T(512)(128)(4,1)} %get-tuple-element.77) | copy-start | bytes 40
  53.7 2.7 %copy-start.1 = (bf16[12,8,2,256]{3,2,1,0:T(2,128)(2,1)}, bf16[12,8,2,256]{3,2,1,0:T(2,128)(2,1)S(1)}, u32[]{:S(2)}) copy-start(bf16[12,8,2,256]{3,2,1,0:T(2,128)(2,1)S(1)} %get-tuple-element.39.lo_ref) | copy-start | bytes 294916
  54.3 2.2 %copy-start.2 = (bf16[12,2,8,256]{3,2,1,0:T(8,128)(2,1)}, bf16[12,2,8,256]{3,2,1,0:T(8,128)(2,1)S(1)}, u32[]{:S(2)}) copy-start(bf16[12,2,8,256]{3,2,1,0:T(8,128)(2,1)S(1)} %broadcast_select_fusion.5) | copy-start | bytes 294916
  54.5 3.1 %collective-permute-start.10 = (bf16[12,2,20,256]{3,2,1,0:T(8,128)(2,1)S(1)}, bf16[12,2,20,256]{3,2,1,0:T(8,128)(2,1)}, u32[]{:S(2)}, u32[]{:S(2)}) collective-permute-start(bf16[12,2,20,256]{3,2,1,0:T(8,128)(2,1)S(1)} %fusion.3), channel_id=1, source_target_pairs={{1,0},{2,1},{3,2},{4,3},{5,4},{6,5},{7,6},{8,7},{9,8},{10,9},{11,1... | collective-permute-start | bytes 737288 | tf_op jit(solution)/shard_map/ppermute | solution.py:71
  56.7 2.9 %collective-permute-start.8 = (bf16[12,2,20,256]{3,2,1,0:T(8,128)(2,1)S(1)}, bf16[12,2,20,256]{3,2,1,0:T(8,128)(2,1)S(1)}, u32[]{:S(2)}, u32[]{:S(2)}) collective-permute-start(bf16[12,2,20,256]{3,2,1,0:T(8,128)(2,1)S(1)} %fusion.1), channel_id=1, source_target_pairs={{0,1},{1,2},{2,3},{3,4},{4,5},{5,6},{6,7},{7,8},{8,9},{9,10},{10,1... | collective-permute-start | bytes 737288 | tf_op jit(solution)/shard_map/ppermute | solution.py:70
  71.4 8.9 %collective-permute-start.12 = (f32[4,2,2,144,128]{4,3,2,1,0:T(8,128)}, f32[4,2,2,144,128]{4,3,2,1,0:T(8,128)S(1)}, u32[]{:S(2)}, u32[]{:S(2)}) collective-permute-start(f32[4,2,2,144,128]{4,3,2,1,0:T(8,128)} %get-tuple-element.8), channel_id=1, source_target_pairs={{0,32},{32,0},{1,33},{33,1},{2,34},{34,2},{3,35},{35,3},{4,36},{36... | collective-permute-start | bytes 3538952 | tf_op jit(solution)/shard_map/ppermute | solution.py:344
  94.6 9.6 %copy-start.4 = (bf16[12,8,16,128]{3,2,1,0:T(8,128)(2,1)S(1)}, bf16[12,8,16,128]{3,2,1,0:T(8,128)(2,1)}, u32[]{:S(2)}) copy-start(bf16[12,8,16,128]{3,2,1,0:T(8,128)(2,1)} %get-tuple-element.6) | copy-start | bytes 1179652
  96.1 19.8 %all-to-all-start.1 = ((bf16[64,5,2,128]{3,2,1,0:T(2,128)(2,1)}), bf16[64,5,2,128]{3,2,1,0:T(2,128)(2,1)S(1)}, u32[]{:S(2)}, u32[]{:S(2)}) async-start(bf16[64,5,2,128]{3,2,1,0:T(2,128)(2,1)} %copy.95), calls=%async_computation.1 | async-start | bytes 327680 | tf_op jit(solution)/shard_map/all_to_all | solution.py:355
